TPU v7x, 128 devices: a whole 4x4x4 slice. The times are simulated.
128 devices in a mesh: row: 16 (over y_hi, x, core), col: 8 (over z, y_lo).
Axes of the slice: x: 4, y: 4 (y_hi: 2, y_lo: 2; y = y_hi * 2 + y_lo), z: 4, core: 2. Of those that a mesh axis runs over, the one named last changes fastest.
Arguments:
- features: bfloat16 [65536, 512], P(('row', 'col')), may hold values from -6 to 6
- weight: bfloat16 [512, 512], replicated, may hold values from -0.25 to 0.25
- bias: float32 [512], replicated, may hold values from -3 to 3
- cotangent: bfloat16 [65536, 512], P(('row', 'col')), may hold values from -6 to 6
- tile_values: bfloat16 [16, 8, 64, 128, 128], P('row', 'col'), may hold values from -0.1875 to 0.1875
- tile_rows: int32 [16, 8, 64], P('row', 'col'), may hold values from 0 to 511, as said below
- tile_cols: int32 [16, 8, 64], P('row', 'col'), may hold values from 0 to 511, as said below
- tile_counts: int32 [16, 8], P('row', 'col'), may hold values from 1 to 64
Outputs:
- output: bfloat16 [65536, 512], P(('row', 'col'))
- feature_grad: bfloat16 [65536, 512], P(('row', 'col'))
- weight_grad: float32 [512, 512], replicated
- bias_grad: float32 [512], replicated
Inputs may be any that keep to these rules, and one draw needn't show every extreme that they name: `tile_rows`: A tile on device (p, q) has its row block in row group p, that is row block // 32 == p, and its column block's atoms on devices of index q along col, that is (column block // 4) % 8 == q. The rows of features held by device (p, q) are blocks p * 4 * 8 + q * 4 to that plus 4 - 1. Row and column pairs may repeat. `tile_cols`: among one device's live tiles at most 8 have their row block held by any one device of that row group, and at most 4 have their column block held by any one device of that column group.
All inputs are finite; a program needn't handle non-finite values.
Results may differ from a plain program's by a relative error of at most 0.013.
Values may be sent and summed in bfloat16 or wider, within the bound.
No kernel may reach another device: no remote copies, remote signals or barrier semaphores. Data moves between devices by JAX's collectives and lax.ppermute only.
A program may use at most 128 MiB of HBM per device.

v0:
```python
import math

import jax
import jax.numpy as jnp
from jax import lax
from jax.sharding import PartitionSpec as P


def sum_rows(products, local_ids, alive_mask, total_blocks):
    block_size = products.shape[1]
    feature_width = products.shape[2]
    target_ids = jnp.where(alive_mask, local_ids, total_blocks)
    blank_sum = jnp.zeros((total_blocks, block_size, feature_width), jnp.float32)
    summed = blank_sum.at[target_ids].add(products, mode="drop")
    return summed.reshape(total_blocks * block_size, feature_width)


def on_device(features, weight, bias, cotangent, tile_values, tile_rows, tile_cols, tile_counts):
    row_count = lax.axis_size("row")
    col_count = lax.axis_size("col")
    node_dev, feature_width = features.shape
    slot_count = tile_values.shape[2]
    block_size = tile_values.shape[3]
    blk_dev = node_dev // block_size
    atom_count = node_dev * row_count * col_count
    values = tile_values.reshape(slot_count, block_size, block_size)
    alive_mask = jnp.arange(slot_count) < tile_counts.reshape(())
    row_local = tile_rows.reshape(slot_count) % (blk_dev * col_count)
    col_ids = tile_cols.reshape(slot_count)
    col_local = col_ids // (blk_dev * col_count) * blk_dev + col_ids % blk_dev
    gathered = lax.all_gather(features, "row", axis=0, tiled=True).reshape(
        row_count * blk_dev, block_size, feature_width
    )
    sources = gathered[col_local]
    products = jnp.einsum("kab,kbd->kad", values, sources, preferred_element_type=jnp.float32)
    partial_value = sum_rows(products, row_local, alive_mask, blk_dev * col_count)
    summed = lax.psum_scatter(partial_value, "col", scatter_dimension=0, tiled=True)
    aggregated = summed.astype(jnp.bfloat16)
    pre_act = jnp.dot(aggregated, weight, preferred_element_type=jnp.float32) + bias
    sigm = jax.nn.sigmoid(pre_act)
    output = (pre_act * sigm).astype(jnp.bfloat16)
    grad_pre = (cotangent.astype(jnp.float32) * sigm * (1.0 + pre_act * (1.0 - sigm))).astype(
        jnp.bfloat16
    )
    scale = 1.0 / math.sqrt(atom_count)
    weight_part = jnp.dot(aggregated.T, grad_pre, preferred_element_type=jnp.float32) * scale
    bias_part = jnp.sum(grad_pre.astype(jnp.float32), axis=0) * scale
    weight_grad, bias_grad = lax.psum((weight_part, bias_part), ("row", "col"))
    grad_agg = jnp.dot(grad_pre, weight.T, preferred_element_type=jnp.float32).astype(jnp.bfloat16)
    spread = lax.all_gather(grad_agg, "col", axis=0, tiled=True).reshape(
        col_count * blk_dev, block_size, feature_width
    )
    upstream = spread[row_local]
    back_products = jnp.einsum("kba,kbd->kad", values, upstream, preferred_element_type=jnp.float32)
    grad_partial = sum_rows(back_products, col_local, alive_mask, blk_dev * row_count)
    grad_summed = lax.psum_scatter(
        grad_partial.astype(jnp.bfloat16), "row", scatter_dimension=0, tiled=True
    )
    return (output, grad_summed, weight_grad, bias_grad)


def solution(mesh):
    return jax.shard_map(
        on_device,
        mesh=mesh,
        in_specs=(
            P(("row", "col"), None),
            P(),
            P(),
            P(("row", "col"), None),
            P("row", "col", None, None, None),
            P("row", "col", None),
            P("row", "col", None),
            P("row", "col"),
        ),
        out_specs=(P(("row", "col"), None), P(("row", "col"), None), P(), P()),
        check_vma=False,
    )
```

profile of v0, /device:TPU:0, one launch (start us, length us, event | category | flops | bytes accessed | tf_op | source)
XLA Modules:
  0.0 693.9 jit_solution(4631823555459440356)
XLA Ops:
  7.2 0.0 copy-start
  7.2 0.0 all-gather.3.cloned.1.call-start
  7.2 0.7 all-gather.3.cloned.1.call-update
  7.9 0.0 reduce-scatter.3.cloned.1.call-start
  8.6 0.7 fusion.8
  9.3 0.7 fusion.9
  10.0 75.7 %all-gather.3.cloned.1.call-done = bf16[8192,512]{1,0:T(8,128)(2,1)} async-done(((bf16[512,512]{1,0:T(8,128)(2,1)}), bf16[8192,512]{1,0:T(8,128)(2,1)}) %all-gather.3.cloned.1.call-update) | async-done | bytes 8388624 | tf_op jit(solution)/shard_map/all_gather | solution.py:31
  85.6 8.9 %gather_fusion = bf16[64,128,512]{2,1,0:T(8,128)(2,1)} fusion(bf16[64,128,512]{2,1,0:T(8,128)(2,1)} %bitcast.48, s32[1024]{0:T(1024)S(1)} %pad_clamp_fusion.1), kind=kCustom, calls=%fused_computation | custom fusion | bytes 16777472 | tf_op jit(solution)/shard_map/gather | solution.py:34
  94.5 0.0 copy-done
  94.5 11.5 %convolution_bitcast_fusion.1 = f32[64,128,512]{1,2,0:T(8,128)} fusion(bf16[64,128,512]{2,1,0:T(8,128)(2,1)} %gather_fusion, bf16[1,1,64,128,128]{4,3,2,1,0:T(8,128)(2,1)S(1)} %copy-done), kind=kOutput, calls=%fused_computation.5 | convolution fusion | flops 1073741824 | bytes 27262976 | tf_op jit(solution)/shard_map/kab,kbd->kad/dot_general | solution.py:35
  106.0 17.5 %copy.15 = f32[64,128,512]{2,1,0:T(8,128)} copy(f32[64,128,512]{1,2,0:T(8,128)} %convolution_bitcast_fusion.1) | data formatting | bytes 33554432 | tf_op jit(solution)/shard_map/kab,kbd->kad/dot_general | solution.py:35
  123.5 4.3 broadcast_in_dim.7
  127.8 33.2 %scatter_fusion = f32[32,128,512]{2,1,0:T(8,128)} fusion(f32[32,128,512]{2,1,0:T(8,128)} %broadcast_in_dim.7, s32[64]{0:T(128)S(1)} %fusion.6, f32[64,128,512]{2,1,0:T(8,128)} %copy.15), kind=kCustom, calls=%fused_computation.2 | custom fusion | flops 4194304 | bytes 50331904 | tf_op jit(solution)/shard_map/scatter-add | solution.py:14
  160.9 0.0 copy-start.2
  160.9 0.0 copy-start.3
  161.0 0.0 reduce-scatter.3.cloned.1.call-update
  161.0 0.0 all-gather.5.cloned.1.call-start
  161.0 168.6 %reduce-scatter.3.cloned.1.call-done = f32[512,512]{1,0:T(8,128)} async-done(((f32[4096,512]{1,0:T(8,128)}), f32[512,512]{1,0:T(8,128)}) %reduce-scatter.3.cloned.1.call-update) | async-done | bytes 1048592 | tf_op jit(solution)/shard_map/reduce_scatter | solution.py:37
  329.6 0.0 copy-done.2
  329.6 0.0 copy-done.3
  329.6 3.0 convert_reduce_fusion
  332.7 1.3 convolution_convert_fusion
  333.9 0.0 all-gather.5.cloned.1.call-update
  334.0 0.0 all-reduce.2.cloned.1.call-start
  334.0 2.7 convolution_multiply_fusion
  336.7 0.0 all-reduce.2.cloned.1.call-update
  336.7 0.2 reduce-scatter.5.cloned.1.call-start
  336.9 89.2 %all-gather.5.cloned.1.call-done = bf16[4096,512]{1,0:T(8,128)(2,1)} async-done(((bf16[512,512]{1,0:T(8,128)(2,1)}), bf16[4096,512]{1,0:T(8,128)(2,1)}) %all-gather.5.cloned.1.call-update) | async-done | bytes 4194320 | tf_op jit(solution)/shard_map/all_gather | solution.py:50
  426.1 7.7 %gather_fusion.1 = bf16[64,128,512]{2,1,0:T(8,128)(2,1)} fusion(bf16[32,128,512]{2,1,0:T(8,128)(2,1)} %bitcast.47, s32[1024]{0:T(1024)S(1)} %pad_clamp_fusion), kind=kCustom, calls=%fused_computation.1 | custom fusion | bytes 16777472 | tf_op jit(solution)/shard_map/gather | solution.py:53
  433.8 11.5 %convolution_bitcast_fusion = f32[64,128,512]{1,2,0:T(8,128)} fusion(bf16[64,128,512]{2,1,0:T(8,128)(2,1)} %gather_fusion.1, bf16[1,1,64,128,128]{4,3,2,1,0:T(8,128)(2,1)S(1)} %copy-done), kind=kOutput, calls=%fused_computation.4 | convolution fusion | flops 1073741824 | bytes 27262976 | tf_op jit(solution)/shard_map/kba,kbd->kad/dot_general | solution.py:54
  445.3 17.5 %copy.17 = f32[64,128,512]{2,1,0:T(8,128)} copy(f32[64,128,512]{1,2,0:T(8,128)} %convolution_bitcast_fusion) | data formatting | bytes 33554432 | tf_op jit(solution)/shard_map/kba,kbd->kad/dot_general | solution.py:54
  462.8 7.9 %broadcast_in_dim.8 = f32[64,128,512]{2,1,0:T(8,128)} broadcast(f32[]{:T(128)} %constant.42.clone.1), dimensions={} | broadcast | bytes 16777220 | tf_op jit(solution)/shard_map/broadcast_in_dim | solution.py:13
  470.6 33.4 %scatter_fusion.1 = f32[64,128,512]{2,1,0:T(8,128)} fusion(f32[64,128,512]{2,1,0:T(8,128)} %broadcast_in_dim.8, s32[64]{0:T(128)S(1)} %get-tuple-element.8, f32[64,128,512]{2,1,0:T(8,128)} %copy.17), kind=kCustom, calls=%fused_computation.3 | custom fusion | flops 4194304 | bytes 50331904 | tf_op jit(solution)/shard_map/scatter-add | solution.py:14
  504.0 0.0 copy-start.1
  504.1 9.2 %convert_element_type.29 = bf16[64,128,512]{2,1,0:T(8,128)(2,1)} convert(f32[64,128,512]{2,1,0:T(8,128)} %scatter_fusion.1) | non-fusion elementwise | flops 4194304 | bytes 25165824 | tf_op jit(solution)/shard_map/convert_element_type | solution.py:57
  513.3 0.0 reduce-scatter.5.cloned.1.call-update
  513.3 66.8 %psum.15 = f32[512]{0:T(512)} all-reduce(f32[512]{0:T(512)S(1)} %broadcast_multiply_fusion), channel_id=1, replica_groups=mesh['row'=16,'col'=8] {'row','col'}, use_global_device_ids=true, to_apply=%region_6.7 | all-reduce | flops 512 | bytes 4096 | tf_op jit(solution)/shard_map/psum | solution.py:48
  580.1 0.0 all-reduce.2.cloned.1.call-done
  580.1 105.0 %reduce-scatter.5.cloned.1.call-done = bf16[512,512]{1,0:T(8,128)(2,1)} async-done(((bf16[8192,512]{1,0:T(8,128)(2,1)}), bf16[512,512]{1,0:T(8,128)(2,1)}) %reduce-scatter.5.cloned.1.call-update) | async-done | bytes 524304 | tf_op jit(solution)/shard_map/reduce_scatter | solution.py:56
  685.1 2.3 copy.24
  687.3 0.0 copy-done.1
  (5 shorter events, 0.0 us)
Async XLA Ops:
  7.2 87.4 %copy-start = (bf16[1,1,64,128,128]{4,3,2,1,0:T(8,128)(2,1)S(1)}, bf16[1,1,64,128,128]{4,3,2,1,0:T(8,128)(2,1)}, u32[]{:S(2)}) copy-start(bf16[1,1,64,128,128]{4,3,2,1,0:T(8,128)(2,1)} %param.12) | copy-start | bytes 6291460
  7.2 78.5 %all-gather.3.cloned.1.call-start = ((), (), s32[]{:S(2)}) async-start(), calls=%async_computation.2 | async-start | bytes 8912896 | tf_op jit(solution)/shard_map/all_gather | solution.py:31
  7.9 321.7 %reduce-scatter.3.cloned.1.call-start = ((), (), s32[]{:S(2)}) async-start(), calls=%async_computation.3 | async-start | bytes 9437184 | tf_op jit(solution)/shard_map/reduce_scatter | solution.py:37
  160.9 168.7 %copy-start.2 = (bf16[512,512]{1,0:T(8,128)(2,1)S(1)}, bf16[512,512]{1,0:T(8,128)(2,1)}, u32[]{:S(2)}) copy-start(bf16[512,512]{1,0:T(8,128)(2,1)} %param.9) | copy-start | bytes 1572868
  160.9 168.7 %copy-start.3 = (f32[512]{0:T(512)S(1)}, f32[512]{0:T(512)}, u32[]{:S(2)}) copy-start(f32[512]{0:T(512)} %param.10) | copy-start | bytes 6148
  161.0 265.1 %all-gather.5.cloned.1.call-start = ((), (), s32[]{:S(2)}) async-start(), calls=%async_computation.4 | async-start | bytes 4718592 | tf_op jit(solution)/shard_map/all_gather | solution.py:50
  334.0 246.1 %all-reduce.2.cloned.1.call-start = ((), (), s32[]{:S(2)}) async-start(), calls=%async_computation.6 | async-start | bytes 2097152 | tf_op jit(solution)/shard_map/psum | solution.py:48
  336.7 348.3 %reduce-scatter.5.cloned.1.call-start = ((), (), s32[]{:S(2)}) async-start(), calls=%async_computation.5 | async-start | bytes 8912896 | tf_op jit(solution)/shard_map/reduce_scatter | solution.py:56
  504.0 183.3 %copy-start.1 = (bf16[1,1,64,128,128]{4,3,2,1,0:T(8,128)(2,1)S(1)}, bf16[1,1,64,128,128]{4,3,2,1,0:T(8,128)(2,1)}, u32[]{:S(2)}) copy-start(bf16[1,1,64,128,128]{4,3,2,1,0:T(8,128)(2,1)} %param.12) | copy-start | bytes 6291460
Sparse Core Ops, SparseCore 0:
  10.5 75.1 all-gather.2
  161.1 168.4 reduce-scatter.2
  334.1 91.9 all-gather.4
  431.3 146.5 all-reduce.1
  583.3 101.7 reduce-scatter.4
where the time goes:
time: 695 us; the launch traced here: 694 us
  waiting for transfers between devices  439 us (63%)
  other arithmetic  77.1 us (11%)
  blocking collectives  66.8 us (10%)
  local copies, waits for them, and re-layouts  66 us (9%)
  matrix products  29.9 us (4%)
  between operations  14.5 us (2%)
    reduce_scatter x1, waiting for transfers between devices, on_device(): lax.psum_scatter(partial_value, 'col', scatter_dimension=0, tiled=True)  169 us
    reduce_scatter x1, waiting for transfers between devices, on_device(): lax.psum_scatter(grad_partial.astype(jnp.bfloat16), 'row', scatter_dimens...  105 us
    all_gather x1, waiting for transfers between devices, on_device(): lax.all_gather(grad_agg, 'col', axis=0, tiled=True)  89.2 us
    all_gather x1, waiting for transfers between devices, on_device(): lax.all_gather(features, 'row', axis=0, tiled=True)  75.7 us
    psum x1, blocking collectives, on_device(): weight_grad, bias_grad = lax.psum((weight_part, bias_part), ('row', 'col'))  66.8 us
    scatter-add x2, other arithmetic, sum_rows(): summed = blank_sum.at[target_ids].add(products, mode='drop')  66.5 us
    dot_general x1, local copies, waits for them, and re-layouts, on_device(): jnp.einsum('kba,kbd->kad', values, upstream, preferred_element_type=jnp.f...  17.5 us
    dot_general x1, local copies, waits for them, and re-layouts, on_device(): jnp.einsum('kab,kbd->kad', values, sources, preferred_element_type=jnp.fl...  17.5 us
  transfers between devices with their start and end apart: 5, of which 4 were waited for; matrix products, arithmetic and copies ran while one was open for 13% of the time, Pallas kernels for 0%

commit v1 on v0

v1 whole, which is shorter than its diff:
```python
import functools
import math

import jax
import jax.numpy as jnp
from jax import lax
from jax.experimental import pallas as pl
from jax.experimental.pallas import tpu as pltpu
from jax.sharding import PartitionSpec as P

BF = jnp.bfloat16
F32 = jnp.float32
X = 4
VMEM_LIMIT = 56 * 2**20
UNROLL = 4


def tile_loop(count, step):
    def body(i, carry):
        for j in range(UNROLL):
            k = i * UNROLL + j
            step(k, k < count)
        return carry

    lax.fori_loop(0, (count + UNROLL - 1) // UNROLL, body, 0)


def zero(acc, blocks):
    def body(i, carry):
        acc[i] = jnp.zeros(acc.shape[1:], acc.dtype)
        return carry

    lax.fori_loop(0, blocks, body, 0)


def forward_kernel(cols, rows, count, tiles, near, far, out, source, vals, acc, sems):
    core = lax.axis_index("row") % 2
    copies = [
        pltpu.make_async_copy(near, source.at[0], sems.at[0]),
        pltpu.make_async_copy(far, source.at[1], sems.at[1]),
        pltpu.make_async_copy(tiles, vals, sems.at[2]),
    ]
    for copy in copies:
        copy.start()
    blocks = acc.shape[0] - 1
    zero(acc, blocks)
    for copy in copies:
        copy.wait()

    def step(k, live):
        col = cols[k]
        owner = col // 32
        far_core = lax.rem(lax.rem(owner, 2) + core, 2)
        place = owner // 2 * 4 + lax.rem(col, 4)
        target = jnp.where(live, lax.rem(rows[k], blocks), blocks)
        acc[target] += jnp.dot(vals[k], source[far_core, place], preferred_element_type=F32)

    tile_loop(count[0], step)

    def store(i, carry):
        out[i] = acc[i].astype(BF)
        return carry

    lax.fori_loop(0, blocks, store, 0)


def backward_kernel(cols, rows, count, tiles, spread, far_out, near_out, weight_out, source, shares, vals, acc, sems):
    node_dev = spread.shape[2] * 4
    me = lax.axis_index("row")
    core = me % 2
    my_y = me // 8
    my_x = me // 2 % X
    members = spread.shape[0]
    copies = [
        pltpu.make_async_copy(spread.at[:, pl.ds(0, 512)], source, sems.at[0]),
        pltpu.make_async_copy(spread.at[:, pl.ds(512, 80)], shares, sems.at[1]),
        pltpu.make_async_copy(tiles, vals, sems.at[2]),
    ]
    for copy in copies:
        copy.start()
    blocks = acc.shape[0] - 1
    zero(acc, blocks)
    for copy in copies:
        copy.wait()
    total = shares[0].astype(F32)
    for j in range(1, members):
        total += shares[j].astype(F32)
    weight_out[...] = total

    def step(k, live):
        col = cols[k]
        owner = col // 32
        far_core = lax.rem(owner % 2 + core, 2)
        far_y = lax.rem(owner // 8 + my_y, 2)
        far_x = lax.rem(owner // 2 % X + X - my_x, X)
        target = far_core * 32 + far_y * 16 + far_x * 4 + lax.rem(col, 4)
        target = jnp.where(live, target, blocks)
        row = lax.rem(rows[k], 32)
        start = pl.multiple_of(lax.rem(row, 4) * 128, 128)
        picked = source[row // 4, pl.ds(start, 128), :]
        acc[target] += lax.dot_general(
            vals[k], picked, (((0,), (0,)), ((), ())), preferred_element_type=F32
        )

    tile_loop(count[0], step)

    def store(i, carry):
        near_out[i] = acc[i].astype(BF)
        far_out[i] = acc[i + 32].astype(BF)
        return carry

    lax.fori_loop(0, 32, store, 0)


def dense_kernel(scale, parts, weight, bias, cotangent, output, spread, agg, grad_pre):
    members = parts.shape[0]
    size = 128

    def body(i, bias_sum):
        at = pl.ds(pl.multiple_of(i * size, size), size)
        total = parts[0, at, :].astype(F32)
        for j in range(1, members):
            total += parts[j, at, :].astype(F32)
        value = total.astype(BF)
        agg[at, :] = value
        pre = jnp.dot(value, weight[...], preferred_element_type=F32) + bias[...]
        s = jax.nn.sigmoid(pre)
        output[at, :] = (pre * s).astype(BF)
        grad = (cotangent[at, :].astype(F32) * s * (1.0 + pre * (1.0 - s))).astype(BF)
        grad_pre[at, :] = grad
        back = lax.dot_general(grad, weight[...], (((1,), (1,)), ((), ())), preferred_element_type=F32).astype(BF)
        for j in range(members):
            spread[j, at, :] = back
        return bias_sum + jnp.sum(grad.astype(F32), axis=0, keepdims=True)

    bias_sum = lax.fori_loop(0, agg.shape[0] // size, body, jnp.zeros((1, agg.shape[1]), F32))
    share = agg.shape[1] // members
    bias_high = (bias_sum * scale).astype(BF).astype(F32)
    bias_low = bias_sum * scale - bias_high
    row = lax.broadcasted_iota(jnp.int32, (16, agg.shape[1]), 0)
    tail = jnp.where(row == 0, bias_high, jnp.where(row == 1, bias_low, 0.0)).astype(BF)
    weight_part = lax.dot_general(agg[...], grad_pre[...], (((0,), (0,)), ((), ())), preferred_element_type=F32)
    for j in range(members):
        spread[j, pl.ds(512, share), :] = (weight_part[j * share : (j + 1) * share] * scale).astype(BF)
        spread[j, pl.ds(512 + share, 16), :] = tail


def any_spec():
    return pl.BlockSpec(memory_space=pl.ANY)


def vmem_spec():
    return pl.BlockSpec(memory_space=pltpu.VMEM)


def call(kernel, ids, args, in_specs, out_shape, scratch, flops, moved):
    shapes = [jax.ShapeDtypeStruct(s, d) for s, d in out_shape]
    return pl.pallas_call(
        kernel,
        grid_spec=pltpu.PrefetchScalarGridSpec(
            num_scalar_prefetch=len(ids),
            in_specs=in_specs,
            out_specs=[vmem_spec() for _ in shapes],
            scratch_shapes=scratch,
        ),
        out_shape=shapes,
        compiler_params=pltpu.CompilerParams(vmem_limit_bytes=VMEM_LIMIT),
        cost_estimate=pl.CostEstimate(flops=flops, bytes_accessed=moved, transcendentals=0),
    )(*ids, *args)


def core_swap(value):
    return lax.ppermute(value, "row", [(i, i ^ 1) for i in range(16)])


def row_shift(value, dy, dx):
    def to(i):
        y, x, core = i // 8, i // 2 % X, i % 2
        return (y ^ dy) * 8 + (x + dx) % X * 2 + core

    return lax.ppermute(value, "row", [(i, to(i)) for i in range(16)])


def on_device(features, weight, bias, cotangent, tile_values, tile_rows, tile_cols, tile_counts):
    same_core = [[i for i in range(16) if i % 2 == c] for c in range(2)]
    tiles = tile_values.reshape(64, 128, 128)
    cols = tile_cols.reshape(64)
    rows = tile_rows.reshape(64)
    count = tile_counts.reshape(1)
    scale = 1.0 / math.sqrt(65536)

    near = lax.all_to_all(
        jnp.broadcast_to(features[None], (8, 512, 512)), "row", 0, 0, tiled=True, axis_index_groups=same_core
    )
    far = core_swap(near)
    (partial,) = call(
        forward_kernel,
        (cols, rows, count),
        (tiles, near.reshape(32, 128, 512), far.reshape(32, 128, 512)),
        [any_spec()] * 3,
        [((32, 128, 512), BF)],
        [
            pltpu.VMEM((2, 32, 128, 512), BF),
            pltpu.VMEM((64, 128, 128), BF),
            pltpu.VMEM((33, 128, 512), F32),
            pltpu.SemaphoreType.DMA((3,)),
        ],
        2 * 64 * 128 * 128 * 512,
        14 * 2**20,
    )
    parts = lax.all_to_all(partial.reshape(8, 512, 512), "col", 0, 0, tiled=True)
    output, spread = call(
        functools.partial(dense_kernel, scale),
        (),
        (parts, weight, bias.reshape(1, 512), cotangent),
        [vmem_spec()] * 4,
        [((512, 512), BF), ((8, 592, 512), BF)],
        [pltpu.VMEM((512, 512), BF), pltpu.VMEM((512, 512), BF)],
        6 * 512**3,
        10 * 2**20,
    )
    spread = lax.all_to_all(spread, "col", 0, 0, tiled=True)
    far_part, near_part, share = call(
        backward_kernel,
        (cols, rows, count),
        (tiles, spread),
        [any_spec()] * 2,
        [((32, 128, 512), BF), ((32, 128, 512), BF), ((80, 512), F32)],
        [
            pltpu.VMEM((8, 512, 512), BF),
            pltpu.VMEM((8, 80, 512), BF),
            pltpu.VMEM((64, 128, 128), BF),
            pltpu.VMEM((65, 128, 512), F32),
            pltpu.SemaphoreType.DMA((3,)),
        ],
        2 * 64 * 128 * 128 * 512,
        14 * 2**20,
    )
    far_part = core_swap(far_part).reshape(8, 512, 512)
    near_part = near_part.reshape(8, 512, 512)
    sums = [near_part[i].astype(F32) + far_part[i].astype(F32) for i in range(8)]
    total = sums[0]
    for i in range(1, 8):
        total = total + row_shift(sums[i].astype(BF), i // X, i % X).astype(F32)
    feature_grad = total.astype(BF)

    bias_share = (share[64:65] + share[65:66]).reshape(1, 1, 512)
    weight_share = share[:64].reshape(16, 4, 512)
    pieces = jnp.concatenate(
        [weight_share, jnp.broadcast_to(bias_share, (16, 1, 512)), jnp.zeros((16, 3, 512), F32)], axis=1
    )
    pieces = jnp.sum(lax.all_to_all(pieces, "row", 0, 0, tiled=True), axis=0)
    bias_grad = pieces[4]
    own = lax.all_to_all(jnp.broadcast_to(pieces[None, :4], (16, 4, 512)), "row", 0, 0, tiled=True)
    whole = lax.all_to_all(jnp.broadcast_to(own.reshape(1, 64, 512), (8, 64, 512)), "col", 0, 0, tiled=True)
    weight_grad = whole.reshape(512, 512)
    return (output, feature_grad, weight_grad, bias_grad)


def solution(mesh):
    return jax.shard_map(
        on_device,
        mesh=mesh,
        in_specs=(
            P(("row", "col"), None),
            P(),
            P(),
            P(("row", "col"), None),
            P("row", "col", None, None, None),
            P("row", "col", None),
            P("row", "col", None),
            P("row", "col"),
        ),
        out_specs=(P(("row", "col"), None), P(("row", "col"), None), P(), P()),
        check_vma=False,
    )
```

time: 695 us -> 316 us (0.45)
  waiting for transfers between devices: 439 us -> 38.6 us
  blocking collectives: 66.8 us -> 208 us
  other arithmetic: 77.1 us -> 10.9 us
  local copies, waits for them, and re-layouts: 66 us -> 7.12 us
  matrix products: 29.9 us -> 0 us
  Pallas kernels: 0 us -> 25.8 us
  starting transfers between devices: 0.38 us -> 23.2 us
  between operations: 14.5 us -> 1.38 us
    reduce_scatter x2 -> x0, waiting for transfers between devices: 274 us -> none  [the longest x1 169 us: on_device(): lax.psum_scatter(partial_value, 'col', scatter_dimension=0, tiled=True)]
    all_to_all x0 -> x4, blocking collectives: none -> 208 us  [the longest x1 61.6 us: on_device(): spread = lax.all_to_all(spread, 'col', 0, 0, tiled=True)]
    all_gather x2 -> x0, waiting for transfers between devices: 165 us -> none  [the longest x1 89.2 us: on_device(): lax.all_gather(grad_agg, 'col', axis=0, tiled=True)]
    psum x1 -> x0, blocking collectives: 66.8 us -> none  [on_device(): weight_grad, bias_grad = lax.psum((weight_part, bias_part), ('row', 'col'))]
    scatter-add x2 -> x0, other arithmetic: 66.5 us -> none  [sum_rows(): summed = blank_sum.at[target_ids].add(products, mode='drop')]
    dot_general x2 -> x0, local copies, waits for them, and re-layouts: 34.9 us -> none  [the longest x1 17.5 us: on_device(): jnp.einsum('kba,kbd->kad', values, upstream, preferred_element_type=jnp.f...]
    dot_general x5 -> x0, matrix products: 29.9 us -> none  [the longest x1 11.5 us: on_device(): jnp.einsum('kab,kbd->kad', values, sources, preferred_element_type=jnp.fl...]
    pallas_call x0 -> x3, Pallas kernels: none -> 25.8 us  [call(): pl.pallas_call(kernel, grid_spec=pltpu.PrefetchScalarGridSpec(num_scalar_...]
  transfers between devices with their start and end apart: 5 -> 11, of which waited for: 4 -> 6; matrix products, arithmetic and copies ran while one was open for 13% -> 3% of each run, Pallas kernels for 0% -> 0%
where the time goes in v1:
time: 316 us; the launch traced here: 315 us
  blocking collectives  208 us (66%)
  waiting for transfers between devices  38.6 us (12%)
  Pallas kernels  25.8 us (8%)
  starting transfers between devices  23.2 us (7%)
  other arithmetic  10.9 us (3%)
  local copies, waits for them, and re-layouts  7.12 us (2%)
    all_to_all x1, blocking collectives, on_device(): spread = lax.all_to_all(spread, 'col', 0, 0, tiled=True)  61.6 us
    all_to_all x1, blocking collectives, on_device(): lax.all_to_all(jnp.broadcast_to(features[None], (8, 512, 512)), 'row', 0,...  57.9 us
    all_to_all x1, blocking collectives, on_device(): lax.all_to_all(partial.reshape(8, 512, 512), 'col', 0, 0, tiled=True)  57.3 us
    all_to_all x1, blocking collectives, on_device(): lax.all_to_all(jnp.broadcast_to(pieces[None, :4], (16, 4, 512)), 'row', 0...  31.4 us
    pallas_call x3, Pallas kernels, call(): pl.pallas_call(kernel, grid_spec=pltpu.PrefetchScalarGridSpec(num_scalar_...  25.8 us
    all_to_all x1, waiting for transfers between devices, on_device(): lax.all_to_all(jnp.broadcast_to(own.reshape(1, 64, 512), (8, 64, 512)), '...  19.3 us
    ppermute x7, starting transfers between devices, row_shift(): return lax.ppermute(value, 'row', [(i, to(i)) for i in range(16)])  15 us
    ppermute x7, waiting for transfers between devices, row_shift(): return lax.ppermute(value, 'row', [(i, to(i)) for i in range(16)])  12.1 us
  transfers between devices with their start and end apart: 11, of which 6 were waited for; matrix products, arithmetic and copies ran while one was open for 3% of the time, Pallas kernels for 0%

profile of v1, /device:TPU:0, one launch (start us, length us, event | category | flops | bytes accessed | tf_op | source)
XLA Modules:
  0.0 315.2 jit_solution(16495332034215542229)
XLA Ops:
  0.6 1.4 broadcast_in_dim.14
  2.0 57.9 %all_to_all.30 = bf16[8,512,512]{2,1,0:T(8,128)(2,1)S(1)} all-to-all(bf16[8,512,512]{2,1,0:T(8,128)(2,1)S(1)} %broadcast_in_dim.14), channel_id=1, replica_groups={{0,16,32,48,64,80,96,112},{8,24,40,56,72,88,104,120},{1,17,33,49,65,81,..., dimensions={0} | all-to-all | bytes 8388608 | tf_op jit(solution)/shard_map/all_to_all | solution.py:192
  60.0 0.0 copy-start
  60.0 0.0 collective-permute-start
  60.6 6.5 %collective-permute-done = bf16[8,512,512]{2,1,0:T(8,128)(2,1)S(1)} collective-permute-done((bf16[8,512,512]{2,1,0:T(8,128)(2,1)S(1)}, bf16[8,512,512]{2,1,0:T(8,128)(2,1)S(1)}, u32[]{:S(2)}, u32[]{:S(2)}) %collective-permute-start) | collective-permute-done | bytes 4194336 | tf_op jit(solution)/shard_map/ppermute | solution.py:173
  67.1 0.0 copy-start.1
  67.1 2.0 copy-done.1
  69.1 0.0 copy-done
  69.1 8.7 %shard_map.111 = bf16[32,128,512]{2,1,0:T(8,128)(2,1)} custom-call(s32[64]{0:T(128)} %bitcast.48, s32[64]{0:T(128)} %bitcast.50, s32[1]{0:T(128)} %bitcast.34.count, bf16[64,128,128]{2,1,0:T(8,128)(2,1)} %bitcast.38, bf16[32,128,512]{2,1,0:T(8,128)(2,1)} %bitcast.36, bf16[32,128,512]{2,1,0:T(8,128)(2,1)} %bitcast.40), custom_call_target="tpu_custom_call" | custom-call | flops 1073741824 | bytes 14680064 | tf_op jit(solution)/shard_map/pallas_call | solution.py:158
  77.8 57.3 %all_to_all.31.parts = bf16[8,512,512]{2,1,0:T(8,128)(2,1)} all-to-all(bf16[8,512,512]{2,1,0:T(8,128)(2,1)} %bitcast.37), channel_id=1, replica_groups=mesh['row'=16,'col'=8] {'col'}, dimensions={0} | all-to-all | bytes 8388608 | tf_op jit(solution)/shard_map/all_to_all | solution.py:211
  135.2 7.3 %shard_map.112 = (bf16[512,512]{1,0:T(8,128)(2,1)}, bf16[8,592,512]{2,1,0:T(8,128)(2,1)}) custom-call(bf16[8,512,512]{2,1,0:T(8,128)(2,1)} %all_to_all.31.parts, bf16[512,512]{1,0:T(8,128)(2,1)} %weight.1, f32[1,512]{1,0:T(1,128)} %bitcast.52, bf16[512,512]{1,0:T(8,128)(2,1)} %cotangent.1), custom_call_target="tpu_custom_call" | custom-call | flops 805306368 | bytes 10485760 | tf_op jit(solution)/shard_map/pallas_call | solution.py:158
  142.4 61.6 %all_to_all.32.spread = bf16[8,592,512]{2,1,0:T(8,128)(2,1)} all-to-all(bf16[8,592,512]{2,1,0:T(8,128)(2,1)} %get-tuple-element.10), channel_id=1, replica_groups=mesh['row'=16,'col'=8] {'col'}, dimensions={0} | all-to-all | bytes 9699328 | tf_op jit(solution)/shard_map/all_to_all | solution.py:222
  204.0 9.7 %shard_map.113 = (bf16[32,128,512]{2,1,0:T(8,128)(2,1)}, bf16[32,128,512]{2,1,0:T(8,128)(2,1)}, f32[80,512]{1,0:T(8,128)}) custom-call(s32[64]{0:T(128)} %bitcast.49, s32[64]{0:T(128)} %bitcast.51, s32[1]{0:T(128)} %bitcast.35.count, bf16[64,128,128]{2,1,0:T(8,128)(2,1)} %bitcast.39, bf16[8,592,512]{2,1,0:T(8,128)(2,1)} %all_to_all.32.spread), custom_call_target="tpu_custom_call" | custom-call | flops 1073741824 | bytes 14680064 | tf_op jit(solution)/shard_map/pallas_call | solution.py:158
  213.8 0.9 collective-permute-start.1
  214.7 0.1 pad.2.clone
  214.7 0.9 slice.95
  215.7 0.8 slice_add_fusion
  216.5 0.8 maximum_maximum_fusion
  217.3 3.8 %all-to-all-start.3 = ((f32[16,8,512]{2,1,0:T(8,128)}), f32[16,8,512]{2,1,0:T(8,128)S(1)}, u32[]{:S(2)}, u32[]{:S(2)}) async-start(f32[16,8,512]{2,1,0:T(8,128)} %maximum_maximum_fusion), calls=%async_computation.3 | async-start | bytes 524288 | tf_op jit(solution)/shard_map/all_to_all | solution.py:252
  221.2 0.6 collective-permute-done.1
  221.8 6.1 %add_convert_fusion.6 = (bf16[4,128,512]{2,1,0:T(8,128)(2,1)S(1)}, bf16[4,128,512]{2,1,0:T(8,128)(2,1)}, bf16[4,128,512]{2,1,0:T(8,128)(2,1)}, bf16[4,128,512]{2...) fusion(bf16[32,128,512]{2,1,0:T(8,128)(2,1)} %collective-permut, ...), kind=kLoop, calls=%fused_computation.14 | loop fusion | flops 8126464 | bytes 13107200 | tf_op jit(solution)/shard_map/convert_element_type | solution.py:244
  227.9 4.9 %collective-permute-start.8 = (bf16[512,512]{1,0:T(8,128)(2,1)}, bf16[512,512]{1,0:T(8,128)(2,1)S(1)}, u32[]{:S(2)}, u32[]{:S(2)}) collective-permute-start(bf16[512,512]{1,0:T(8,128)(2,1)} %bitcast.15), channel_id=1, source_target_pairs={{0,112},{8,120},{16,64},{24,72},{32,80},{40,88},{48,96},{56,104},{... | collective-permute-start | bytes 1572872 | tf_op jit(solution)/shard_map/ppermute | solution.py:181
  232.8 1.7 collective-permute-start.7
  234.5 0.0 all-to-all-done.3
  234.6 31.4 %all_to_all.33 = f32[16,4,512]{2,1,0:T(4,128)S(1)} all-to-all(f32[16,4,512]{2,1,0:T(4,128)S(1)} %broadcast_in_dim.33), channel_id=1, replica_groups=mesh['row'=16,'col'=8] {'row'}, dimensions={0} | all-to-all | bytes 262144 | tf_op jit(solution)/shard_map/all_to_all | solution.py:254
  266.0 1.1 broadcast_in_dim.35
  267.1 3.6 %all-to-all-start.5 = ((f32[8,64,512]{2,1,0:T(8,128)}), f32[8,64,512]{2,1,0:T(8,128)S(1)}, u32[]{:S(2)}, u32[]{:S(2)}) async-start(f32[8,64,512]{2,1,0:T(8,128)} %broadcast_in_dim.35), calls=%async_computation.5 | async-start | bytes 2097152 | tf_op jit(solution)/shard_map/all_to_all | solution.py:255
  270.7 4.5 %collective-permute-start.6 = (bf16[512,512]{1,0:T(8,128)(2,1)}, bf16[512,512]{1,0:T(8,128)(2,1)}, u32[]{:S(2)}, u32[]{:S(2)}) collective-permute-start(bf16[512,512]{1,0:T(8,128)(2,1)} %bitcast.46), channel_id=1, source_target_pairs={{0,80},{8,88},{16,96},{24,104},{32,112},{40,120},{48,64},{56,72},{... | collective-permute-start | bytes 1572872 | tf_op jit(solution)/shard_map/ppermute | solution.py:181
  275.2 0.7 collective-permute-start.5
  275.9 1.0 collective-permute-start.4
  277.0 0.0 collective-permute-done.8
  277.0 1.7 collective-permute-start.3
  278.7 0.0 collective-permute-done.7
  278.7 0.4 collective-permute-start.2
  279.0 0.6 slice.109
  279.6 19.3 %all-to-all-done.5 = f32[8,64,512]{2,1,0:T(8,128)S(1)} async-done(((f32[8,64,512]{2,1,0:T(8,128)}), f32[8,64,512]{2,1,0:T(8,128)S(1)}, u32[]{:S(2)}, u32[]{:S(2)}) %all-to-all-start.5) | async-done | bytes 1048608 | tf_op jit(solution)/shard_map/all_to_all | solution.py:255
  299.0 1.1 collective-permute-done.6
  300.1 8.5 %collective-permute-done.5 = bf16[512,512]{1,0:T(8,128)(2,1)} collective-permute-done((bf16[512,512]{1,0:T(8,128)(2,1)}, bf16[512,512]{1,0:T(8,128)(2,1)}, u32[]{:S(2)}, u32[]{:S(2)}) %collective-permute-start.5) | collective-permute-done | bytes 524320 | tf_op jit(solution)/shard_map/ppermute | solution.py:181
  308.5 0.0 collective-permute-done.4
  308.5 0.0 collective-permute-done.3
  308.5 2.5 collective-permute-done.2
  311.0 3.2 %fusion.6 = bf16[512,512]{1,0:T(8,128)(2,1)} fusion(f32[4,128,512]{2,1,0:T(8,128)S(1)} %get-tuple-element.21, bf16[512,512]{1,0:T(8,128)(2,1)S(1)} %collective-permute-done.8, bf16[512,512]{1,0:T(8,128)(2,1)} %collective-permute-done.7, bf16[512,512]{1,0:T(8,128)(2,1)} %collective-permute-done.6, bf16[512,512]{1,0:T(8,128)(2,1)} %collective-permute-done.5, ...), kind=kLoop, calls=%fused_computation.7 | loop fusion | flops 3932160 | bytes 5242880 | tf_op jit(solution)/shard_map/convert_element_type | solution.py:245
  314.2 1.0 copy.14
  (7 shorter events, 0.1 us)
Async XLA Ops:
  60.0 9.1 %copy-start = (bf16[8,512,512]{2,1,0:T(8,128)(2,1)}, bf16[8,512,512]{2,1,0:T(8,128)(2,1)S(1)}, u32[]{:S(2)}) copy-start(bf16[8,512,512]{2,1,0:T(8,128)(2,1)S(1)} %all_to_all.30) | copy-start | bytes 12582916
  60.0 7.2 %collective-permute-start = (bf16[8,512,512]{2,1,0:T(8,128)(2,1)S(1)}, bf16[8,512,512]{2,1,0:T(8,128)(2,1)S(1)}, u32[]{:S(2)}, u32[]{:S(2)}) collective-permute-start(bf16[8,512,512]{2,1,0:T(8,128)(2,1)S(1)} %all_to_all.30), channel_id=1, source_target_pairs={{0,8},{8,0},{16,24},{24,16},{32,40},{40,32},{48,56},{56,48},{64,72... | collective-permute-start | bytes 12582920 | tf_op jit(solution)/shard_map/ppermute | solution.py:173
  67.1 2.0 copy-start.1
  213.8 8.0 %collective-permute-start.1 = (bf16[32,128,512]{2,1,0:T(8,128)(2,1)}, bf16[32,128,512]{2,1,0:T(8,128)(2,1)}, u32[]{:S(2)}, u32[]{:S(2)}) collective-permute-start(bf16[32,128,512]{2,1,0:T(8,128)(2,1)} %get-tuple-element.12), channel_id=1, source_target_pairs={{0,8},{8,0},{16,24},{24,16},{32,40},{40,32},{48,56},{56,48},{64,72... | collective-permute-start | bytes 12582920 | tf_op jit(solution)/shard_map/ppermute | solution.py:173
  217.3 17.2 %all-to-all-start.3 = ((f32[16,8,512]{2,1,0:T(8,128)}), f32[16,8,512]{2,1,0:T(8,128)S(1)}, u32[]{:S(2)}, u32[]{:S(2)}) async-start(f32[16,8,512]{2,1,0:T(8,128)} %maximum_maximum_fusion), calls=%async_computation.3 | async-start | bytes 524288 | tf_op jit(solution)/shard_map/all_to_all | solution.py:252
  227.9 49.1 %collective-permute-start.8 = (bf16[512,512]{1,0:T(8,128)(2,1)}, bf16[512,512]{1,0:T(8,128)(2,1)S(1)}, u32[]{:S(2)}, u32[]{:S(2)}) collective-permute-start(bf16[512,512]{1,0:T(8,128)(2,1)} %bitcast.15), channel_id=1, source_target_pairs={{0,112},{8,120},{16,64},{24,72},{32,80},{40,88},{48,96},{56,104},{... | collective-permute-start | bytes 1572872 | tf_op jit(solution)/shard_map/ppermute | solution.py:181
  232.8 45.9 %collective-permute-start.7 = (bf16[512,512]{1,0:T(8,128)(2,1)}, bf16[512,512]{1,0:T(8,128)(2,1)}, u32[]{:S(2)}, u32[]{:S(2)}) collective-permute-start(bf16[512,512]{1,0:T(8,128)(2,1)} %bitcast.14), channel_id=1, source_target_pairs={{0,96},{8,104},{16,112},{24,120},{32,64},{40,72},{48,80},{56,88},{... | collective-permute-start | bytes 1572872 | tf_op jit(solution)/shard_map/ppermute | solution.py:181
  267.1 31.8 %all-to-all-start.5 = ((f32[8,64,512]{2,1,0:T(8,128)}), f32[8,64,512]{2,1,0:T(8,128)S(1)}, u32[]{:S(2)}, u32[]{:S(2)}) async-start(f32[8,64,512]{2,1,0:T(8,128)} %broadcast_in_dim.35), calls=%async_computation.5 | async-start | bytes 2097152 | tf_op jit(solution)/shard_map/all_to_all | solution.py:255
  270.7 29.4 %collective-permute-start.6 = (bf16[512,512]{1,0:T(8,128)(2,1)}, bf16[512,512]{1,0:T(8,128)(2,1)}, u32[]{:S(2)}, u32[]{:S(2)}) collective-permute-start(bf16[512,512]{1,0:T(8,128)(2,1)} %bitcast.46), channel_id=1, source_target_pairs={{0,80},{8,88},{16,96},{24,104},{32,112},{40,120},{48,64},{56,72},{... | collective-permute-start | bytes 1572872 | tf_op jit(solution)/shard_map/ppermute | solution.py:181
  275.2 33.3 %collective-permute-start.5 = (bf16[512,512]{1,0:T(8,128)(2,1)}, bf16[512,512]{1,0:T(8,128)(2,1)}, u32[]{:S(2)}, u32[]{:S(2)}) collective-permute-start(bf16[512,512]{1,0:T(8,128)(2,1)} %bitcast.45), channel_id=1, source_target_pairs={{0,64},{8,72},{16,80},{24,88},{32,96},{40,104},{48,112},{56,120},{... | collective-permute-start | bytes 1572872 | tf_op jit(solution)/shard_map/ppermute | solution.py:181
  275.9 32.6 %collective-permute-start.4 = (bf16[512,512]{1,0:T(8,128)(2,1)}, bf16[512,512]{1,0:T(8,128)(2,1)}, u32[]{:S(2)}, u32[]{:S(2)}) collective-permute-start(bf16[512,512]{1,0:T(8,128)(2,1)} %bitcast.44), channel_id=1, source_target_pairs={{0,48},{8,56},{16,0},{24,8},{32,16},{40,24},{48,32},{56,40},{64,11... | collective-permute-start | bytes 1572872 | tf_op jit(solution)/shard_map/ppermute | solution.py:181
  277.0 31.5 %collective-permute-start.3 = (bf16[512,512]{1,0:T(8,128)(2,1)}, bf16[512,512]{1,0:T(8,128)(2,1)}, u32[]{:S(2)}, u32[]{:S(2)}) collective-permute-start(bf16[512,512]{1,0:T(8,128)(2,1)} %bitcast.43), channel_id=1, source_target_pairs={{0,32},{8,40},{16,48},{24,56},{32,0},{40,8},{48,16},{56,24},{64,96... | collective-permute-start | bytes 1572872 | tf_op jit(solution)/shard_map/ppermute | solution.py:181
  278.7 32.4 %collective-permute-start.2 = (bf16[512,512]{1,0:T(8,128)(2,1)S(1)}, bf16[512,512]{1,0:T(8,128)(2,1)}, u32[]{:S(2)}, u32[]{:S(2)}) collective-permute-start(bf16[512,512]{1,0:T(8,128)(2,1)S(1)} %bitcast.42), channel_id=1, source_target_pairs={{0,16},{8,24},{16,32},{24,40},{32,48},{40,56},{48,0},{56,8},{64,80... | collective-permute-start | bytes 1572872 | tf_op jit(solution)/shard_map/ppermute | solution.py:181

commit v2 on v0

v2 whole, which is shorter than its diff:
```python
import functools
import math

import jax
import jax.numpy as jnp
from jax import lax
from jax.experimental import pallas as pl
from jax.experimental.pallas import tpu as pltpu
from jax.sharding import PartitionSpec as P

BF = jnp.bfloat16
F32 = jnp.float32
VMEM_LIMIT = 56 * 2**20
UNROLL = 16
HALF = 256
SHARE = 32
TAIL = 16
LINES = [[(chip * 2 + core) * 8 + q for core in range(2) for q in range(8)] for chip in range(8)]


def tile_loop(count, acc, step):
    def body(i, carry):
        found = [step(i * UNROLL + j, i * UNROLL + j < count) for j in range(UNROLL)]
        for target, product in found:
            acc[target] += product
        return carry

    lax.fori_loop(0, (count + UNROLL - 1) // UNROLL, body, 0)


def loop(n, step):
    def body(i, carry):
        step(i)
        return carry

    lax.fori_loop(0, n, body, 0)


def start_loads(sources, acc, sems):
    copies = [pltpu.make_async_copy(a, b, sems.at[i]) for i, (a, b) in enumerate(sources)]
    for copy in copies:
        copy.start()

    @functools.partial(loop, acc.shape[0] - 1)
    def _(i):
        acc[i] = jnp.zeros(acc.shape[1:], F32)

    for copy in copies:
        copy.wait()


def copies_kernel(features, out, sems):
    copies = [
        pltpu.make_async_copy(features.at[:, pl.ds(j % 2 * HALF, HALF)], out.at[j], sems.at[j]) for j in range(16)
    ]
    for copy in copies:
        copy.start()
    for copy in copies:
        copy.wait()


def forward_kernel(ids, other_ids, tiles, other_tiles, gathered, out, source, vals, acc, sems):
    core = lax.axis_index("row") % 2
    start_loads([(tiles, vals.at[0]), (other_tiles, vals.at[1]), (gathered, source)], acc, sems)
    for side, table in enumerate((ids, other_ids)):
        group = core if side == 0 else 1 - core

        @functools.partial(tile_loop, table[128], acc)
        def _(k, live, side=side, table=table, group=group):
            col, row = table[k], table[64 + k]
            start = pl.multiple_of(lax.rem(col, 4) * 128, 128)
            picked = source[col // 32, pl.ds(start, 128), :]
            target = jnp.where(live, group * 32 + lax.rem(row, 32), 64)
            return target, jnp.dot(vals[side, k], picked, preferred_element_type=F32)

    @functools.partial(loop, 64)
    def _(i):
        out[i] = acc[i].astype(BF)


def backward_kernel(ids, other_ids, tiles, other_tiles, spread, out, source, vals, acc, sems):
    core = lax.axis_index("row") % 2
    start_loads(
        [(tiles, vals.at[0]), (other_tiles, vals.at[1]), (spread, source)], acc, sems
    )
    for side, table in enumerate((ids, other_ids)):
        group = core if side == 0 else 1 - core

        @functools.partial(tile_loop, table[128], acc)
        def _(k, live, side=side, table=table, group=group):
            col, row = table[k], lax.rem(table[64 + k], 32)
            start = pl.multiple_of(lax.rem(row, 4) * 128, 128)
            picked = source[group * 8 + row // 4, pl.ds(start, 128), :]
            target = jnp.where(live, col // 32 * 4 + lax.rem(col, 4), 64)
            return target, lax.dot_general(
                vals[side, k], picked, (((0,), (0,)), ((), ())), preferred_element_type=F32
            )

    @functools.partial(loop, 64)
    def _(i):
        out[i] = acc[i].astype(BF)


def row_place():
    me = lax.axis_index("row")
    return lax.rem(me // 2, 4), lax.rem(me, 2)


def dense_kernel(scale, parts, weight, bias, cotangent, output, spread, chunks, agg, grad_pre, product):
    size = 128

    def body(i, bias_sum):
        at = pl.ds(pl.multiple_of(i * size, size), size)
        for half in range(2):
            total = parts[half * 8, at, :].astype(F32)
            for j in range(1, 8):
                total += parts[half * 8 + j, at, :].astype(F32)
            agg[at, half * HALF : (half + 1) * HALF] = total.astype(BF)
        pre = jnp.dot(agg[at, :], weight[...], preferred_element_type=F32) + bias[...]
        s = jax.nn.sigmoid(pre)
        output[at, :] = (pre * s).astype(BF)
        grad = (cotangent[at, :].astype(F32) * s * (1.0 + pre * (1.0 - s))).astype(BF)
        grad_pre[at, :] = grad
        back = lax.dot_general(grad, weight[...], (((1,), (1,)), ((), ())), preferred_element_type=F32).astype(BF)
        for j in range(16):
            spread[j, at, :] = back[:, j // 8 * HALF : (j // 8 + 1) * HALF]
        return bias_sum + jnp.sum(grad.astype(F32), axis=0, keepdims=True)

    bias_sum = lax.fori_loop(0, agg.shape[0] // size, body, jnp.zeros((1, agg.shape[1]), F32)) * scale
    product[...] = lax.dot_general(agg[...], grad_pre[...], (((0,), (0,)), ((), ())), preferred_element_type=F32)
    tail = jnp.broadcast_to(bias_sum, (TAIL, agg.shape[1])).astype(BF)
    my_x, my_core = row_place()
    for core in range(2):
        for x in range(4):
            for y in range(2):
                owner = y * 8 + lax.rem(my_x + x, 4) * 2 + lax.rem(my_core + core, 2)
                rows = product[pl.ds(pl.multiple_of(owner * SHARE, SHARE), SHARE), :]
                chunks[core, x, y, :SHARE, :] = (rows * scale).astype(BF)
                chunks[core, x, y, SHARE:, :] = tail


def place_kernel(own, moved_1, moved_2, moved_3, weight_grad, bias_grad):
    my_x, my_core = row_place()
    my_z = lax.axis_index("col") // 2
    for d, piece in enumerate((own, moved_1, moved_2, moved_3)):
        for j in range(4):
            flat = lax.rem(my_z + 4 - d, 4) * 4 + j
            core, x, y = flat // 8, lax.rem(flat // 2, 4), j % 2
            owner = y * 8 + lax.rem(my_x + 4 - x, 4) * 2 + lax.rem(my_core + core, 2)
            at = pl.ds(pl.multiple_of(owner * SHARE, SHARE), SHARE)
            weight_grad[at, :] = piece[j, :SHARE, :].astype(F32)
    bias_grad[...] = own[0, SHARE : SHARE + 1, :].astype(F32)


def final_kernel(parts, out):
    @functools.partial(loop, 4)
    def _(i):
        at = pl.ds(pl.multiple_of(i * 128, 128), 128)
        for half in range(2):
            total = parts[half, at, :].astype(F32)
            for j in range(1, 8):
                total += parts[2 * j + half, at, :].astype(F32)
            out[at, half * HALF : (half + 1) * HALF] = total.astype(BF)


def any_spec():
    return pl.BlockSpec(memory_space=pl.ANY)


def vmem_spec():
    return pl.BlockSpec(memory_space=pltpu.VMEM)


def call(kernel, args, out_shape, ids=(), in_specs=None, out_specs=None, scratch=(), flops=0, moved=4 * 2**20):
    shapes = [jax.ShapeDtypeStruct(s, d) for s, d in out_shape]
    return pl.pallas_call(
        kernel,
        grid_spec=pltpu.PrefetchScalarGridSpec(
            num_scalar_prefetch=len(ids),
            in_specs=in_specs or [vmem_spec() for _ in args],
            out_specs=out_specs or [vmem_spec() for _ in shapes],
            scratch_shapes=scratch,
        ),
        out_shape=shapes,
        compiler_params=pltpu.CompilerParams(vmem_limit_bytes=VMEM_LIMIT),
        cost_estimate=pl.CostEstimate(flops=flops, bytes_accessed=moved, transcendentals=0),
    )(*ids, *args)


def core_swap(value):
    return lax.ppermute(value, "row", [(i, i ^ 1) for i in range(16)])


def swap_y(value, high, low):
    to = [(i, i ^ (64 * high + low)) for i in range(128)]
    return lax.ppermute(value, ("row", "col"), to)


def shift(value, axis, d):
    if axis == "row":
        to = [(i, i // 8 * 8 + (i + 2 * d) % 8) for i in range(16)]
    else:
        to = [(i, (i + 2 * d) % 8) for i in range(8)]
    return lax.ppermute(value, axis, to)


def add(*parts):
    total = parts[0].astype(F32)
    for part in parts[1:]:
        total = total + part.astype(F32)
    return total.astype(BF)


def plane_sum(chunks):
    part = add(chunks[0], core_swap(chunks[1]))
    part = add(part[0], *(shift(part[d], "row", d) for d in range(1, 4)))
    return add(part, swap_y(part, 0, 1), swap_y(part, 1, 0), swap_y(part, 1, 1))


def ring(part, axis):
    return (part, *(shift(part, axis, d) for d in range(1, 4)))


def z_sum(chunks):
    z = lax.axis_index("col") // 2
    parts = chunks.reshape(4, 4, *chunks.shape[-2:])

    def part_of(d):
        return lax.dynamic_index_in_dim(parts, (z + d) % 4, 0, keepdims=False)

    return ring(add(part_of(0), *(shift(part_of(d), "col", d) for d in range(1, 4))), "col")


def row_exchange(value):
    return lax.all_to_all(value, "row", 0, 0, tiled=True)


def line_exchange(value):
    return lax.all_to_all(value, ("row", "col"), 0, 0, tiled=True, axis_index_groups=LINES)


def on_device(features, weight, bias, cotangent, tile_values, tile_rows, tile_cols, tile_counts):
    tiles = tile_values.reshape(64, 128, 128)
    ids = jnp.concatenate([tile_cols.reshape(64), tile_rows.reshape(64), tile_counts.reshape(1)])
    other_tiles, other_ids = core_swap(tiles), core_swap(ids)
    scale = 1.0 / math.sqrt(65536)
    tables = (ids, other_ids)
    scratch = [
        pltpu.VMEM((16, 512, HALF), BF),
        pltpu.VMEM((2, 64, 128, 128), BF),
        pltpu.VMEM((65, 128, HALF), F32),
        pltpu.SemaphoreType.DMA((3,)),
    ]
    work = dict(
        ids=tables, in_specs=[any_spec()] * 3, scratch=scratch, flops=2 * 64 * 128 * 128 * 512, moved=16 * 2**20
    )

    (copies,) = call(
        copies_kernel,
        (features,),
        [((16, 512, HALF), BF)],
        out_specs=[any_spec()],
        scratch=[pltpu.SemaphoreType.DMA((16,))],
    )
    gathered = row_exchange(copies)
    (partial,) = call(forward_kernel, (tiles, other_tiles, gathered), [((64, 128, HALF), BF)], **work)
    parts = line_exchange(partial.reshape(16, 512, HALF))
    output, spread, chunks = call(
        functools.partial(dense_kernel, scale),
        (parts, weight, bias.reshape(1, 512), cotangent),
        [((512, 512), BF), ((16, 512, HALF), BF), ((2, 4, 2, SHARE + TAIL, 512), BF)],
        scratch=[pltpu.VMEM((512, 512), BF), pltpu.VMEM((512, 512), BF), pltpu.VMEM((512, 512), F32)],
        flops=6 * 512**3,
        moved=8 * 2**20,
    )
    spread = line_exchange(spread)
    chunks, spread = lax.optimization_barrier((plane_sum(chunks), spread))
    (back,) = call(backward_kernel, (tiles, other_tiles, spread), [((64, 128, HALF), BF)], **work)
    chunks, back = lax.optimization_barrier((jnp.stack(ring(chunks, "row")), back))
    back = row_exchange(back.reshape(16, 512, HALF))
    chunks = jnp.stack([chunks, core_swap(chunks)])
    weight_grad, bias_grad = call(place_kernel, z_sum(chunks), [((512, 512), F32), ((1, 512), F32)])
    (feature_grad,) = call(final_kernel, (back,), [((512, 512), BF)])
    return (output, feature_grad, weight_grad, bias_grad.reshape(512))


def solution(mesh):
    return jax.shard_map(
        on_device,
        mesh=mesh,
        in_specs=(
            P(("row", "col"), None),
            P(),
            P(),
            P(("row", "col"), None),
            P("row", "col", None, None, None),
            P("row", "col", None),
            P("row", "col", None),
            P("row", "col"),
        ),
        out_specs=(P(("row", "col"), None), P(("row", "col"), None), P(), P()),
        check_vma=False,
    )
```

time: 695 us -> 281 us (0.40)
  waiting for transfers between devices: 439 us -> 140 us
  other arithmetic: 77.1 us -> 0.53 us
  local copies, waits for them, and re-layouts: 66 us -> 1.5 us
  starting transfers between devices: 0.38 us -> 44.7 us
  Pallas kernels: 0 us -> 35.6 us
  matrix products: 29.9 us -> 0 us
  between operations: 14.5 us -> 1.51 us
  blocking collectives: 66.8 us -> 54.7 us
    reduce_scatter x2 -> x0, waiting for transfers between devices: 274 us -> none  [the longest x1 169 us: on_device(): lax.psum_scatter(partial_value, 'col', scatter_dimension=0, tiled=True)]
    all_gather x2 -> x0, waiting for transfers between devices: 165 us -> none  [the longest x1 89.2 us: on_device(): lax.all_gather(grad_agg, 'col', axis=0, tiled=True)]
    all_to_all x0 -> x3, waiting for transfers between devices: none -> 75.7 us  [the longest x2 75.7 us: row_exchange(): return lax.all_to_all(value, 'row', 0, 0, tiled=True)]
    psum x1 -> x0, blocking collectives: 66.8 us -> none  [on_device(): weight_grad, bias_grad = lax.psum((weight_part, bias_part), ('row', 'col'))]
    scatter-add x2 -> x0, other arithmetic: 66.5 us -> none  [sum_rows(): summed = blank_sum.at[target_ids].add(products, mode='drop')]
    ppermute x0 -> x19, waiting for transfers between devices: none -> 64.5 us  [the longest x3 38.7 us: swap_y(): return lax.ppermute(value, ('row', 'col'), to)]
    all_to_all x0 -> x1, blocking collectives: none -> 54.7 us  [line_exchange(): lax.all_to_all(value, ('row', 'col'), 0, 0, tiled=True, axis_index_groups...]
    pallas_call x0 -> x6, Pallas kernels: none -> 35.6 us  [call(): pl.pallas_call(kernel, grid_spec=pltpu.PrefetchScalarGridSpec(num_scalar_...]
  transfers between devices with their start and end apart: 5 -> 22, of which waited for: 4 -> 14; matrix products, arithmetic and copies ran while one was open for 13% -> 0% of each run, Pallas kernels for 0% -> 4%
where the time goes in v2:
time: 281 us; the launch traced here: 279 us
  waiting for transfers between devices  140 us (50%)
  blocking collectives  54.7 us (19%)
  starting transfers between devices  44.7 us (16%)
  Pallas kernels  35.6 us (13%)
    all_to_all x2, waiting for transfers between devices, row_exchange(): return lax.all_to_all(value, 'row', 0, 0, tiled=True)  75.7 us
    all_to_all x1, blocking collectives, line_exchange(): lax.all_to_all(value, ('row', 'col'), 0, 0, tiled=True, axis_index_groups...  54.7 us
    ppermute x3, waiting for transfers between devices, swap_y(): return lax.ppermute(value, ('row', 'col'), to)  38.7 us
    pallas_call x6, Pallas kernels, call(): pl.pallas_call(kernel, grid_spec=pltpu.PrefetchScalarGridSpec(num_scalar_...  35.6 us
    ppermute x12, starting transfers between devices, shift(): return lax.ppermute(value, axis, to)  21.7 us
    ppermute x12, waiting for transfers between devices, shift(): return lax.ppermute(value, axis, to)  19.7 us
    all_to_all x2, starting transfers between devices, row_exchange(): return lax.all_to_all(value, 'row', 0, 0, tiled=True)  11.9 us
    ppermute x4, waiting for transfers between devices, core_swap(): return lax.ppermute(value, 'row', [(i, i ^ 1) for i in range(16)])  6.18 us
  transfers between devices with their start and end apart: 22, of which 14 were waited for; matrix products, arithmetic and copies ran while one was open for 0% of the time, Pallas kernels for 4%

profile of v2, /device:TPU:0, one launch (start us, length us, event | category | flops | bytes accessed | tf_op | source)
XLA Modules:
  0.0 278.8 jit_solution(3318582882716396294)
XLA Ops:
  0.6 3.2 %shard_map.111 = bf16[16,512,256]{2,1,0:T(8,128)(2,1)} custom-call(bf16[512,512]{1,0:T(8,128)(2,1)} %features.1), custom_call_target="tpu_custom_call" | custom-call | bytes 4194304 | tf_op jit(solution)/shard_map/pallas_call | solution.py:176
  3.8 0.0 copy-start
  3.9 0.0 copy-start.8
  3.9 0.0 copy-start.9
  3.9 7.3 %all-to-all-start = ((bf16[16,512,256]{2,1,0:T(8,128)(2,1)}), bf16[16,512,256]{2,1,0:T(8,128)(2,1)}, u32[]{:S(2)}, u32[]{:S(2)}) async-start(bf16[16,512,256]{2,1,0:T(8,128)(2,1)} %shard_map.111), calls=%async_computation | async-start | bytes 8388608 | tf_op jit(solution)/shard_map/all_to_all | solution.py:235
  11.2 0.4 collective-permute-start.1
  12.3 0.1 pad_add_fusion.ids
  12.4 0.2 collective-permute-start
  12.6 3.0 %collective-permute-done.other_ids = s32[129]{0:T(256)S(1)} collective-permute-done((s32[129]{0:T(256)S(1)}, s32[129]{0:T(256)S(1)}, u32[]{:S(2)}, u32[]{:S(2)}) %collective-permute-start) | collective-permute-done | bytes 548 | tf_op jit(solution)/shard_map/ppermute | solution.py:191
  15.6 0.2 collective-permute-done.1.other_tiles
  15.7 51.8 %all-to-all-done.gathered = bf16[16,512,256]{2,1,0:T(8,128)(2,1)} async-done(((bf16[16,512,256]{2,1,0:T(8,128)(2,1)}), bf16[16,512,256]{2,1,0:T(8,128)(2,1)}, u32[]{:S(2)}, u32[]{:S(2)}) %all-to-all-start) | async-done | bytes 4194336 | tf_op jit(solution)/shard_map/all_to_all | solution.py:235
  67.6 9.6 %shard_map.112 = bf16[64,128,256]{2,1,0:T(8,128)(2,1)} custom-call(s32[129]{0:T(256)} %copy-done.6, s32[129]{0:T(256)} %copy-done.7, bf16[64,128,128]{2,1,0:T(8,128)(2,1)} %bitcast.43, bf16[64,128,128]{2,1,0:T(8,128)(2,1)} %collective-permute-done.1.other_tiles, bf16[16,512,256]{2,1,0:T(8,128)(2,1)} %all-to-all-done.gathered), custom_call_target="tpu_custom_call" | custom-call | flops 1073741824 | bytes 16777216 | tf_op jit(solution)/shard_map/pallas_call | solution.py:176
  77.2 54.7 %all_to_all.20.parts = bf16[16,512,256]{2,1,0:T(8,128)(2,1)} all-to-all(bf16[16,512,256]{2,1,0:T(8,128)(2,1)} %bitcast.42), channel_id=1, replica_groups={{0,1,2,3,4,5,6,7,8,9,10,11,12,13,14,15},{16,17,18,19,20,21,22,23,24,25,..., dimensions={0} | all-to-all | bytes 8388608 | tf_op jit(solution)/shard_map/all_to_all | solution.py:239
  131.9 7.0 %shard_map.113 = (bf16[512,512]{1,0:T(8,128)(2,1)}, bf16[16,512,256]{2,1,0:T(8,128)(2,1)}, bf16[2,4,2,48,512]{4,3,2,1,0:T(8,128)(2,1)}) custom-call(bf16[16,512,256]{2,1,0:T(8,128)(2,1)} %all_to_all.20.parts, bf16[512,512]{1,0:T(8,128)(2,1)} %weight.1, f32[1,512]{1,0:T(1,128)} %bitcast.54, bf16[512,512]{1,0:T(8,128)(2,1)} %cotangent.1), custom_call_target="tpu_custom_call" | custom-call | flops 805306368 | bytes 8388608 | tf_op jit(solution)/shard_map/pallas_call | solution.py:176
  138.9 4.7 %all-to-all-start.2 = ((bf16[16,512,256]{2,1,0:T(8,128)(2,1)}), bf16[16,512,256]{2,1,0:T(8,128)(2,1)}, u32[]{:S(2)}, u32[]{:S(2)}) async-start(bf16[16,512,256]{2,1,0:T(8,128)(2,1)} %get-tuple-element.15), calls=%async_computation.2 | async-start | bytes 8388608 | tf_op jit(solution)/shard_map/all_to_all | solution.py:239
  143.7 0.4 collective-permute-start.2
  144.0 1.5 collective-permute-done.2
  145.5 0.1 fusion
  145.6 3.0 %collective-permute-start.3 = (bf16[2,48,512]{2,1,0:T(8,128)(2,1)S(1)}, bf16[2,48,512]{2,1,0:T(8,128)(2,1)S(1)}, u32[]{:S(2)}, u32[]{:S(2)}) collective-permute-start(bf16[2,48,512]{2,1,0:T(8,128)(2,1)S(1)} %get-tuple-element.25), channel_id=1, source_target_pairs={{0,16},{8,24},{16,32},{24,40},{32,48},{40,56},{48,0},{56,8},{64,80... | collective-permute-start | bytes 294920 | tf_op jit(solution)/shard_map/ppermute | solution.py:204
  148.6 0.0 collective-permute-start.4
  148.6 2.8 collective-permute-start.5
  151.4 0.5 collective-permute-done.3
  151.9 3.0 %collective-permute-done.4 = bf16[2,48,512]{2,1,0:T(8,128)(2,1)S(1)} collective-permute-done((bf16[2,48,512]{2,1,0:T(8,128)(2,1)S(1)}, bf16[2,48,512]{2,1,0:T(8,128)(2,1)S(1)}, u32[]{:S(2)}, u32[]{:S(2)}) %collective-permute-start.4) | collective-permute-done | bytes 98336 | tf_op jit(solution)/shard_map/ppermute | solution.py:204
  154.8 0.0 collective-permute-done.5
  154.8 0.1 fusion.6
  154.9 1.8 collective-permute-start.6
  156.7 3.4 %collective-permute-start.7 = (bf16[2,48,512]{2,1,0:T(8,128)(2,1)S(1)}, bf16[2,48,512]{2,1,0:T(8,128)(2,1)S(1)}, u32[]{:S(2)}, u32[]{:S(2)}) collective-permute-start(bf16[2,48,512]{2,1,0:T(8,128)(2,1)S(1)} %fusion.6), channel_id=1, source_target_pairs={{0,64},{1,65},{2,66},{3,67},{4,68},{5,69},{6,70},{7,71},{8,72},{9,... | collective-permute-start | bytes 294920 | tf_op jit(solution)/shard_map/ppermute | solution.py:196
  160.1 0.0 collective-permute-start.8
  160.1 36.2 %collective-permute-done.6 = bf16[2,48,512]{2,1,0:T(8,128)(2,1)S(1)} collective-permute-done((bf16[2,48,512]{2,1,0:T(8,128)(2,1)S(1)}, bf16[2,48,512]{2,1,0:T(8,128)(2,1)S(1)}, u32[]{:S(2)}, u32[]{:S(2)}) %collective-permute-start.6) | collective-permute-done | bytes 98336 | tf_op jit(solution)/shard_map/ppermute | solution.py:196
  196.3 2.5 collective-permute-done.7
  198.8 0.0 collective-permute-done.8
  198.8 0.1 add_convert_fusion
  198.8 0.0 all-to-all-done.2.spread
  198.8 3.0 %collective-permute-start.9 = (bf16[2,48,512]{2,1,0:T(8,128)(2,1)S(1)}, bf16[2,48,512]{2,1,0:T(8,128)(2,1)S(1)}, u32[]{:S(2)}, u32[]{:S(2)}) collective-permute-start(bf16[2,48,512]{2,1,0:T(8,128)(2,1)S(1)} %add_convert_fusion), channel_id=1, source_target_pairs={{0,16},{8,24},{16,32},{24,40},{32,48},{40,56},{48,0},{56,8},{64,80... | collective-permute-start | bytes 294920 | tf_op jit(solution)/shard_map/ppermute | solution.py:204
  201.8 0.0 collective-permute-start.10
  201.8 2.8 collective-permute-start.11
  204.6 9.8 %shard_map.114 = bf16[64,128,256]{2,1,0:T(8,128)(2,1)} custom-call(s32[129]{0:T(256)} %copy-done.6, s32[129]{0:T(256)} %copy-done.7, bf16[64,128,128]{2,1,0:T(8,128)(2,1)} %bitcast.44, bf16[64,128,128]{2,1,0:T(8,128)(2,1)} %collective-permute-done.1.other_tiles, bf16[16,512,256]{2,1,0:T(8,128)(2,1)} %all-to-all-done.2.spread), custom_call_target="tpu_custom_call" | custom-call | flops 1073741824 | bytes 16777216 | tf_op jit(solution)/shard_map/pallas_call | solution.py:176
  214.4 0.0 collective-permute-done.9
  214.4 0.0 collective-permute-done.10
  214.4 0.0 collective-permute-done.11
  214.4 0.1 pad_maximum_fusion.1
  214.5 4.6 %all-to-all-start.3 = ((bf16[16,512,256]{2,1,0:T(8,128)(2,1)}), bf16[16,512,256]{2,1,0:T(8,128)(2,1)}, u32[]{:S(2)}, u32[]{:S(2)}) async-start(bf16[16,512,256]{2,1,0:T(8,128)(2,1)} %bitcast.41), calls=%async_computation.3 | async-start | bytes 8388608 | tf_op jit(solution)/shard_map/all_to_all | solution.py:235
  219.1 0.2 collective-permute-start.12
  219.3 1.6 collective-permute-done.12
  220.9 0.1 pad_maximum_fusion
  221.0 0.2 collective-permute-start.13
  221.2 2.9 %collective-permute-start.14 = (bf16[4,48,512]{2,1,0:T(8,128)(2,1)S(1)}, bf16[4,48,512]{2,1,0:T(8,128)(2,1)S(1)}, u32[]{:S(2)}, u32[]{:S(2)}) collective-permute-start(bf16[4,48,512]{2,1,0:T(8,128)(2,1)S(1)} %get-tuple-element.24), channel_id=1, source_target_pairs={{0,4},{1,5},{2,6},{3,7},{4,0},{5,1},{6,2},{7,3},{8,12},{9,13},{10,... | collective-permute-start | bytes 589832 | tf_op jit(solution)/shard_map/ppermute | solution.py:204
  224.1 2.0 collective-permute-start.15
  226.1 7.4 %collective-permute-done.13 = bf16[4,48,512]{2,1,0:T(8,128)(2,1)S(1)} collective-permute-done((bf16[4,48,512]{2,1,0:T(8,128)(2,1)S(1)}, bf16[4,48,512]{2,1,0:T(8,128)(2,1)S(1)}, u32[]{:S(2)}, u32[]{:S(2)}) %collective-permute-start.13) | collective-permute-done | bytes 196640 | tf_op jit(solution)/shard_map/ppermute | solution.py:204
  233.5 0.0 collective-permute-done.14
  233.5 0.6 collective-permute-done.15
  234.1 0.1 fusion.3.own
  234.2 0.0 copy-start.1
  234.2 1.8 collective-permute-start.16
  236.0 2.4 collective-permute-start.17
  238.4 0.9 collective-permute-start.18
  239.3 2.8 %collective-permute-done.16.moved_1 = bf16[4,48,512]{2,1,0:T(8,128)(2,1)S(1)} collective-permute-done((bf16[4,48,512]{2,1,0:T(8,128)(2,1)S(1)}, bf16[4,48,512]{2,1,0:T(8,128)(2,1)S(1)}, u32[]{:S(2)}, u32[]{:S(2)}) %collective-permute-start.16) | collective-permute-done | bytes 196640 | tf_op jit(solution)/shard_map/ppermute | solution.py:204
  242.1 5.4 %collective-permute-done.17.moved_2 = bf16[4,48,512]{2,1,0:T(8,128)(2,1)S(1)} collective-permute-done((bf16[4,48,512]{2,1,0:T(8,128)(2,1)S(1)}, bf16[4,48,512]{2,1,0:T(8,128)(2,1)S(1)}, u32[]{:S(2)}, u32[]{:S(2)}) %collective-permute-start.17) | collective-permute-done | bytes 196640 | tf_op jit(solution)/shard_map/ppermute | solution.py:204
  247.5 0.0 collective-permute-done.18.moved_3
  247.5 0.7 copy-done.4
  248.2 0.7 copy-done.5
  248.9 2.5 shard_map.116
  251.4 23.9 %all-to-all-done.3.parts = bf16[16,512,256]{2,1,0:T(8,128)(2,1)} async-done(((bf16[16,512,256]{2,1,0:T(8,128)(2,1)}), bf16[16,512,256]{2,1,0:T(8,128)(2,1)}, u32[]{:S(2)}, u32[]{:S(2)}) %all-to-all-start.3) | async-done | bytes 4194336 | tf_op jit(solution)/shard_map/all_to_all | solution.py:235
  275.3 3.5 %shard_map.115 = bf16[512,512]{1,0:T(8,128)(2,1)} custom-call(bf16[16,512,256]{2,1,0:T(8,128)(2,1)} %all-to-all-done.3.parts), custom_call_target="tpu_custom_call" | custom-call | bytes 4194304 | tf_op jit(solution)/shard_map/pallas_call | solution.py:176
  (17 shorter events, 0.1 us)
Async XLA Ops:
  3.8 7.4 %copy-start = (bf16[1,1,64,128,128]{4,3,2,1,0:T(8,128)(2,1)S(1)}, bf16[1,1,64,128,128]{4,3,2,1,0:T(8,128)(2,1)}, u32[]{:S(2)}) copy-start(bf16[1,1,64,128,128]{4,3,2,1,0:T(8,128)(2,1)} %param.12) | copy-start | bytes 6291460
  3.9 8.4 %copy-start.8 = (s32[1,1,64]{2,1,0:T(1,128)S(1)}, s32[1,1,64]{2,1,0:T(1,128)}, u32[]{:S(2)}) copy-start(s32[1,1,64]{2,1,0:T(1,128)} %param.13) | copy-start | bytes 772
  3.9 8.4 %copy-start.9 = (s32[1,1,64]{2,1,0:T(1,128)S(1)}, s32[1,1,64]{2,1,0:T(1,128)}, u32[]{:S(2)}) copy-start(s32[1,1,64]{2,1,0:T(1,128)} %param.14) | copy-start | bytes 772
  3.9 63.7 %all-to-all-start = ((bf16[16,512,256]{2,1,0:T(8,128)(2,1)}), bf16[16,512,256]{2,1,0:T(8,128)(2,1)}, u32[]{:S(2)}, u32[]{:S(2)}) async-start(bf16[16,512,256]{2,1,0:T(8,128)(2,1)} %shard_map.111), calls=%async_computation | async-start | bytes 8388608 | tf_op jit(solution)/shard_map/all_to_all | solution.py:235
  11.2 4.5 %collective-permute-start.1 = (bf16[64,128,128]{2,1,0:T(8,128)(2,1)S(1)}, bf16[64,128,128]{2,1,0:T(8,128)(2,1)}, u32[]{:S(2)}, u32[]{:S(2)}) collective-permute-start(bf16[64,128,128]{2,1,0:T(8,128)(2,1)S(1)} %bitcast.45), channel_id=1, source_target_pairs={{0,8},{8,0},{16,24},{24,16},{32,40},{40,32},{48,56},{56,48},{64,72... | collective-permute-start | bytes 6291464 | tf_op jit(solution)/shard_map/ppermute | solution.py:191
  12.4 55.2 %copy-start.6 = (s32[129]{0:T(256)}, s32[129]{0:T(256)S(1)}, u32[]{:S(2)}) copy-start(s32[129]{0:T(256)S(1)} %pad_add_fusion.ids) | copy-start | bytes 1552
  12.4 3.2 %collective-permute-start = (s32[129]{0:T(256)S(1)}, s32[129]{0:T(256)S(1)}, u32[]{:S(2)}, u32[]{:S(2)}) collective-permute-start(s32[129]{0:T(256)S(1)} %pad_add_fusion.ids), channel_id=1, source_target_pairs={{0,8},{8,0},{16,24},{24,16},{32,40},{40,32},{48,56},{56,48},{64,72... | collective-permute-start | bytes 1556 | tf_op jit(solution)/shard_map/ppermute | solution.py:191
  15.6 52.0 %copy-start.7 = (s32[129]{0:T(256)}, s32[129]{0:T(256)S(1)}, u32[]{:S(2)}) copy-start(s32[129]{0:T(256)S(1)} %collective-permute-done.other_ids) | copy-start | bytes 1552
  138.9 4.7 %copy-start.2 = (bf16[2,4,2,48,512]{4,3,2,1,0:T(8,128)(2,1)S(1)}, bf16[2,4,2,48,512]{4,3,2,1,0:T(8,128)(2,1)}, u32[]{:S(2)}) copy-start(bf16[2,4,2,48,512]{4,3,2,1,0:T(8,128)(2,1)} %get-tuple-element.14) | copy-start | bytes 2359300
  138.9 59.9 %all-to-all-start.2 = ((bf16[16,512,256]{2,1,0:T(8,128)(2,1)}), bf16[16,512,256]{2,1,0:T(8,128)(2,1)}, u32[]{:S(2)}, u32[]{:S(2)}) async-start(bf16[16,512,256]{2,1,0:T(8,128)(2,1)} %get-tuple-element.15), calls=%async_computation.2 | async-start | bytes 8388608 | tf_op jit(solution)/shard_map/all_to_all | solution.py:239
  143.7 1.8 collective-permute-start.2
  145.6 6.2 %collective-permute-start.3 = (bf16[2,48,512]{2,1,0:T(8,128)(2,1)S(1)}, bf16[2,48,512]{2,1,0:T(8,128)(2,1)S(1)}, u32[]{:S(2)}, u32[]{:S(2)}) collective-permute-start(bf16[2,48,512]{2,1,0:T(8,128)(2,1)S(1)} %get-tuple-element.25), channel_id=1, source_target_pairs={{0,16},{8,24},{16,32},{24,40},{32,48},{40,56},{48,0},{56,8},{64,80... | collective-permute-start | bytes 294920 | tf_op jit(solution)/shard_map/ppermute | solution.py:204
  148.6 6.2 %collective-permute-start.4 = (bf16[2,48,512]{2,1,0:T(8,128)(2,1)S(1)}, bf16[2,48,512]{2,1,0:T(8,128)(2,1)S(1)}, u32[]{:S(2)}, u32[]{:S(2)}) collective-permute-start(bf16[2,48,512]{2,1,0:T(8,128)(2,1)S(1)} %get-tuple-element.27), channel_id=1, source_target_pairs={{0,32},{8,40},{16,48},{24,56},{32,0},{40,8},{48,16},{56,24},{64,96... | collective-permute-start | bytes 294920 | tf_op jit(solution)/shard_map/ppermute | solution.py:204
  148.6 6.2 %collective-permute-start.5 = (bf16[2,48,512]{2,1,0:T(8,128)(2,1)S(1)}, bf16[2,48,512]{2,1,0:T(8,128)(2,1)S(1)}, u32[]{:S(2)}, u32[]{:S(2)}) collective-permute-start(bf16[2,48,512]{2,1,0:T(8,128)(2,1)S(1)} %get-tuple-element.26), channel_id=1, source_target_pairs={{0,48},{8,56},{16,0},{24,8},{32,16},{40,24},{48,32},{56,40},{64,11... | collective-permute-start | bytes 294920 | tf_op jit(solution)/shard_map/ppermute | solution.py:204
  154.9 41.4 %collective-permute-start.6 = (bf16[2,48,512]{2,1,0:T(8,128)(2,1)S(1)}, bf16[2,48,512]{2,1,0:T(8,128)(2,1)S(1)}, u32[]{:S(2)}, u32[]{:S(2)}) collective-permute-start(bf16[2,48,512]{2,1,0:T(8,128)(2,1)S(1)} %fusion.6), channel_id=1, source_target_pairs={{0,1},{1,0},{2,3},{3,2},{4,5},{5,4},{6,7},{7,6},{8,9},{9,8},{10,11... | collective-permute-start | bytes 294920 | tf_op jit(solution)/shard_map/ppermute | solution.py:196
  156.7 42.1 %collective-permute-start.7 = (bf16[2,48,512]{2,1,0:T(8,128)(2,1)S(1)}, bf16[2,48,512]{2,1,0:T(8,128)(2,1)S(1)}, u32[]{:S(2)}, u32[]{:S(2)}) collective-permute-start(bf16[2,48,512]{2,1,0:T(8,128)(2,1)S(1)} %fusion.6), channel_id=1, source_target_pairs={{0,64},{1,65},{2,66},{3,67},{4,68},{5,69},{6,70},{7,71},{8,72},{9,... | collective-permute-start | bytes 294920 | tf_op jit(solution)/shard_map/ppermute | solution.py:196
  160.1 38.7 %collective-permute-start.8 = (bf16[2,48,512]{2,1,0:T(8,128)(2,1)S(1)}, bf16[2,48,512]{2,1,0:T(8,128)(2,1)S(1)}, u32[]{:S(2)}, u32[]{:S(2)}) collective-permute-start(bf16[2,48,512]{2,1,0:T(8,128)(2,1)S(1)} %fusion.6), channel_id=1, source_target_pairs={{0,65},{1,64},{2,67},{3,66},{4,69},{5,68},{6,71},{7,70},{8,73},{9,... | collective-permute-start | bytes 294920 | tf_op jit(solution)/shard_map/ppermute | solution.py:196
  198.8 15.6 %collective-permute-start.9 = (bf16[2,48,512]{2,1,0:T(8,128)(2,1)S(1)}, bf16[2,48,512]{2,1,0:T(8,128)(2,1)S(1)}, u32[]{:S(2)}, u32[]{:S(2)}) collective-permute-start(bf16[2,48,512]{2,1,0:T(8,128)(2,1)S(1)} %add_convert_fusion), channel_id=1, source_target_pairs={{0,16},{8,24},{16,32},{24,40},{32,48},{40,56},{48,0},{56,8},{64,80... | collective-permute-start | bytes 294920 | tf_op jit(solution)/shard_map/ppermute | solution.py:204
  201.8 12.6 %collective-permute-start.10 = (bf16[2,48,512]{2,1,0:T(8,128)(2,1)S(1)}, bf16[2,48,512]{2,1,0:T(8,128)(2,1)S(1)}, u32[]{:S(2)}, u32[]{:S(2)}) collective-permute-start(bf16[2,48,512]{2,1,0:T(8,128)(2,1)S(1)} %add_convert_fusion), channel_id=1, source_target_pairs={{0,32},{8,40},{16,48},{24,56},{32,0},{40,8},{48,16},{56,24},{64,96... | collective-permute-start | bytes 294920 | tf_op jit(solution)/shard_map/ppermute | solution.py:204
  201.8 12.6 %collective-permute-start.11 = (bf16[2,48,512]{2,1,0:T(8,128)(2,1)S(1)}, bf16[2,48,512]{2,1,0:T(8,128)(2,1)S(1)}, u32[]{:S(2)}, u32[]{:S(2)}) collective-permute-start(bf16[2,48,512]{2,1,0:T(8,128)(2,1)S(1)} %add_convert_fusion), channel_id=1, source_target_pairs={{0,48},{8,56},{16,0},{24,8},{32,16},{40,24},{48,32},{56,40},{64,11... | collective-permute-start | bytes 294920 | tf_op jit(solution)/shard_map/ppermute | solution.py:204
  214.5 60.8 %all-to-all-start.3 = ((bf16[16,512,256]{2,1,0:T(8,128)(2,1)}), bf16[16,512,256]{2,1,0:T(8,128)(2,1)}, u32[]{:S(2)}, u32[]{:S(2)}) async-start(bf16[16,512,256]{2,1,0:T(8,128)(2,1)} %bitcast.41), calls=%async_computation.3 | async-start | bytes 8388608 | tf_op jit(solution)/shard_map/all_to_all | solution.py:235
  219.1 1.8 collective-permute-start.12
  221.0 12.5 %collective-permute-start.13 = (bf16[4,48,512]{2,1,0:T(8,128)(2,1)S(1)}, bf16[4,48,512]{2,1,0:T(8,128)(2,1)S(1)}, u32[]{:S(2)}, u32[]{:S(2)}) collective-permute-start(bf16[4,48,512]{2,1,0:T(8,128)(2,1)S(1)} %get-tuple-element.22), channel_id=1, source_target_pairs={{0,2},{1,3},{2,4},{3,5},{4,6},{5,7},{6,0},{7,1},{8,10},{9,11},{10,... | collective-permute-start | bytes 589832 | tf_op jit(solution)/shard_map/ppermute | solution.py:204
  221.2 12.3 %collective-permute-start.14 = (bf16[4,48,512]{2,1,0:T(8,128)(2,1)S(1)}, bf16[4,48,512]{2,1,0:T(8,128)(2,1)S(1)}, u32[]{:S(2)}, u32[]{:S(2)}) collective-permute-start(bf16[4,48,512]{2,1,0:T(8,128)(2,1)S(1)} %get-tuple-element.24), channel_id=1, source_target_pairs={{0,4},{1,5},{2,6},{3,7},{4,0},{5,1},{6,2},{7,3},{8,12},{9,13},{10,... | collective-permute-start | bytes 589832 | tf_op jit(solution)/shard_map/ppermute | solution.py:204
  224.1 10.1 %collective-permute-start.15 = (bf16[4,48,512]{2,1,0:T(8,128)(2,1)S(1)}, bf16[4,48,512]{2,1,0:T(8,128)(2,1)S(1)}, u32[]{:S(2)}, u32[]{:S(2)}) collective-permute-start(bf16[4,48,512]{2,1,0:T(8,128)(2,1)S(1)} %get-tuple-element.23), channel_id=1, source_target_pairs={{0,6},{1,7},{2,0},{3,1},{4,2},{5,3},{6,4},{7,5},{8,14},{9,15},{10,... | collective-permute-start | bytes 589832 | tf_op jit(solution)/shard_map/ppermute | solution.py:204
  234.2 13.3 %copy-start.1 = (bf16[4,48,512]{2,1,0:T(8,128)(2,1)}, bf16[4,48,512]{2,1,0:T(8,128)(2,1)S(1)}, u32[]{:S(2)}) copy-start(bf16[4,48,512]{2,1,0:T(8,128)(2,1)S(1)} %fusion.3.own) | copy-start | bytes 589828
  234.2 7.9 %collective-permute-start.16 = (bf16[4,48,512]{2,1,0:T(8,128)(2,1)S(1)}, bf16[4,48,512]{2,1,0:T(8,128)(2,1)S(1)}, u32[]{:S(2)}, u32[]{:S(2)}) collective-permute-start(bf16[4,48,512]{2,1,0:T(8,128)(2,1)S(1)} %fusion.3.own), channel_id=1, source_target_pairs={{0,2},{1,3},{2,4},{3,5},{4,6},{5,7},{6,0},{7,1},{8,10},{9,11},{10,... | collective-permute-start | bytes 589832 | tf_op jit(solution)/shard_map/ppermute | solution.py:204
  236.0 11.5 %collective-permute-start.17 = (bf16[4,48,512]{2,1,0:T(8,128)(2,1)S(1)}, bf16[4,48,512]{2,1,0:T(8,128)(2,1)S(1)}, u32[]{:S(2)}, u32[]{:S(2)}) collective-permute-start(bf16[4,48,512]{2,1,0:T(8,128)(2,1)S(1)} %fusion.3.own), channel_id=1, source_target_pairs={{0,4},{1,5},{2,6},{3,7},{4,0},{5,1},{6,2},{7,3},{8,12},{9,13},{10,... | collective-permute-start | bytes 589832 | tf_op jit(solution)/shard_map/ppermute | solution.py:204
  238.4 9.1 %collective-permute-start.18 = (bf16[4,48,512]{2,1,0:T(8,128)(2,1)S(1)}, bf16[4,48,512]{2,1,0:T(8,128)(2,1)S(1)}, u32[]{:S(2)}, u32[]{:S(2)}) collective-permute-start(bf16[4,48,512]{2,1,0:T(8,128)(2,1)S(1)} %fusion.3.own), channel_id=1, source_target_pairs={{0,6},{1,7},{2,0},{3,1},{4,2},{5,3},{6,4},{7,5},{8,14},{9,15},{10,... | collective-permute-start | bytes 589832 | tf_op jit(solution)/shard_map/ppermute | solution.py:204
  242.1 5.4 %copy-start.3 = (bf16[4,48,512]{2,1,0:T(8,128)(2,1)}, bf16[4,48,512]{2,1,0:T(8,128)(2,1)S(1)}, u32[]{:S(2)}) copy-start(bf16[4,48,512]{2,1,0:T(8,128)(2,1)S(1)} %collective-permute-done.16.moved_1) | copy-start | bytes 589828
  247.5 0.7 copy-start.4
  248.2 0.7 copy-start.5

commit v3 on v2

--- a/solution.py
+++ b/solution.py
@@ -10,9 +10,10 @@
 
 BF = jnp.bfloat16
 F32 = jnp.float32
-VMEM_LIMIT = 56 * 2**20
+VMEM_LIMIT = 26 * 2**20
 UNROLL = 16
 HALF = 256
+FIRST = 256
 SHARE = 32
 TAIL = 16
 LINES = [[(chip * 2 + core) * 8 + q for core in range(2) for q in range(8)] for chip in range(8)]
@@ -49,19 +50,25 @@
         copy.wait()
 
 
-def copies_kernel(features, out, sems):
-    copies = [
-        pltpu.make_async_copy(features.at[:, pl.ds(j % 2 * HALF, HALF)], out.at[j], sems.at[j]) for j in range(16)
-    ]
-    for copy in copies:
-        copy.start()
-    for copy in copies:
-        copy.wait()
-
-
-def forward_kernel(ids, other_ids, tiles, other_tiles, gathered, out, source, vals, acc, sems):
-    core = lax.axis_index("row") % 2
-    start_loads([(tiles, vals.at[0]), (other_tiles, vals.at[1]), (gathered, source)], acc, sems)
+def halves_kernel(features, mine, other):
+    left = lax.axis_index("row") % 2 == 0
+    first, second = features[:, :HALF], features[:, HALF:]
+    mine[...] = jnp.where(left, first, second)
+    other[...] = jnp.where(left, second, first)
+
+
+def route_loads(pieces, source):
+    own, ring_1, ring_2, ring_3, near, far = pieces
+    low, high = pl.ds(0, FIRST), pl.ds(FIRST, 512 - FIRST)
+    loads = [(piece, source.at[d, :, :, low]) for d, piece in enumerate((own, ring_1, ring_2, ring_3))]
+    return loads + [(near, source.at[:, 0, :, high]), (far, source.at[:, 1, :, high])]
+
+
+def forward_kernel(ids, other_ids, tiles, other_tiles, *refs):
+    *pieces, out, source, vals, acc, sems = refs
+    me = lax.axis_index("row")
+    core, my_x, my_y = lax.rem(me, 2), lax.rem(me // 2, 4), me // 8
+    start_loads([(tiles, vals.at[0]), (other_tiles, vals.at[1]), *route_loads(pieces, source)], acc, sems)
     for side, table in enumerate((ids, other_ids)):
         group = core if side == 0 else 1 - core
 
@@ -69,7 +76,10 @@
         def _(k, live, side=side, table=table, group=group):
             col, row = table[k], table[64 + k]
             start = pl.multiple_of(lax.rem(col, 4) * 128, 128)
-            picked = source[col // 32, pl.ds(start, 128), :]
+            owner = col // 32
+            behind = lax.rem(my_x + 4 - lax.rem(owner // 2, 4), 4)
+            y, far_core = lax.rem(owner // 8 + my_y, 2), lax.rem(owner + core, 2)
+            picked = source[behind, y, far_core, pl.ds(start, 128), :]
             target = jnp.where(live, group * 32 + lax.rem(row, 32), 64)
             return target, jnp.dot(vals[side, k], picked, preferred_element_type=F32)
 
@@ -221,6 +231,16 @@
     return (part, *(shift(part, axis, d) for d in range(1, 4)))
 
 
+def two_way_gather(mine, other, axis):
+    pair = jnp.stack([mine, other])
+    high, low = (1, 0) if axis == "row" else (0, 1)
+    first, rest = pair[:, :FIRST], pair[:, FIRST:]
+    near = jnp.stack(ring(rest, axis))
+    first = jnp.stack([first, swap_y(first, high, low)])
+    first, near = lax.optimization_barrier((first, near))
+    return (*ring(first, axis), near, swap_y(near, high, low))
+
+
 def z_sum(chunks):
     z = lax.axis_index("col") // 2
     parts = chunks.reshape(4, 4, *chunks.shape[-2:])
@@ -245,25 +265,23 @@
     other_tiles, other_ids = core_swap(tiles), core_swap(ids)
     scale = 1.0 / math.sqrt(65536)
     tables = (ids, other_ids)
-    scratch = [
-        pltpu.VMEM((16, 512, HALF), BF),
-        pltpu.VMEM((2, 64, 128, 128), BF),
-        pltpu.VMEM((65, 128, HALF), F32),
-        pltpu.SemaphoreType.DMA((3,)),
-    ]
-    work = dict(
-        ids=tables, in_specs=[any_spec()] * 3, scratch=scratch, flops=2 * 64 * 128 * 128 * 512, moved=16 * 2**20
-    )
-
-    (copies,) = call(
-        copies_kernel,
-        (features,),
-        [((16, 512, HALF), BF)],
-        out_specs=[any_spec()],
-        scratch=[pltpu.SemaphoreType.DMA((16,))],
-    )
-    gathered = row_exchange(copies)
-    (partial,) = call(forward_kernel, (tiles, other_tiles, gathered), [((64, 128, HALF), BF)], **work)
+    def work(source, loads):
+        return dict(
+            ids=tables,
+            in_specs=[any_spec()] * loads,
+            scratch=[
+                pltpu.VMEM(source, BF),
+                pltpu.VMEM((2, 64, 128, 128), BF),
+                pltpu.VMEM((65, 128, HALF), F32),
+                pltpu.SemaphoreType.DMA((loads,)),
+            ],
+            flops=2 * 64 * 128 * 128 * 512,
+            moved=16 * 2**20,
+        )
+
+    mine, other = call(halves_kernel, (features,), [((512, HALF), BF)] * 2)
+    pieces = two_way_gather(mine, core_swap(other), "row")
+    (partial,) = call(forward_kernel, (tiles, other_tiles, *pieces), [((64, 128, HALF), BF)], **work((4, 2, 2, 512, HALF), 8))
     parts = line_exchange(partial.reshape(16, 512, HALF))
     output, spread, chunks = call(
         functools.partial(dense_kernel, scale),
@@ -275,7 +293,7 @@
     )
     spread = line_exchange(spread)
     chunks, spread = lax.optimization_barrier((plane_sum(chunks), spread))
-    (back,) = call(backward_kernel, (tiles, other_tiles, spread), [((64, 128, HALF), BF)], **work)
+    (back,) = call(backward_kernel, (tiles, other_tiles, spread), [((64, 128, HALF), BF)], **work((16, 512, HALF), 3))
     chunks, back = lax.optimization_barrier((jnp.stack(ring(chunks, "row")), back))
     back = row_exchange(back.reshape(16, 512, HALF))
     chunks = jnp.stack([chunks, core_swap(chunks)])

time: 281 us -> 261 us (0.929)
  waiting for transfers between devices: 140 us -> 122 us
  Pallas kernels: 35.6 us -> 19.6 us
  starting transfers between devices: 44.7 us -> 51.8 us
  local copies, waits for them, and re-layouts: 1.5 us -> 6.93 us
    all_to_all x2 -> x1, waiting for transfers between devices: 75.7 us -> 26.4 us  [row_exchange(): return lax.all_to_all(value, 'row', 0, 0, tiled=True)]
    ppermute x12 -> x18, waiting for transfers between devices: 19.7 us -> 48.9 us  [shift(): return lax.ppermute(value, axis, to)]
    pallas_call x6, Pallas kernels: 35.6 us -> 19.6 us  [call(): pl.pallas_call(kernel, grid_spec=pltpu.PrefetchScalarGridSpec(num_scalar_...]
    ppermute x12 -> x18, starting transfers between devices: 21.7 us -> 32.5 us  [shift(): return lax.ppermute(value, axis, to)]
    all_to_all x2 -> x1, starting transfers between devices: 11.9 us -> 4.56 us  [row_exchange(): return lax.all_to_all(value, 'row', 0, 0, tiled=True)]
    unnamed x20 -> x22, local copies, waits for them, and re-layouts: 1.41 us -> 6.83 us
    ppermute x3 -> x5, starting transfers between devices: 5.2 us -> 9.07 us  [swap_y(): return lax.ppermute(value, ('row', 'col'), to)]
    ppermute x3 -> x5, waiting for transfers between devices: 38.7 us -> 40.5 us  [swap_y(): return lax.ppermute(value, ('row', 'col'), to)]
  transfers between devices with their start and end apart: 22 -> 30, of which waited for: 14 -> 17; matrix products, arithmetic and copies ran while one was open for 0% -> 0% of each run, Pallas kernels for 4% -> 3%
where the time goes in v3:
time: 261 us; the launch traced here: 258 us
  waiting for transfers between devices  122 us (47%)
  blocking collectives  55.9 us (21%)
  starting transfers between devices  51.8 us (20%)
  Pallas kernels  19.6 us (8%)
  local copies, waits for them, and re-layouts  6.93 us (3%)
    all_to_all x1, blocking collectives, line_exchange(): lax.all_to_all(value, ('row', 'col'), 0, 0, tiled=True, axis_index_groups...  55.9 us
    ppermute x18, waiting for transfers between devices, shift(): return lax.ppermute(value, axis, to)  48.9 us
    ppermute x5, waiting for transfers between devices, swap_y(): return lax.ppermute(value, ('row', 'col'), to)  40.5 us
    ppermute x18, starting transfers between devices, shift(): return lax.ppermute(value, axis, to)  32.5 us
    all_to_all x1, waiting for transfers between devices, row_exchange(): return lax.all_to_all(value, 'row', 0, 0, tiled=True)  26.4 us
    pallas_call x6, Pallas kernels, call(): pl.pallas_call(kernel, grid_spec=pltpu.PrefetchScalarGridSpec(num_scalar_...  19.6 us
    ppermute x5, starting transfers between devices, swap_y(): return lax.ppermute(value, ('row', 'col'), to)  9.07 us
    unnamed x22, local copies, waits for them, and re-layouts  6.83 us
  transfers between devices with their start and end apart: 30, of which 17 were waited for; matrix products, arithmetic and copies ran while one was open for 0% of the time, Pallas kernels for 3%

profile of v3, /device:TPU:0, one launch (start us, length us, event | category | flops | bytes accessed | tf_op | source)
XLA Modules:
  0.0 258.3 jit_solution(6947539398591246314)
XLA Ops:
  0.6 0.1 collective-permute-start.1
  0.7 1.2 copy-done.7
  1.9 0.1 shard_map.111
  2.0 0.4 collective-permute-start.2
  2.4 2.8 %collective-permute-done.2 = bf16[512,256]{1,0:T(8,128)(2,1)S(1)} collective-permute-done((bf16[512,256]{1,0:T(8,128)(2,1)S(1)}, bf16[512,256]{1,0:T(8,128)(2,1)S(1)}, u32[]{:S(2)}, u32[]{:S(2)}) %collective-permute-start.2) | collective-permute-done | bytes 262176 | tf_op jit(solution)/shard_map/ppermute | solution.py:201
  5.3 3.4 %collective-permute-start.3 = (bf16[2,256,256]{2,1,0:T(8,128)(2,1)S(1)}, bf16[2,256,256]{2,1,0:T(8,128)(2,1)S(1)}, u32[]{:S(2)}, u32[]{:S(2)}) collective-permute-start(bf16[2,256,256]{2,1,0:T(8,128)(2,1)S(1)} %get-tuple-element.34), channel_id=1, source_target_pairs={{0,64},{1,65},{2,66},{3,67},{4,68},{5,69},{6,70},{7,71},{8,72},{9,... | collective-permute-start | bytes 786440 | tf_op jit(solution)/shard_map/ppermute | solution.py:206
  8.7 3.0 %collective-permute-start.5 = (bf16[2,256,256]{2,1,0:T(8,128)(2,1)S(1)}, bf16[2,256,256]{2,1,0:T(8,128)(2,1)S(1)}, u32[]{:S(2)}, u32[]{:S(2)}) collective-permute-start(bf16[2,256,256]{2,1,0:T(8,128)(2,1)S(1)} %get-tuple-element.33), channel_id=1, source_target_pairs={{0,32},{8,40},{16,48},{24,56},{32,0},{40,8},{48,16},{56,24},{64,96... | collective-permute-start | bytes 786440 | tf_op jit(solution)/shard_map/ppermute | solution.py:214
  11.7 1.1 collective-permute-start.6
  12.8 0.9 collective-permute-start.4
  13.7 1.6 collective-permute-done.3
  15.3 4.0 %collective-permute-done.5 = bf16[2,256,256]{2,1,0:T(8,128)(2,1)S(1)} collective-permute-done((bf16[2,256,256]{2,1,0:T(8,128)(2,1)S(1)}, bf16[2,256,256]{2,1,0:T(8,128)(2,1)S(1)}, u32[]{:S(2)}, u32[]{:S(2)}) %collective-permute-start.5) | collective-permute-done | bytes 262176 | tf_op jit(solution)/shard_map/ppermute | solution.py:214
  19.4 4.6 %collective-permute-done.6 = bf16[2,256,256]{2,1,0:T(8,128)(2,1)S(1)} collective-permute-done((bf16[2,256,256]{2,1,0:T(8,128)(2,1)S(1)}, bf16[2,256,256]{2,1,0:T(8,128)(2,1)S(1)}, u32[]{:S(2)}, u32[]{:S(2)}) %collective-permute-start.6) | collective-permute-done | bytes 262176 | tf_op jit(solution)/shard_map/ppermute | solution.py:214
  24.0 0.1 pad_maximum_fusion.refs_4_
  24.1 0.5 collective-permute-start.10
  25.2 0.1 pad_add_fusion.ids
  25.4 1.5 collective-permute-start.7
  26.9 2.7 %collective-permute-start.8 = (bf16[2,2,256,256]{3,2,1,0:T(8,128)(2,1)S(1)}, bf16[2,2,256,256]{3,2,1,0:T(8,128)(2,1)S(1)}, u32[]{:S(2)}, u32[]{:S(2)}) collective-permute-start(bf16[2,2,256,256]{3,2,1,0:T(8,128)(2,1)S(1)} %pad_maximum_fusion.2.refs_0_), channel_id=1, source_target_pairs={{0,32},{8,40},{16,48},{24,56},{32,0},{40,8},{48,16},{56,24},{64,96... | collective-permute-start | bytes 1572872 | tf_op jit(solution)/shard_map/ppermute | solution.py:214
  29.5 1.4 collective-permute-start.9
  31.0 10.0 %collective-permute-done.7.refs_1_ = bf16[2,2,256,256]{3,2,1,0:T(8,128)(2,1)S(1)} collective-permute-done((bf16[2,2,256,256]{3,2,1,0:T(8,128)(2,1)S(1)}, bf16[2,2,256,256]{3,2,1,0:T(8,128)(2,1)S(1)}, u32[]{:S(2)}, u32[]{:S(2)}) %collective-permute-start.7) | collective-permute-done | bytes 524320 | tf_op jit(solution)/shard_map/ppermute | solution.py:214
  40.9 12.1 %collective-permute-done.8.refs_2_ = bf16[2,2,256,256]{3,2,1,0:T(8,128)(2,1)S(1)} collective-permute-done((bf16[2,2,256,256]{3,2,1,0:T(8,128)(2,1)S(1)}, bf16[2,2,256,256]{3,2,1,0:T(8,128)(2,1)S(1)}, u32[]{:S(2)}, u32[]{:S(2)}) %collective-permute-start.8) | collective-permute-done | bytes 524320 | tf_op jit(solution)/shard_map/ppermute | solution.py:214
  53.0 5.5 %shard_map.112 = bf16[64,128,256]{2,1,0:T(8,128)(2,1)S(1)} custom-call(s32[129]{0:T(256)S(1)} %pad_add_fusion.ids, s32[129]{0:T(256)S(1)} %collective-permute-done.other_ids, bf16[64,128,128]{2,1,0:T(8,128)(2,1)S(1)} %bitcast.52, bf16[64,128,128]{2,1,0:T(8,128)(2,1)S(1)} %collective-permute-done.1.other_tiles, ...), custom_call_target="tpu_custom_call" | custom-call | flops 1073741824 | bytes 16777216 | tf_op jit(solution)/shard_map/pallas_call | solution.py:186
  58.6 55.9 %all_to_all.15.parts = bf16[16,512,256]{2,1,0:T(8,128)(2,1)S(1)} all-to-all(bf16[16,512,256]{2,1,0:T(8,128)(2,1)S(1)} %bitcast.50), channel_id=1, replica_groups={{0,1,2,3,4,5,6,7,8,9,10,11,12,13,14,15},{16,17,18,19,20,21,22,23,24,25,..., dimensions={0} | all-to-all | bytes 8388608 | tf_op jit(solution)/shard_map/all_to_all | solution.py:259
  114.5 3.1 %shard_map.113 = (bf16[512,512]{1,0:T(8,128)(2,1)}, bf16[16,512,256]{2,1,0:T(8,128)(2,1)S(1)}, bf16[2,4,2,48,512]{4,3,2,1,0:T(8,128)(2,1)S(1)}) custom-call(bf16[16,512,256]{2,1,0:T(8,128)(2,1)S(1)} %all_to_all.15.parts, bf16[512,512]{1,0:T(8,128)(2,1)S(1)} %copy-done.5, f32[1,512]{1,0:T(1,128)S(1)} %bitcast.55, bf16[512,512]{1,0:T(8,128)(2,1)S(1)} %copy-done.6), custom_call_target="tpu_custom_call" | custom-call | flops 805306368 | bytes 8388608 | tf_op jit(solution)/shard_map/pallas_call | solution.py:186
  117.6 2.0 copy-done.4
  119.6 4.5 %all-to-all-start.1 = ((bf16[16,512,256]{2,1,0:T(8,128)(2,1)}), bf16[16,512,256]{2,1,0:T(8,128)(2,1)}, u32[]{:S(2)}, u32[]{:S(2)}) async-start(bf16[16,512,256]{2,1,0:T(8,128)(2,1)} %copy-done.4), calls=%async_computation.1 | async-start | bytes 8388608 | tf_op jit(solution)/shard_map/all_to_all | solution.py:259
  124.2 0.4 collective-permute-start.11
  124.5 1.5 collective-permute-done.11
  126.0 0.1 fusion
  126.1 1.0 collective-permute-start.12
  127.1 2.9 %collective-permute-start.13 = (bf16[2,48,512]{2,1,0:T(8,128)(2,1)S(1)}, bf16[2,48,512]{2,1,0:T(8,128)(2,1)S(1)}, u32[]{:S(2)}, u32[]{:S(2)}) collective-permute-start(bf16[2,48,512]{2,1,0:T(8,128)(2,1)S(1)} %get-tuple-element.37), channel_id=1, source_target_pairs={{0,32},{8,40},{16,48},{24,56},{32,0},{40,8},{48,16},{56,24},{64,96... | collective-permute-start | bytes 294920 | tf_op jit(solution)/shard_map/ppermute | solution.py:214
  130.1 2.0 collective-permute-start.14
  132.1 0.3 collective-permute-done.12
  132.4 2.7 %collective-permute-done.13 = bf16[2,48,512]{2,1,0:T(8,128)(2,1)S(1)} collective-permute-done((bf16[2,48,512]{2,1,0:T(8,128)(2,1)S(1)}, bf16[2,48,512]{2,1,0:T(8,128)(2,1)S(1)}, u32[]{:S(2)}, u32[]{:S(2)}) %collective-permute-start.13) | collective-permute-done | bytes 98336 | tf_op jit(solution)/shard_map/ppermute | solution.py:214
  135.1 0.1 fusion.7
  135.2 1.8 collective-permute-start.15
  137.0 3.5 %collective-permute-start.16 = (bf16[2,48,512]{2,1,0:T(8,128)(2,1)S(1)}, bf16[2,48,512]{2,1,0:T(8,128)(2,1)S(1)}, u32[]{:S(2)}, u32[]{:S(2)}) collective-permute-start(bf16[2,48,512]{2,1,0:T(8,128)(2,1)S(1)} %fusion.7), channel_id=1, source_target_pairs={{0,64},{1,65},{2,66},{3,67},{4,68},{5,69},{6,70},{7,71},{8,72},{9,... | collective-permute-start | bytes 294920 | tf_op jit(solution)/shard_map/ppermute | solution.py:206
  140.4 36.4 %collective-permute-done.15 = bf16[2,48,512]{2,1,0:T(8,128)(2,1)S(1)} collective-permute-done((bf16[2,48,512]{2,1,0:T(8,128)(2,1)S(1)}, bf16[2,48,512]{2,1,0:T(8,128)(2,1)S(1)}, u32[]{:S(2)}, u32[]{:S(2)}) %collective-permute-start.15) | collective-permute-done | bytes 98336 | tf_op jit(solution)/shard_map/ppermute | solution.py:206
  176.8 2.5 collective-permute-done.16
  179.4 0.1 add_convert_fusion
  179.5 0.9 collective-permute-start.18
  180.4 2.4 collective-permute-start.19
  182.8 1.4 collective-permute-start.20
  184.2 1.6 copy-done.3
  185.8 6.1 %shard_map.114 = bf16[64,128,256]{2,1,0:T(8,128)(2,1)S(1)} custom-call(s32[129]{0:T(256)S(1)} %pad_add_fusion.ids, s32[129]{0:T(256)S(1)} %collective-permute-done.other_ids, bf16[64,128,128]{2,1,0:T(8,128)(2,1)S(1)} %bitcast.53, bf16[64,128,128]{2,1,0:T(8,128)(2,1)S(1)} %copy-done.3, bf16[16,512,256]{2,1,0:T(8,128)(2,1)} %all-to-all-done.1.spread), custom_call_target="tpu_custom_call" | custom-call | flops 1073741824 | bytes 16777216 | tf_op jit(solution)/shard_map/pallas_call | solution.py:186
  192.0 2.0 copy-done
  194.0 0.1 pad_maximum_fusion.3
  194.0 4.6 %all-to-all-start.2 = ((bf16[16,512,256]{2,1,0:T(8,128)(2,1)}), bf16[16,512,256]{2,1,0:T(8,128)(2,1)}, u32[]{:S(2)}, u32[]{:S(2)}) async-start(bf16[16,512,256]{2,1,0:T(8,128)(2,1)} %bitcast.49), calls=%async_computation.2 | async-start | bytes 8388608 | tf_op jit(solution)/shard_map/all_to_all | solution.py:255
  198.6 0.3 collective-permute-start.21
  199.0 1.6 collective-permute-done.21
  200.6 0.1 pad_maximum_fusion.1
  200.7 1.1 collective-permute-start.22
  201.9 1.9 collective-permute-start.23
  203.8 2.5 collective-permute-start.24
  206.3 6.9 %collective-permute-done.22 = bf16[4,48,512]{2,1,0:T(8,128)(2,1)S(1)} collective-permute-done((bf16[4,48,512]{2,1,0:T(8,128)(2,1)S(1)}, bf16[4,48,512]{2,1,0:T(8,128)(2,1)S(1)}, u32[]{:S(2)}, u32[]{:S(2)}) %collective-permute-start.22) | collective-permute-done | bytes 196640 | tf_op jit(solution)/shard_map/ppermute | solution.py:214
  213.2 0.6 collective-permute-done.24
  213.7 0.1 fusion.3.own
  213.9 1.8 collective-permute-start.25
  215.7 2.4 collective-permute-start.26
  218.1 1.4 collective-permute-start.27
  219.4 2.3 collective-permute-done.25.moved_1
  221.8 5.4 %collective-permute-done.26.moved_2 = bf16[4,48,512]{2,1,0:T(8,128)(2,1)S(1)} collective-permute-done((bf16[4,48,512]{2,1,0:T(8,128)(2,1)S(1)}, bf16[4,48,512]{2,1,0:T(8,128)(2,1)S(1)}, u32[]{:S(2)}, u32[]{:S(2)}) %collective-permute-start.26) | collective-permute-done | bytes 196640 | tf_op jit(solution)/shard_map/ppermute | solution.py:214
  227.2 1.3 shard_map.116
  228.5 26.4 %all-to-all-done.2.parts = bf16[16,512,256]{2,1,0:T(8,128)(2,1)} async-done(((bf16[16,512,256]{2,1,0:T(8,128)(2,1)}), bf16[16,512,256]{2,1,0:T(8,128)(2,1)}, u32[]{:S(2)}, u32[]{:S(2)}) %all-to-all-start.2) | async-done | bytes 4194336 | tf_op jit(solution)/shard_map/all_to_all | solution.py:255
  254.8 3.5 %shard_map.115 = bf16[512,512]{1,0:T(8,128)(2,1)} custom-call(bf16[16,512,256]{2,1,0:T(8,128)(2,1)} %all-to-all-done.2.parts), custom_call_target="tpu_custom_call" | custom-call | bytes 4194304 | tf_op jit(solution)/shard_map/pallas_call | solution.py:186
  (38 shorter events, 0.3 us)
Async XLA Ops:
  0.6 52.4 %copy-start.1 = (bf16[1,1,64,128,128]{4,3,2,1,0:T(8,128)(2,1)S(1)}, bf16[1,1,64,128,128]{4,3,2,1,0:T(8,128)(2,1)}, u32[]{:S(2)}) copy-start(bf16[1,1,64,128,128]{4,3,2,1,0:T(8,128)(2,1)} %param.12) | copy-start | bytes 6291460
  0.6 52.4 %collective-permute-start.1 = (bf16[64,128,128]{2,1,0:T(8,128)(2,1)}, bf16[64,128,128]{2,1,0:T(8,128)(2,1)S(1)}, u32[]{:S(2)}, u32[]{:S(2)}) collective-permute-start(bf16[64,128,128]{2,1,0:T(8,128)(2,1)} %bitcast.51), channel_id=1, source_target_pairs={{0,8},{8,0},{16,24},{24,16},{32,40},{40,32},{48,56},{56,48},{64,72... | collective-permute-start | bytes 6291464 | tf_op jit(solution)/shard_map/ppermute | solution.py:201
  0.7 1.2 copy-start.7
  1.9 23.3 %copy-start.9 = (s32[1,1,64]{2,1,0:T(1,128)S(1)}, s32[1,1,64]{2,1,0:T(1,128)}, u32[]{:S(2)}) copy-start(s32[1,1,64]{2,1,0:T(1,128)} %param.13) | copy-start | bytes 772
  1.9 23.3 %copy-start.10 = (s32[1,1,64]{2,1,0:T(1,128)S(1)}, s32[1,1,64]{2,1,0:T(1,128)}, u32[]{:S(2)}) copy-start(s32[1,1,64]{2,1,0:T(1,128)} %param.14) | copy-start | bytes 772
  2.0 3.3 %collective-permute-start.2 = (bf16[512,256]{1,0:T(8,128)(2,1)S(1)}, bf16[512,256]{1,0:T(8,128)(2,1)S(1)}, u32[]{:S(2)}, u32[]{:S(2)}) collective-permute-start(bf16[512,256]{1,0:T(8,128)(2,1)S(1)} %get-tuple-element.18), channel_id=1, source_target_pairs={{0,8},{8,0},{16,24},{24,16},{32,40},{40,32},{48,56},{56,48},{64,72... | collective-permute-start | bytes 786440 | tf_op jit(solution)/shard_map/ppermute | solution.py:201
  5.3 10.0 %collective-permute-start.3 = (bf16[2,256,256]{2,1,0:T(8,128)(2,1)S(1)}, bf16[2,256,256]{2,1,0:T(8,128)(2,1)S(1)}, u32[]{:S(2)}, u32[]{:S(2)}) collective-permute-start(bf16[2,256,256]{2,1,0:T(8,128)(2,1)S(1)} %get-tuple-element.34), channel_id=1, source_target_pairs={{0,64},{1,65},{2,66},{3,67},{4,68},{5,69},{6,70},{7,71},{8,72},{9,... | collective-permute-start | bytes 786440 | tf_op jit(solution)/shard_map/ppermute | solution.py:206
  8.7 10.7 %collective-permute-start.5 = (bf16[2,256,256]{2,1,0:T(8,128)(2,1)S(1)}, bf16[2,256,256]{2,1,0:T(8,128)(2,1)S(1)}, u32[]{:S(2)}, u32[]{:S(2)}) collective-permute-start(bf16[2,256,256]{2,1,0:T(8,128)(2,1)S(1)} %get-tuple-element.33), channel_id=1, source_target_pairs={{0,32},{8,40},{16,48},{24,56},{32,0},{40,8},{48,16},{56,24},{64,96... | collective-permute-start | bytes 786440 | tf_op jit(solution)/shard_map/ppermute | solution.py:214
  11.7 12.3 %collective-permute-start.6 = (bf16[2,256,256]{2,1,0:T(8,128)(2,1)S(1)}, bf16[2,256,256]{2,1,0:T(8,128)(2,1)S(1)}, u32[]{:S(2)}, u32[]{:S(2)}) collective-permute-start(bf16[2,256,256]{2,1,0:T(8,128)(2,1)S(1)} %get-tuple-element.33), channel_id=1, source_target_pairs={{0,48},{8,56},{16,0},{24,8},{32,16},{40,24},{48,32},{56,40},{64,11... | collective-permute-start | bytes 786440 | tf_op jit(solution)/shard_map/ppermute | solution.py:214
  12.8 11.2 %collective-permute-start.4 = (bf16[2,256,256]{2,1,0:T(8,128)(2,1)S(1)}, bf16[2,256,256]{2,1,0:T(8,128)(2,1)S(1)}, u32[]{:S(2)}, u32[]{:S(2)}) collective-permute-start(bf16[2,256,256]{2,1,0:T(8,128)(2,1)S(1)} %get-tuple-element.33), channel_id=1, source_target_pairs={{0,16},{8,24},{16,32},{24,40},{32,48},{40,56},{48,0},{56,8},{64,80... | collective-permute-start | bytes 786440 | tf_op jit(solution)/shard_map/ppermute | solution.py:214
  24.1 28.9 %collective-permute-start.10 = (bf16[4,2,256,256]{3,2,1,0:T(8,128)(2,1)S(1)}, bf16[4,2,256,256]{3,2,1,0:T(8,128)(2,1)S(1)}, u32[]{:S(2)}, u32[]{:S(2)}) collective-permute-start(bf16[4,2,256,256]{3,2,1,0:T(8,128)(2,1)S(1)} %pad_maximum_fusion.refs_4_), channel_id=1, source_target_pairs={{0,64},{1,65},{2,66},{3,67},{4,68},{5,69},{6,70},{7,71},{8,72},{9,... | collective-permute-start | bytes 3145736 | tf_op jit(solution)/shard_map/ppermute | solution.py:206
  25.3 4.2 %collective-permute-start = (s32[129]{0:T(256)S(1)}, s32[129]{0:T(256)S(1)}, u32[]{:S(2)}, u32[]{:S(2)}) collective-permute-start(s32[129]{0:T(256)S(1)} %pad_add_fusion.ids), channel_id=1, source_target_pairs={{0,8},{8,0},{16,24},{24,16},{32,40},{40,32},{48,56},{56,48},{64,72... | collective-permute-start | bytes 1556 | tf_op jit(solution)/shard_map/ppermute | solution.py:201
  25.4 15.6 %collective-permute-start.7 = (bf16[2,2,256,256]{3,2,1,0:T(8,128)(2,1)S(1)}, bf16[2,2,256,256]{3,2,1,0:T(8,128)(2,1)S(1)}, u32[]{:S(2)}, u32[]{:S(2)}) collective-permute-start(bf16[2,2,256,256]{3,2,1,0:T(8,128)(2,1)S(1)} %pad_maximum_fusion.2.refs_0_), channel_id=1, source_target_pairs={{0,16},{8,24},{16,32},{24,40},{32,48},{40,56},{48,0},{56,8},{64,80... | collective-permute-start | bytes 1572872 | tf_op jit(solution)/shard_map/ppermute | solution.py:214
  26.9 26.1 %collective-permute-start.8 = (bf16[2,2,256,256]{3,2,1,0:T(8,128)(2,1)S(1)}, bf16[2,2,256,256]{3,2,1,0:T(8,128)(2,1)S(1)}, u32[]{:S(2)}, u32[]{:S(2)}) collective-permute-start(bf16[2,2,256,256]{3,2,1,0:T(8,128)(2,1)S(1)} %pad_maximum_fusion.2.refs_0_), channel_id=1, source_target_pairs={{0,32},{8,40},{16,48},{24,56},{32,0},{40,8},{48,16},{56,24},{64,96... | collective-permute-start | bytes 1572872 | tf_op jit(solution)/shard_map/ppermute | solution.py:214
  29.5 23.5 %collective-permute-start.9 = (bf16[2,2,256,256]{3,2,1,0:T(8,128)(2,1)S(1)}, bf16[2,2,256,256]{3,2,1,0:T(8,128)(2,1)S(1)}, u32[]{:S(2)}, u32[]{:S(2)}) collective-permute-start(bf16[2,2,256,256]{3,2,1,0:T(8,128)(2,1)S(1)} %pad_maximum_fusion.2.refs_0_), channel_id=1, source_target_pairs={{0,48},{8,56},{16,0},{24,8},{32,16},{40,24},{48,32},{56,40},{64,11... | collective-permute-start | bytes 1572872 | tf_op jit(solution)/shard_map/ppermute | solution.py:214
  53.0 5.5 %copy-start.2 = (bf16[64,128,128]{2,1,0:T(8,128)(2,1)}, bf16[64,128,128]{2,1,0:T(8,128)(2,1)S(1)}, u32[]{:S(2)}) copy-start(bf16[64,128,128]{2,1,0:T(8,128)(2,1)S(1)} %collective-permute-done.1.other_tiles) | copy-start | bytes 6291460
  58.6 55.9 %copy-start.5 = (bf16[512,512]{1,0:T(8,128)(2,1)S(1)}, bf16[512,512]{1,0:T(8,128)(2,1)}, u32[]{:S(2)}) copy-start(bf16[512,512]{1,0:T(8,128)(2,1)} %weight.1) | copy-start | bytes 1572868
  58.6 55.9 %copy-start.6 = (bf16[512,512]{1,0:T(8,128)(2,1)S(1)}, bf16[512,512]{1,0:T(8,128)(2,1)}, u32[]{:S(2)}) copy-start(bf16[512,512]{1,0:T(8,128)(2,1)} %cotangent.1) | copy-start | bytes 1572868
  58.6 55.9 %copy-start.8 = (f32[512]{0:T(512)S(1)}, f32[512]{0:T(512)}, u32[]{:S(2)}) copy-start(f32[512]{0:T(512)} %param.10) | copy-start | bytes 6148
  117.6 2.0 copy-start.4
  119.6 59.9 %all-to-all-start.1 = ((bf16[16,512,256]{2,1,0:T(8,128)(2,1)}), bf16[16,512,256]{2,1,0:T(8,128)(2,1)}, u32[]{:S(2)}, u32[]{:S(2)}) async-start(bf16[16,512,256]{2,1,0:T(8,128)(2,1)} %copy-done.4), calls=%async_computation.1 | async-start | bytes 8388608 | tf_op jit(solution)/shard_map/all_to_all | solution.py:259
  124.2 1.8 collective-permute-start.11
  126.1 6.3 %collective-permute-start.12 = (bf16[2,48,512]{2,1,0:T(8,128)(2,1)S(1)}, bf16[2,48,512]{2,1,0:T(8,128)(2,1)S(1)}, u32[]{:S(2)}, u32[]{:S(2)}) collective-permute-start(bf16[2,48,512]{2,1,0:T(8,128)(2,1)S(1)} %get-tuple-element.35), channel_id=1, source_target_pairs={{0,16},{8,24},{16,32},{24,40},{32,48},{40,56},{48,0},{56,8},{64,80... | collective-permute-start | bytes 294920 | tf_op jit(solution)/shard_map/ppermute | solution.py:214
  127.1 8.0 %collective-permute-start.13 = (bf16[2,48,512]{2,1,0:T(8,128)(2,1)S(1)}, bf16[2,48,512]{2,1,0:T(8,128)(2,1)S(1)}, u32[]{:S(2)}, u32[]{:S(2)}) collective-permute-start(bf16[2,48,512]{2,1,0:T(8,128)(2,1)S(1)} %get-tuple-element.37), channel_id=1, source_target_pairs={{0,32},{8,40},{16,48},{24,56},{32,0},{40,8},{48,16},{56,24},{64,96... | collective-permute-start | bytes 294920 | tf_op jit(solution)/shard_map/ppermute | solution.py:214
  130.1 5.0 %collective-permute-start.14 = (bf16[2,48,512]{2,1,0:T(8,128)(2,1)S(1)}, bf16[2,48,512]{2,1,0:T(8,128)(2,1)S(1)}, u32[]{:S(2)}, u32[]{:S(2)}) collective-permute-start(bf16[2,48,512]{2,1,0:T(8,128)(2,1)S(1)} %get-tuple-element.36), channel_id=1, source_target_pairs={{0,48},{8,56},{16,0},{24,8},{32,16},{40,24},{48,32},{56,40},{64,11... | collective-permute-start | bytes 294920 | tf_op jit(solution)/shard_map/ppermute | solution.py:214
  135.2 41.7 %collective-permute-start.15 = (bf16[2,48,512]{2,1,0:T(8,128)(2,1)S(1)}, bf16[2,48,512]{2,1,0:T(8,128)(2,1)S(1)}, u32[]{:S(2)}, u32[]{:S(2)}) collective-permute-start(bf16[2,48,512]{2,1,0:T(8,128)(2,1)S(1)} %fusion.7), channel_id=1, source_target_pairs={{0,1},{1,0},{2,3},{3,2},{4,5},{5,4},{6,7},{7,6},{8,9},{9,8},{10,11... | collective-permute-start | bytes 294920 | tf_op jit(solution)/shard_map/ppermute | solution.py:206
  137.0 42.4 %collective-permute-start.16 = (bf16[2,48,512]{2,1,0:T(8,128)(2,1)S(1)}, bf16[2,48,512]{2,1,0:T(8,128)(2,1)S(1)}, u32[]{:S(2)}, u32[]{:S(2)}) collective-permute-start(bf16[2,48,512]{2,1,0:T(8,128)(2,1)S(1)} %fusion.7), channel_id=1, source_target_pairs={{0,64},{1,65},{2,66},{3,67},{4,68},{5,69},{6,70},{7,71},{8,72},{9,... | collective-permute-start | bytes 294920 | tf_op jit(solution)/shard_map/ppermute | solution.py:206
  140.4 39.0 %collective-permute-start.17 = (bf16[2,48,512]{2,1,0:T(8,128)(2,1)S(1)}, bf16[2,48,512]{2,1,0:T(8,128)(2,1)S(1)}, u32[]{:S(2)}, u32[]{:S(2)}) collective-permute-start(bf16[2,48,512]{2,1,0:T(8,128)(2,1)S(1)} %fusion.7), channel_id=1, source_target_pairs={{0,65},{1,64},{2,67},{3,66},{4,69},{5,68},{6,71},{7,70},{8,73},{9,... | collective-permute-start | bytes 294920 | tf_op jit(solution)/shard_map/ppermute | solution.py:206
  179.5 14.5 %collective-permute-start.18 = (bf16[2,48,512]{2,1,0:T(8,128)(2,1)S(1)}, bf16[2,48,512]{2,1,0:T(8,128)(2,1)S(1)}, u32[]{:S(2)}, u32[]{:S(2)}) collective-permute-start(bf16[2,48,512]{2,1,0:T(8,128)(2,1)S(1)} %add_convert_fusion), channel_id=1, source_target_pairs={{0,16},{8,24},{16,32},{24,40},{32,48},{40,56},{48,0},{56,8},{64,80... | collective-permute-start | bytes 294920 | tf_op jit(solution)/shard_map/ppermute | solution.py:214
  180.4 13.6 %collective-permute-start.19 = (bf16[2,48,512]{2,1,0:T(8,128)(2,1)S(1)}, bf16[2,48,512]{2,1,0:T(8,128)(2,1)S(1)}, u32[]{:S(2)}, u32[]{:S(2)}) collective-permute-start(bf16[2,48,512]{2,1,0:T(8,128)(2,1)S(1)} %add_convert_fusion), channel_id=1, source_target_pairs={{0,32},{8,40},{16,48},{24,56},{32,0},{40,8},{48,16},{56,24},{64,96... | collective-permute-start | bytes 294920 | tf_op jit(solution)/shard_map/ppermute | solution.py:214
  182.8 11.2 %collective-permute-start.20 = (bf16[2,48,512]{2,1,0:T(8,128)(2,1)S(1)}, bf16[2,48,512]{2,1,0:T(8,128)(2,1)S(1)}, u32[]{:S(2)}, u32[]{:S(2)}) collective-permute-start(bf16[2,48,512]{2,1,0:T(8,128)(2,1)S(1)} %add_convert_fusion), channel_id=1, source_target_pairs={{0,48},{8,56},{16,0},{24,8},{32,16},{40,24},{48,32},{56,40},{64,11... | collective-permute-start | bytes 294920 | tf_op jit(solution)/shard_map/ppermute | solution.py:214
  184.2 1.6 copy-start.3
  191.9 2.0 copy-start
  194.0 60.8 %all-to-all-start.2 = ((bf16[16,512,256]{2,1,0:T(8,128)(2,1)}), bf16[16,512,256]{2,1,0:T(8,128)(2,1)}, u32[]{:S(2)}, u32[]{:S(2)}) async-start(bf16[16,512,256]{2,1,0:T(8,128)(2,1)} %bitcast.49), calls=%async_computation.2 | async-start | bytes 8388608 | tf_op jit(solution)/shard_map/all_to_all | solution.py:255
  198.6 2.0 collective-permute-start.21
  200.7 12.4 %collective-permute-start.22 = (bf16[4,48,512]{2,1,0:T(8,128)(2,1)S(1)}, bf16[4,48,512]{2,1,0:T(8,128)(2,1)S(1)}, u32[]{:S(2)}, u32[]{:S(2)}) collective-permute-start(bf16[4,48,512]{2,1,0:T(8,128)(2,1)S(1)} %get-tuple-element.30), channel_id=1, source_target_pairs={{0,2},{1,3},{2,4},{3,5},{4,6},{5,7},{6,0},{7,1},{8,10},{9,11},{10,... | collective-permute-start | bytes 589832 | tf_op jit(solution)/shard_map/ppermute | solution.py:214
  201.9 11.3 %collective-permute-start.23 = (bf16[4,48,512]{2,1,0:T(8,128)(2,1)S(1)}, bf16[4,48,512]{2,1,0:T(8,128)(2,1)S(1)}, u32[]{:S(2)}, u32[]{:S(2)}) collective-permute-start(bf16[4,48,512]{2,1,0:T(8,128)(2,1)S(1)} %get-tuple-element.32), channel_id=1, source_target_pairs={{0,4},{1,5},{2,6},{3,7},{4,0},{5,1},{6,2},{7,3},{8,12},{9,13},{10,... | collective-permute-start | bytes 589832 | tf_op jit(solution)/shard_map/ppermute | solution.py:214
  203.8 10.0 %collective-permute-start.24 = (bf16[4,48,512]{2,1,0:T(8,128)(2,1)S(1)}, bf16[4,48,512]{2,1,0:T(8,128)(2,1)S(1)}, u32[]{:S(2)}, u32[]{:S(2)}) collective-permute-start(bf16[4,48,512]{2,1,0:T(8,128)(2,1)S(1)} %get-tuple-element.31), channel_id=1, source_target_pairs={{0,6},{1,7},{2,0},{3,1},{4,2},{5,3},{6,4},{7,5},{8,14},{9,15},{10,... | collective-permute-start | bytes 589832 | tf_op jit(solution)/shard_map/ppermute | solution.py:214
  213.9 7.9 %collective-permute-start.25 = (bf16[4,48,512]{2,1,0:T(8,128)(2,1)S(1)}, bf16[4,48,512]{2,1,0:T(8,128)(2,1)S(1)}, u32[]{:S(2)}, u32[]{:S(2)}) collective-permute-start(bf16[4,48,512]{2,1,0:T(8,128)(2,1)S(1)} %fusion.3.own), channel_id=1, source_target_pairs={{0,2},{1,3},{2,4},{3,5},{4,6},{5,7},{6,0},{7,1},{8,10},{9,11},{10,... | collective-permute-start | bytes 589832 | tf_op jit(solution)/shard_map/ppermute | solution.py:214
  215.7 11.5 %collective-permute-start.26 = (bf16[4,48,512]{2,1,0:T(8,128)(2,1)S(1)}, bf16[4,48,512]{2,1,0:T(8,128)(2,1)S(1)}, u32[]{:S(2)}, u32[]{:S(2)}) collective-permute-start(bf16[4,48,512]{2,1,0:T(8,128)(2,1)S(1)} %fusion.3.own), channel_id=1, source_target_pairs={{0,4},{1,5},{2,6},{3,7},{4,0},{5,1},{6,2},{7,3},{8,12},{9,13},{10,... | collective-permute-start | bytes 589832 | tf_op jit(solution)/shard_map/ppermute | solution.py:214
  218.1 9.1 %collective-permute-start.27 = (bf16[4,48,512]{2,1,0:T(8,128)(2,1)S(1)}, bf16[4,48,512]{2,1,0:T(8,128)(2,1)S(1)}, u32[]{:S(2)}, u32[]{:S(2)}) collective-permute-start(bf16[4,48,512]{2,1,0:T(8,128)(2,1)S(1)} %fusion.3.own), channel_id=1, source_target_pairs={{0,6},{1,7},{2,0},{3,1},{4,2},{5,3},{6,4},{7,5},{8,14},{9,15},{10,... | collective-permute-start | bytes 589832 | tf_op jit(solution)/shard_map/ppermute | solution.py:214

commit v4 on v3

v4 whole, which is shorter than its diff:
```python
import functools
import math

import jax
import jax.numpy as jnp
from jax import lax
from jax.experimental import pallas as pl
from jax.experimental.pallas import tpu as pltpu
from jax.sharding import PartitionSpec as P

BF = jnp.bfloat16
F32 = jnp.float32
VMEM_LIMIT = 26 * 2**20
UNROLL = 16
HALF = 256
FIRST = 256
SHARE = 32
TAIL = 16
X_LINES = [[y * 8 + x * 2 + core for x in range(4)] for y in range(2) for core in range(2)]
Z_LINES = [[z * 2 + y for z in range(4)] for y in range(2)]
Y_LINES = [
    [(high * 8 + line) * 8 + z * 2 + low for high in range(2) for low in range(2)] for line in range(8) for z in range(4)
]


def tile_loop(count, acc, step):
    def body(i, carry):
        found = [step(i * UNROLL + j, i * UNROLL + j < count) for j in range(UNROLL)]
        for target, product in found:
            acc[target] += product
        return carry

    lax.fori_loop(0, (count + UNROLL - 1) // UNROLL, body, 0)


def loop(n, step):
    def body(i, carry):
        step(i)
        return carry

    lax.fori_loop(0, n, body, 0)


def start_loads(sources, acc, sems):
    copies = [pltpu.make_async_copy(a, b, sems.at[i]) for i, (a, b) in enumerate(sources)]
    for copy in copies:
        copy.start()

    @functools.partial(loop, acc.shape[0] - 1)
    def _(i):
        acc[i] = jnp.zeros(acc.shape[1:], F32)

    for copy in copies:
        copy.wait()


def halves_kernel(features, mine, other):
    left = lax.axis_index("row") % 2 == 0
    first, second = features[:, :HALF], features[:, HALF:]
    mine[...] = jnp.where(left, first, second)
    other[...] = jnp.where(left, second, first)


def route_loads(pieces, source):
    own, ring_1, ring_2, ring_3, near, far = pieces
    low, high = pl.ds(0, FIRST), pl.ds(FIRST, 512 - FIRST)
    loads = [(piece, source.at[d, :, :, low]) for d, piece in enumerate((own, ring_1, ring_2, ring_3))]
    return loads + [(near, source.at[:, 0, :, high]), (far, source.at[:, 1, :, high])]


def store_parts(acc, outs):
    stay_first, over_y, stay_rest, *ahead = outs
    for d in range(4):
        for y in range(2):
            for core in range(2):
                at = ((d * 2 + y) * 2 + core) * 4
                for b in range(2):
                    rows = slice(b * 128, (b + 1) * 128)
                    (over_y if y else stay_first)[d, core, rows, :] = acc[at + b].astype(BF)
                    (stay_rest if d == 0 else ahead[d - 1])[y, core, rows, :] = acc[at + 2 + b].astype(BF)


def places(k, table, side):
    row_me, col_me = lax.axis_index("row"), lax.axis_index("col")
    col, row = table[k], lax.rem(table[64 + k], 32)
    owner = col // 32
    x = lax.rem(owner // 2, 4) - lax.rem(row_me // 2, 4)
    z = row // 8 - col_me // 2
    col_place = (x, lax.rem(owner // 8 + row_me // 8, 2), lax.rem(owner + row_me, 2), lax.rem(col, 4))
    return col_place, (z, lax.rem(row // 4 + col_me, 2), side, lax.rem(row, 4))


def pick(source, place):
    step, y, core, block = place
    return source[lax.rem(4 - step, 4), y, core, pl.ds(pl.multiple_of(block * 128, 128), 128), :]


def place_in_acc(place, live):
    step, y, core, block = place
    return jnp.where(live, lax.rem(step + 4, 4) * 16 + y * 8 + core * 4 + block, 64)


def tiles_kernel(transposed, ids, other_ids, tiles, other_tiles, *refs):
    pieces, outs, (source, vals, acc, sems) = refs[:6], refs[6:12], refs[12:]
    start_loads([(tiles, vals.at[0]), (other_tiles, vals.at[1]), *route_loads(pieces, source)], acc, sems)
    for side, table in enumerate((ids, other_ids)):

        @functools.partial(tile_loop, table[128], acc)
        def _(k, live, side=side, table=table):
            col_place, row_place = places(k, table, side)
            if transposed:
                product = lax.dot_general(
                    vals[side, k], pick(source, row_place), (((0,), (0,)), ((), ())), preferred_element_type=F32
                )
                return place_in_acc(col_place, live), product
            product = jnp.dot(vals[side, k], pick(source, col_place), preferred_element_type=F32)
            return place_in_acc(row_place, live), product

    store_parts(acc, outs)


def dense_kernel(
    scale, mine, other, weight, bias, cotangent, output, grad_mine, grad_other, chunks, agg, grad_pre, product
):
    size = 128
    core = lax.rem(lax.axis_index("row"), 2)
    left = core == 0

    def body(i, bias_sum):
        at = pl.ds(pl.multiple_of(i * size, size), size)
        a, b = mine[at, :], other[at, :]
        agg[at, :HALF] = jnp.where(left, a, b)
        agg[at, HALF:] = jnp.where(left, b, a)
        pre = jnp.dot(agg[at, :], weight[...], preferred_element_type=F32) + bias[...]
        s = jax.nn.sigmoid(pre)
        output[at, :] = (pre * s).astype(BF)
        grad = (cotangent[at, :].astype(F32) * s * (1.0 + pre * (1.0 - s))).astype(BF)
        grad_pre[at, :] = grad
        back = lax.dot_general(grad, weight[...], (((1,), (1,)), ((), ())), preferred_element_type=F32).astype(BF)
        grad_mine[at, :] = jnp.where(left, back[:, :HALF], back[:, HALF:])
        grad_other[at, :] = jnp.where(left, back[:, HALF:], back[:, :HALF])
        return bias_sum + jnp.sum(grad.astype(F32), axis=0, keepdims=True)

    bias_sum = lax.fori_loop(0, agg.shape[0] // size, body, jnp.zeros((1, agg.shape[1]), F32)) * scale
    product[...] = lax.dot_general(agg[...], grad_pre[...], (((0,), (0,)), ((), ())), preferred_element_type=F32)
    tail = jnp.broadcast_to(bias_sum, (TAIL, agg.shape[1])).astype(BF)
    for far in range(2):
        for x in range(4):
            for y in range(2):
                owner = y * 8 + x * 2 + lax.rem(core + far, 2)
                rows = product[pl.ds(pl.multiple_of(owner * SHARE, SHARE), SHARE), :]
                chunks[far, x, y, :SHARE, :] = (rows * scale).astype(BF)
                chunks[far, x, y, SHARE:, :] = tail


def place_kernel(chunks, weight_grad, bias_grad):
    me = lax.axis_index("row")
    for flat in range(16):
        far, x, y = flat // 8, flat // 2 % 4, flat % 2
        owner = y * 8 + lax.rem(lax.rem(me // 2, 4) + 4 - x, 4) * 2 + lax.rem(me + far, 2)
        at = pl.ds(pl.multiple_of(owner * SHARE, SHARE), SHARE)
        weight_grad[at, :] = chunks[flat // 4, flat % 4, :SHARE, :].astype(F32)
    bias_grad[...] = chunks[0, 0, SHARE : SHARE + 1, :].astype(F32)


def final_kernel(mine, other, out):
    left = lax.axis_index("row") % 2 == 0
    a, b = mine[...], other[...]
    out[:, :HALF] = jnp.where(left, a, b)
    out[:, HALF:] = jnp.where(left, b, a)


def any_spec():
    return pl.BlockSpec(memory_space=pl.ANY)


def vmem_spec():
    return pl.BlockSpec(memory_space=pltpu.VMEM)


def call(kernel, args, out_shape, ids=(), in_specs=None, out_specs=None, scratch=(), flops=0, moved=4 * 2**20):
    shapes = [jax.ShapeDtypeStruct(s, d) for s, d in out_shape]
    return pl.pallas_call(
        kernel,
        grid_spec=pltpu.PrefetchScalarGridSpec(
            num_scalar_prefetch=len(ids),
            in_specs=in_specs or [vmem_spec() for _ in args],
            out_specs=out_specs or [vmem_spec() for _ in shapes],
            scratch_shapes=scratch,
        ),
        out_shape=shapes,
        compiler_params=pltpu.CompilerParams(vmem_limit_bytes=VMEM_LIMIT),
        cost_estimate=pl.CostEstimate(flops=flops, bytes_accessed=moved, transcendentals=0),
    )(*ids, *args)


def core_swap(value):
    return lax.ppermute(value, "row", [(i, i ^ 1) for i in range(16)])


def swap_y(value, high, low):
    to = [(i, i ^ (64 * high + low)) for i in range(128)]
    return lax.ppermute(value, ("row", "col"), to)


def shift(value, axis, d):
    if axis == "row":
        to = [(i, i // 8 * 8 + (i + 2 * d) % 8) for i in range(16)]
    else:
        to = [(i, (i + 2 * d) % 8) for i in range(8)]
    return lax.ppermute(value, axis, to)


def add(*parts):
    total = parts[0].astype(F32)
    for part in parts[1:]:
        total = total + part.astype(F32)
    return total.astype(BF)


def plane_sum(chunks):
    part = add(chunks[0], core_swap(chunks[1]))
    part = add(*lax.all_to_all(part, "row", 0, 0, tiled=True, axis_index_groups=X_LINES))
    return add(*lax.all_to_all(fourfold(part), ("row", "col"), 0, 0, tiled=True, axis_index_groups=Y_LINES))


def fourfold(value):
    return jnp.broadcast_to(value[None], (4, *value.shape))


def ring(part, axis):
    return (part, *(shift(part, axis, d) for d in range(1, 4)))


def two_way_gather(mine, other, axis):
    pair = jnp.stack([mine, other])
    high, low = (1, 0) if axis == "row" else (0, 1)
    first, rest = pair[:, :FIRST], pair[:, FIRST:]
    near = jnp.stack(ring(rest, axis))
    first = jnp.stack([first, swap_y(first, high, low)])
    first, near = lax.optimization_barrier((first, near))
    return (*ring(first, axis), near, swap_y(near, high, low))


def two_way_scatter(parts, axis):
    stay_first, over_y, stay_rest, *ahead = parts
    high, low = (1, 0) if axis == "row" else (0, 1)
    from_y = swap_y(over_y, high, low)
    moved = [shift(part, axis, d + 1) for d, part in enumerate(ahead)]
    rest = [add(stay_rest[y], *(part[y] for part in moved)) for y in range(2)]
    first = [add(stay_first[d], from_y[d]) for d in range(4)]
    first, rest = lax.optimization_barrier((first, rest))
    first = add(first[0], *(shift(first[d], axis, d) for d in range(1, 4)))
    rest = add(rest[0], swap_y(rest[1], high, low))
    total = jnp.concatenate([first, rest], axis=1)
    return total[0], core_swap(total[1])


def z_sum(chunks):
    parts = chunks.reshape(4, 4, *chunks.shape[-2:])
    part = add(*lax.all_to_all(parts, "col", 0, 0, tiled=True, axis_index_groups=Z_LINES))
    return lax.all_to_all(fourfold(part), "col", 0, 0, tiled=True, axis_index_groups=Z_LINES)


def on_device(features, weight, bias, cotangent, tile_values, tile_rows, tile_cols, tile_counts):
    tiles = tile_values.reshape(64, 128, 128)
    ids = jnp.concatenate([tile_cols.reshape(64), tile_rows.reshape(64), tile_counts.reshape(1)])
    other_tiles, other_ids = core_swap(tiles), core_swap(ids)
    scale = 1.0 / math.sqrt(65536)
    tables = (ids, other_ids)
    def multiply(transposed, pieces):
        rest, whole = 512 - FIRST, (4, 2, 2, 512, HALF)
        return call(
            functools.partial(tiles_kernel, transposed),
            (tiles, other_tiles, *pieces),
            [((4, 2, FIRST, HALF), BF)] * 2 + [((2, 2, rest, HALF), BF)] * 4,
            ids=tables,
            in_specs=[any_spec()] * 8,
            scratch=[
                pltpu.VMEM(whole, BF),
                pltpu.VMEM((2, 64, 128, 128), BF),
                pltpu.VMEM((65, 128, HALF), F32),
                pltpu.SemaphoreType.DMA((8,)),
            ],
            flops=2 * 64 * 128 * 128 * 512,
            moved=16 * 2**20,
        )

    mine, other = call(halves_kernel, (features,), [((512, HALF), BF)] * 2)
    pieces = two_way_gather(mine, core_swap(other), "row")
    mine, other = two_way_scatter(multiply(False, pieces), "col")
    output, mine, other, chunks = call(
        functools.partial(dense_kernel, scale),
        (mine, other, weight, bias.reshape(1, 512), cotangent),
        [((512, 512), BF), ((512, HALF), BF), ((512, HALF), BF), ((2, 4, 2, SHARE + TAIL, 512), BF)],
        scratch=[pltpu.VMEM((512, 512), BF), pltpu.VMEM((512, 512), BF), pltpu.VMEM((512, 512), F32)],
        flops=6 * 512**3,
        moved=8 * 2**20,
    )
    pieces = two_way_gather(mine, core_swap(other), "col")
    chunks, pieces = lax.optimization_barrier((plane_sum(chunks), pieces))
    parts = multiply(True, pieces)
    chunks, parts = lax.optimization_barrier((jnp.stack(ring(chunks, "row")), parts))
    mine, other = two_way_scatter(parts, "row")
    chunks = jnp.stack([chunks, core_swap(chunks)])
    weight_grad, bias_grad = call(place_kernel, (z_sum(chunks),), [((512, 512), F32), ((1, 512), F32)])
    (feature_grad,) = call(final_kernel, (mine, other), [((512, 512), BF)])
    return (output, feature_grad, weight_grad, bias_grad.reshape(512))


def solution(mesh):
    return jax.shard_map(
        on_device,
        mesh=mesh,
        in_specs=(
            P(("row", "col"), None),
            P(),
            P(),
            P(("row", "col"), None),
            P("row", "col", None, None, None),
            P("row", "col", None),
            P("row", "col", None),
            P("row", "col"),
        ),
        out_specs=(P(("row", "col"), None), P(("row", "col"), None), P(), P()),
        check_vma=False,
    )
```

time: 261 us -> 237 us (0.908)
  blocking collectives: 55.9 us -> 17.5 us
  starting transfers between devices: 51.8 us -> 67.4 us
  other arithmetic: 0.76 us -> 7.87 us
  waiting for transfers between devices: 122 us -> 118 us
    ppermute x18 -> x27, waiting for transfers between devices: 48.9 us -> 93.7 us  [shift(): return lax.ppermute(value, axis, to)]
    all_to_all x1, blocking collectives: 55.9 us -> 17.5 us  [plane_sum(): lax.all_to_all(fourfold(part), ('row', 'col'), 0, 0, tiled=True, axis_ind...]
    ppermute x5 -> x8, waiting for transfers between devices: 40.5 us -> 7.88 us  [swap_y(): return lax.ppermute(value, ('row', 'col'), to)]
    all_to_all x2 -> x3, waiting for transfers between devices: 26.4 us -> 10.3 us  [the longest x1 5.14 us: plane_sum(): lax.all_to_all(part, 'row', 0, 0, tiled=True, axis_index_groups=X_LINES)]
    ppermute x18 -> x27, starting transfers between devices: 32.5 us -> 43.5 us  [shift(): return lax.ppermute(value, axis, to)]
    ppermute x5 -> x8, starting transfers between devices: 9.07 us -> 12.3 us  [swap_y(): return lax.ppermute(value, ('row', 'col'), to)]
    unnamed x22 -> x28, local copies, waits for them, and re-layouts: 6.83 us -> 3.86 us
    add x0 -> x3, other arithmetic: none -> 2.78 us  [add(): total = total + part.astype(F32)]
  transfers between devices with their start and end apart: 30 -> 46, of which waited for: 17 -> 21; matrix products, arithmetic and copies ran while one was open for 0% -> 4% of each run, Pallas kernels for 3% -> 4%
where the time goes in v4:
time: 237 us; the launch traced here: 236 us
  waiting for transfers between devices  118 us (50%)
  starting transfers between devices  67.4 us (28%)
  Pallas kernels  19.4 us (8%)
  blocking collectives  17.5 us (7%)
  other arithmetic  7.87 us (3%)
  local copies, waits for them, and re-layouts  4.87 us (2%)
    ppermute x27, waiting for transfers between devices, shift(): return lax.ppermute(value, axis, to)  93.7 us
    ppermute x27, starting transfers between devices, shift(): return lax.ppermute(value, axis, to)  43.5 us
    pallas_call x6, Pallas kernels, call(): pl.pallas_call(kernel, grid_spec=pltpu.PrefetchScalarGridSpec(num_scalar_...  19.4 us
    all_to_all x1, blocking collectives, plane_sum(): lax.all_to_all(fourfold(part), ('row', 'col'), 0, 0, tiled=True, axis_ind...  17.5 us
    ppermute x8, starting transfers between devices, swap_y(): return lax.ppermute(value, ('row', 'col'), to)  12.3 us
    ppermute x8, waiting for transfers between devices, swap_y(): return lax.ppermute(value, ('row', 'col'), to)  7.88 us
    ppermute x8, waiting for transfers between devices, core_swap(): return lax.ppermute(value, 'row', [(i, i ^ 1) for i in range(16)])  5.77 us
    all_to_all x1, waiting for transfers between devices, plane_sum(): lax.all_to_all(part, 'row', 0, 0, tiled=True, axis_index_groups=X_LINES)  5.14 us
  transfers between devices with their start and end apart: 46, of which 21 were waited for; matrix products, arithmetic and copies ran while one was open for 4% of the time, Pallas kernels for 4%

profile of v4, /device:TPU:0, one launch (start us, length us, event | category | flops | bytes accessed | tf_op | source)
XLA Modules:
  0.0 236.4 jit_solution(9491036086230074639)
XLA Ops:
  0.7 1.0 copy-done.7
  2.4 2.8 %collective-permute-done.2 = bf16[512,256]{1,0:T(8,128)(2,1)S(1)} collective-permute-done((bf16[512,256]{1,0:T(8,128)(2,1)S(1)}, bf16[512,256]{1,0:T(8,128)(2,1)S(1)}, u32[]{:S(2)}, u32[]{:S(2)}) %collective-permute-start.2) | collective-permute-done | bytes 262176 | tf_op jit(solution)/shard_map/ppermute | solution.py:198
  5.3 3.4 %collective-permute-start.3 = (bf16[2,256,256]{2,1,0:T(8,128)(2,1)S(1)}, bf16[2,256,256]{2,1,0:T(8,128)(2,1)S(1)}, u32[]{:S(2)}, u32[]{:S(2)}) collective-permute-start(bf16[2,256,256]{2,1,0:T(8,128)(2,1)S(1)} %get-tuple-element.123), channel_id=1, source_target_pairs={{0,64},{1,65},{2,66},{3,67},{4,68},{5,69},{6,70},{7,71},{8,72},{9,... | collective-permute-start | bytes 786440 | tf_op jit(solution)/shard_map/ppermute | solution.py:203
  8.7 3.0 %collective-permute-start.5 = (bf16[2,256,256]{2,1,0:T(8,128)(2,1)S(1)}, bf16[2,256,256]{2,1,0:T(8,128)(2,1)S(1)}, u32[]{:S(2)}, u32[]{:S(2)}) collective-permute-start(bf16[2,256,256]{2,1,0:T(8,128)(2,1)S(1)} %get-tuple-element.122), channel_id=1, source_target_pairs={{0,32},{8,40},{16,48},{24,56},{32,0},{40,8},{48,16},{56,24},{64,96... | collective-permute-start | bytes 786440 | tf_op jit(solution)/shard_map/ppermute | solution.py:211
  12.3 2.6 %collective-permute-start.6 = (bf16[2,256,256]{2,1,0:T(8,128)(2,1)S(1)}, bf16[2,256,256]{2,1,0:T(8,128)(2,1)S(1)}, u32[]{:S(2)}, u32[]{:S(2)}) collective-permute-start(bf16[2,256,256]{2,1,0:T(8,128)(2,1)S(1)} %get-tuple-element.122), channel_id=1, source_target_pairs={{0,48},{8,56},{16,0},{24,8},{32,16},{40,24},{48,32},{56,40},{64,11... | collective-permute-start | bytes 786440 | tf_op jit(solution)/shard_map/ppermute | solution.py:211
  15.3 4.1 %collective-permute-done.5 = bf16[2,256,256]{2,1,0:T(8,128)(2,1)S(1)} collective-permute-done((bf16[2,256,256]{2,1,0:T(8,128)(2,1)S(1)}, bf16[2,256,256]{2,1,0:T(8,128)(2,1)S(1)}, u32[]{:S(2)}, u32[]{:S(2)}) %collective-permute-start.5) | collective-permute-done | bytes 262176 | tf_op jit(solution)/shard_map/ppermute | solution.py:211
  19.4 4.4 %collective-permute-done.4 = bf16[2,256,256]{2,1,0:T(8,128)(2,1)S(1)} collective-permute-done((bf16[2,256,256]{2,1,0:T(8,128)(2,1)S(1)}, bf16[2,256,256]{2,1,0:T(8,128)(2,1)S(1)}, u32[]{:S(2)}, u32[]{:S(2)}) %collective-permute-start.4) | collective-permute-done | bytes 262176 | tf_op jit(solution)/shard_map/ppermute | solution.py:211
  25.3 2.7 %collective-permute-start.9 = (bf16[2,2,256,256]{3,2,1,0:T(8,128)(2,1)S(1)}, bf16[2,2,256,256]{3,2,1,0:T(8,128)(2,1)S(1)}, u32[]{:S(2)}, u32[]{:S(2)}) collective-permute-start(bf16[2,2,256,256]{3,2,1,0:T(8,128)(2,1)S(1)} %pad_maximum_fusion.3.refs_0_), channel_id=1, source_target_pairs={{0,48},{8,56},{16,0},{24,8},{32,16},{40,24},{48,32},{56,40},{64,11... | collective-permute-start | bytes 1572872 | tf_op jit(solution)/shard_map/ppermute | solution.py:211
  28.0 0.9 collective-permute-start.8
  29.0 22.1 %collective-permute-done.9.refs_3_ = bf16[2,2,256,256]{3,2,1,0:T(8,128)(2,1)S(1)} collective-permute-done((bf16[2,2,256,256]{3,2,1,0:T(8,128)(2,1)S(1)}, bf16[2,2,256,256]{3,2,1,0:T(8,128)(2,1)S(1)}, u32[]{:S(2)}, u32[]{:S(2)}) %collective-permute-start.9) | collective-permute-done | bytes 524320 | tf_op jit(solution)/shard_map/ppermute | solution.py:211
  51.1 3.7 %collective-permute-done.7.refs_1_ = bf16[2,2,256,256]{3,2,1,0:T(8,128)(2,1)S(1)} collective-permute-done((bf16[2,2,256,256]{3,2,1,0:T(8,128)(2,1)S(1)}, bf16[2,2,256,256]{3,2,1,0:T(8,128)(2,1)S(1)}, u32[]{:S(2)}, u32[]{:S(2)}) %collective-permute-start.7) | collective-permute-done | bytes 524320 | tf_op jit(solution)/shard_map/ppermute | solution.py:211
  54.8 6.2 %shard_map.112 = (bf16[4,2,256,256]{3,2,1,0:T(8,128)(2,1)S(1)}, bf16[4,2,256,256]{3,2,1,0:T(8,128)(2,1)S(1)}, bf16[2,2,256,256]{3,2,1,0:T(8,128)(2,1)S(1)}, bf16...) custom-call(s32[129]{0:T(256)S(1)} %pad_add_fusion.ids, ...), custom_call_target="tpu_custom_call" | custom-call | flops 1073741824 | bytes 16777216 | tf_op jit(solution)/shard_map/pallas_call | solution.py:183
  61.1 1.6 collective-permute-start.11
  62.7 1.1 collective-permute-start.12
  63.8 4.4 %collective-permute-start.13 = (bf16[2,2,256,256]{3,2,1,0:T(8,128)(2,1)S(1)}, bf16[2,2,256,256]{3,2,1,0:T(8,128)(2,1)S(1)}, u32[]{:S(2)}, u32[]{:S(2)}) collective-permute-start(bf16[2,2,256,256]{3,2,1,0:T(8,128)(2,1)S(1)} %get-tuple-element.62), channel_id=1, source_target_pairs={{0,4},{1,5},{2,6},{3,7},{4,0},{5,1},{6,2},{7,3},{8,12},{9,13},{10,... | collective-permute-start | bytes 1572872 | tf_op jit(solution)/shard_map/ppermute | solution.py:211
  68.4 10.2 %collective-permute-done.12 = bf16[2,2,256,256]{3,2,1,0:T(8,128)(2,1)S(1)} collective-permute-done((bf16[2,2,256,256]{3,2,1,0:T(8,128)(2,1)S(1)}, bf16[2,2,256,256]{3,2,1,0:T(8,128)(2,1)S(1)}, u32[]{:S(2)}, u32[]{:S(2)}) %collective-permute-start.12) | collective-permute-done | bytes 524320 | tf_op jit(solution)/shard_map/ppermute | solution.py:211
  78.6 12.3 %collective-permute-done.13 = bf16[2,2,256,256]{3,2,1,0:T(8,128)(2,1)S(1)} collective-permute-done((bf16[2,2,256,256]{3,2,1,0:T(8,128)(2,1)S(1)}, bf16[2,2,256,256]{3,2,1,0:T(8,128)(2,1)S(1)}, u32[]{:S(2)}, u32[]{:S(2)}) %collective-permute-start.13) | collective-permute-done | bytes 524320 | tf_op jit(solution)/shard_map/ppermute | solution.py:211
  92.1 1.1 collective-permute-start.15
  93.3 2.4 %collective-permute-start.16 = (bf16[2,256,256]{2,1,0:T(8,128)(2,1)S(1)}, bf16[2,256,256]{2,1,0:T(8,128)(2,1)S(1)}, u32[]{:S(2)}, u32[]{:S(2)}) collective-permute-start(bf16[2,256,256]{2,1,0:T(8,128)(2,1)S(1)} %get-tuple-element.66), channel_id=1, source_target_pairs={{0,4},{1,5},{2,6},{3,7},{4,0},{5,1},{6,2},{7,3},{8,12},{9,13},{10,... | collective-permute-start | bytes 786440 | tf_op jit(solution)/shard_map/ppermute | solution.py:211
  95.7 1.3 collective-permute-start.17
  97.0 1.7 collective-permute-done.18
  98.8 1.7 collective-permute-done.15
  100.5 6.7 %collective-permute-done.16 = bf16[2,256,256]{2,1,0:T(8,128)(2,1)S(1)} collective-permute-done((bf16[2,256,256]{2,1,0:T(8,128)(2,1)S(1)}, bf16[2,256,256]{2,1,0:T(8,128)(2,1)S(1)}, u32[]{:S(2)}, u32[]{:S(2)}) %collective-permute-start.16) | collective-permute-done | bytes 262176 | tf_op jit(solution)/shard_map/ppermute | solution.py:211
  107.5 1.5 collective-permute-done.19.other
  109.0 3.2 %shard_map.113 = (bf16[512,512]{1,0:T(8,128)(2,1)}, bf16[512,256]{1,0:T(8,128)(2,1)S(1)}, bf16[512,256]{1,0:T(8,128)(2,1)S(1)}, bf16[2,4,2,48,512]{4,3,2,1,0:T(8,128)(2,1)S(1)}) custom-call(bf16[512,256]{1,0:T(8,128)(2,1)S(1)} %get-tuple-element.121.mine, bf16[512,256]{1,0:T(8,128)(2,1)S(1)} %collective-permute-done.19.other, ...), custom_call_target="tpu_custom_call" | custom-call | flops 805306368 | bytes 8388608 | tf_op jit(solution)/shard_map/pallas_call | solution.py:183
  112.4 1.4 collective-permute-done.21
  113.8 1.5 collective-permute-start.24
  115.3 1.5 collective-permute-start.23
  116.8 1.7 collective-permute-start.25
  118.5 1.6 collective-permute-start.22
  120.2 5.8 %collective-permute-done.22 = bf16[2,256,256]{2,1,0:T(8,128)(2,1)S(1)} collective-permute-done((bf16[2,256,256]{2,1,0:T(8,128)(2,1)S(1)}, bf16[2,256,256]{2,1,0:T(8,128)(2,1)S(1)}, u32[]{:S(2)}, u32[]{:S(2)}) %collective-permute-start.22) | collective-permute-done | bytes 262176 | tf_op jit(solution)/shard_map/ppermute | solution.py:203
  126.0 0.8 pad_maximum_fusion.4.refs_0_
  126.9 2.5 %collective-permute-done.23 = bf16[2,256,256]{2,1,0:T(8,128)(2,1)S(1)} collective-permute-done((bf16[2,256,256]{2,1,0:T(8,128)(2,1)S(1)}, bf16[2,256,256]{2,1,0:T(8,128)(2,1)S(1)}, u32[]{:S(2)}, u32[]{:S(2)}) %collective-permute-start.23) | collective-permute-done | bytes 262176 | tf_op jit(solution)/shard_map/ppermute | solution.py:211
  129.5 1.6 collective-permute-start.29
  131.1 0.9 fusion
  132.0 3.5 %all-to-all-start = ((bf16[4,2,48,512]{3,2,1,0:T(8,128)(2,1)}), bf16[4,2,48,512]{3,2,1,0:T(8,128)(2,1)S(1)}, u32[]{:S(2)}, u32[]{:S(2)}) async-start(bf16[4,2,48,512]{3,2,1,0:T(8,128)(2,1)} %fusion), calls=%async_computation | async-start | bytes 786432 | tf_op jit(solution)/shard_map/all_to_all | solution.py:223
  135.5 2.1 collective-permute-start.28
  137.6 0.8 collective-permute-start.27
  138.5 5.1 %all-to-all-done = bf16[4,2,48,512]{3,2,1,0:T(8,128)(2,1)S(1)} async-done(((bf16[4,2,48,512]{3,2,1,0:T(8,128)(2,1)}), bf16[4,2,48,512]{3,2,1,0:T(8,128)(2,1)S(1)}, u32[]{:S(2)}, u32[]{:S(2)}) %all-to-all-start) | async-done | bytes 393248 | tf_op jit(solution)/shard_map/all_to_all | solution.py:223
  143.8 17.5 %all_to_all.20 = bf16[4,2,48,512]{3,2,1,0:T(8,128)(2,1)S(1)} all-to-all(bf16[4,2,48,512]{3,2,1,0:T(8,128)(2,1)S(1)} %broadcast_in_dim.17), channel_id=1, replica_groups={{0,1,64,65},{2,3,66,67},{4,5,68,69},{6,7,70,71},{8,9,72,73},{10,11,74,7..., dimensions={0} | all-to-all | bytes 786432 | tf_op jit(solution)/shard_map/all_to_all | solution.py:224
  161.4 2.5 %collective-permute-done.26.refs_1_ = bf16[2,2,256,256]{3,2,1,0:T(8,128)(2,1)} collective-permute-done((bf16[2,2,256,256]{3,2,1,0:T(8,128)(2,1)}, bf16[2,2,256,256]{3,2,1,0:T(8,128)(2,1)}, u32[]{:S(2)}, u32[]{:S(2)}) %collective-permute-start.26) | collective-permute-done | bytes 524320 | tf_op jit(solution)/shard_map/ppermute | solution.py:211
  163.9 2.9 %collective-permute-start.32 = (bf16[2,48,512]{2,1,0:T(8,128)(2,1)S(1)}, bf16[2,48,512]{2,1,0:T(8,128)(2,1)S(1)}, u32[]{:S(2)}, u32[]{:S(2)}) collective-permute-start(bf16[2,48,512]{2,1,0:T(8,128)(2,1)S(1)} %fusion.23), channel_id=1, source_target_pairs={{0,48},{8,56},{16,0},{24,8},{32,16},{40,24},{48,32},{56,40},{64,11... | collective-permute-start | bytes 294920 | tf_op jit(solution)/shard_map/ppermute | solution.py:211
  166.8 0.9 collective-permute-start.31
  167.6 0.9 collective-permute-start.30
  168.5 1.0 copy-done.3
  169.5 8.0 %shard_map.114 = (bf16[4,2,256,256]{3,2,1,0:T(8,128)(2,1)S(1)}, bf16[4,2,256,256]{3,2,1,0:T(8,128)(2,1)}, bf16[2,2,256,256]{3,2,1,0:T(8,128)(2,1)S(1)}, bf16[2,2...) custom-call(s32[129]{0:T(256)S(1)} %pad_add_fusion.ids, ...), custom_call_target="tpu_custom_call" | custom-call | flops 1073741824 | bytes 16777216 | tf_op jit(solution)/shard_map/pallas_call | solution.py:183
  177.6 1.0 copy-done.4
  178.6 3.0 %collective-permute-start.33 = (bf16[4,2,256,256]{3,2,1,0:T(8,128)(2,1)}, bf16[4,2,256,256]{3,2,1,0:T(8,128)(2,1)S(1)}, u32[]{:S(2)}, u32[]{:S(2)}) collective-permute-start(bf16[4,2,256,256]{3,2,1,0:T(8,128)(2,1)} %get-tuple-element.90), channel_id=1, source_target_pairs={{0,64},{1,65},{2,66},{3,67},{4,68},{5,69},{6,70},{7,71},{8,72},{9,... | collective-permute-start | bytes 3145736 | tf_op jit(solution)/shard_map/ppermute | solution.py:203
  181.6 2.5 %collective-permute-start.34 = (bf16[2,2,256,256]{3,2,1,0:T(8,128)(2,1)}, bf16[2,2,256,256]{3,2,1,0:T(8,128)(2,1)S(1)}, u32[]{:S(2)}, u32[]{:S(2)}) collective-permute-start(bf16[2,2,256,256]{3,2,1,0:T(8,128)(2,1)} %get-tuple-element.92), channel_id=1, source_target_pairs={{0,16},{8,24},{16,32},{24,40},{32,48},{40,56},{48,0},{56,8},{64,80... | collective-permute-start | bytes 1572872 | tf_op jit(solution)/shard_map/ppermute | solution.py:211
  184.7 2.1 collective-permute-start.36
  186.8 1.0 pad_maximum_fusion.2
  187.8 3.6 %all-to-all-start.2 = ((bf16[4,4,48,512]{3,2,1,0:T(8,128)(2,1)}), bf16[4,4,48,512]{3,2,1,0:T(8,128)(2,1)S(1)}, u32[]{:S(2)}, u32[]{:S(2)}) async-start(bf16[4,4,48,512]{3,2,1,0:T(8,128)(2,1)} %bitcast.47), calls=%async_computation.2 | async-start | bytes 1572864 | tf_op jit(solution)/shard_map/all_to_all | solution.py:261
  191.4 17.2 %collective-permute-done.34 = bf16[2,2,256,256]{3,2,1,0:T(8,128)(2,1)S(1)} collective-permute-done((bf16[2,2,256,256]{3,2,1,0:T(8,128)(2,1)}, bf16[2,2,256,256]{3,2,1,0:T(8,128)(2,1)S(1)}, u32[]{:S(2)}, u32[]{:S(2)}) %collective-permute-start.34) | collective-permute-done | bytes 524320 | tf_op jit(solution)/shard_map/ppermute | solution.py:211
  209.4 2.5 %fusion.12 = (bf16[2,256,256]{2,1,0:T(8,128)(2,1)}, bf16[2,256,256]{2,1,0:T(8,128)(2,1)S(1)}) fusion(bf16[2,2,256,256]{3,2,1,0:T(8,128)(2,1)} %collective-permute-done.36, bf16[2,2,256,256]{3,2,1,0:T(8,128)(2,1)} %collective-permute-done.35, bf16[2,2,256,256]{3,2,1,0:T(8,128)(2,1)} %copy-done.11, bf16[2,2,256,256]{3,2,1,0:T(8,128)(2,1)} %copy-done.6), kind=kLoop, calls=%fused_computation.45 | loop fusion | flops 2097152 | bytes 2621440 | tf_op jit(solution)/shard_map/add | solution.py:217
  211.9 1.0 fusion.10
  212.9 1.8 collective-permute-start.37
  214.7 2.2 collective-permute-start.38
  216.9 1.4 collective-permute-start.39
  218.5 1.0 broadcast_in_dim.19
  219.5 3.5 %all-to-all-start.3 = ((bf16[4,4,48,512]{3,2,1,0:T(8,128)(2,1)}), bf16[4,4,48,512]{3,2,1,0:T(8,128)(2,1)S(1)}, u32[]{:S(2)}, u32[]{:S(2)}) async-start(bf16[4,4,48,512]{3,2,1,0:T(8,128)(2,1)} %broadcast_in_dim.19), calls=%async_computation.3 | async-start | bytes 1572864 | tf_op jit(solution)/shard_map/all_to_all | solution.py:262
  223.0 6.0 %collective-permute-done.38 = bf16[2,256,256]{2,1,0:T(8,128)(2,1)S(1)} collective-permute-done((bf16[2,256,256]{2,1,0:T(8,128)(2,1)}, bf16[2,256,256]{2,1,0:T(8,128)(2,1)S(1)}, u32[]{:S(2)}, u32[]{:S(2)}) %collective-permute-start.38) | collective-permute-done | bytes 262176 | tf_op jit(solution)/shard_map/ppermute | solution.py:211
  229.3 5.1 %all-to-all-done.3.chunks = bf16[4,4,48,512]{3,2,1,0:T(8,128)(2,1)S(1)} async-done(((bf16[4,4,48,512]{3,2,1,0:T(8,128)(2,1)}), bf16[4,4,48,512]{3,2,1,0:T(8,128)(2,1)S(1)}, u32[]{:S(2)}, u32[]{:S(2)}) %all-to-all-start.3) | async-done | bytes 786464 | tf_op jit(solution)/shard_map/all_to_all | solution.py:262
  234.5 1.0 shard_map.116
  235.5 0.9 shard_map.115
  (89 shorter events, 7.0 us)
Async XLA Ops:
  0.6 54.2 %collective-permute-start.1 = (bf16[64,128,128]{2,1,0:T(8,128)(2,1)}, bf16[64,128,128]{2,1,0:T(8,128)(2,1)S(1)}, u32[]{:S(2)}, u32[]{:S(2)}) collective-permute-start(bf16[64,128,128]{2,1,0:T(8,128)(2,1)} %bitcast.73), channel_id=1, source_target_pairs={{0,8},{8,0},{16,24},{24,16},{32,40},{40,32},{48,56},{56,48},{64,72... | collective-permute-start | bytes 6291464 | tf_op jit(solution)/shard_map/ppermute | solution.py:198
  0.7 1.0 copy-start.7
  1.8 3.4 %collective-permute-start.2 = (bf16[512,256]{1,0:T(8,128)(2,1)S(1)}, bf16[512,256]{1,0:T(8,128)(2,1)S(1)}, u32[]{:S(2)}, u32[]{:S(2)}) collective-permute-start(bf16[512,256]{1,0:T(8,128)(2,1)S(1)} %get-tuple-element.55), channel_id=1, source_target_pairs={{0,8},{8,0},{16,24},{24,16},{32,40},{40,32},{48,56},{56,48},{64,72... | collective-permute-start | bytes 786440 | tf_op jit(solution)/shard_map/ppermute | solution.py:198
  5.2 20.0 %copy-start.12 = (s32[1,1,64]{2,1,0:T(1,128)S(1)}, s32[1,1,64]{2,1,0:T(1,128)}, u32[]{:S(2)}) copy-start(s32[1,1,64]{2,1,0:T(1,128)} %param.13) | copy-start | bytes 772
  5.2 20.0 %copy-start.13 = (s32[1,1,64]{2,1,0:T(1,128)S(1)}, s32[1,1,64]{2,1,0:T(1,128)}, u32[]{:S(2)}) copy-start(s32[1,1,64]{2,1,0:T(1,128)} %param.14) | copy-start | bytes 772
  5.2 49.5 %copy-start = (bf16[1,1,64,128,128]{4,3,2,1,0:T(8,128)(2,1)S(1)}, bf16[1,1,64,128,128]{4,3,2,1,0:T(8,128)(2,1)}, u32[]{:S(2)}) copy-start(bf16[1,1,64,128,128]{4,3,2,1,0:T(8,128)(2,1)} %param.12) | copy-start | bytes 6291460
  5.3 10.0 %collective-permute-start.3 = (bf16[2,256,256]{2,1,0:T(8,128)(2,1)S(1)}, bf16[2,256,256]{2,1,0:T(8,128)(2,1)S(1)}, u32[]{:S(2)}, u32[]{:S(2)}) collective-permute-start(bf16[2,256,256]{2,1,0:T(8,128)(2,1)S(1)} %get-tuple-element.123), channel_id=1, source_target_pairs={{0,64},{1,65},{2,66},{3,67},{4,68},{5,69},{6,70},{7,71},{8,72},{9,... | collective-permute-start | bytes 786440 | tf_op jit(solution)/shard_map/ppermute | solution.py:203
  8.7 10.7 %collective-permute-start.5 = (bf16[2,256,256]{2,1,0:T(8,128)(2,1)S(1)}, bf16[2,256,256]{2,1,0:T(8,128)(2,1)S(1)}, u32[]{:S(2)}, u32[]{:S(2)}) collective-permute-start(bf16[2,256,256]{2,1,0:T(8,128)(2,1)S(1)} %get-tuple-element.122), channel_id=1, source_target_pairs={{0,32},{8,40},{16,48},{24,56},{32,0},{40,8},{48,16},{56,24},{64,96... | collective-permute-start | bytes 786440 | tf_op jit(solution)/shard_map/ppermute | solution.py:211
  11.7 12.2 %collective-permute-start.4 = (bf16[2,256,256]{2,1,0:T(8,128)(2,1)S(1)}, bf16[2,256,256]{2,1,0:T(8,128)(2,1)S(1)}, u32[]{:S(2)}, u32[]{:S(2)}) collective-permute-start(bf16[2,256,256]{2,1,0:T(8,128)(2,1)S(1)} %get-tuple-element.122), channel_id=1, source_target_pairs={{0,16},{8,24},{16,32},{24,40},{32,48},{40,56},{48,0},{56,8},{64,80... | collective-permute-start | bytes 786440 | tf_op jit(solution)/shard_map/ppermute | solution.py:211
  12.3 11.7 %collective-permute-start.6 = (bf16[2,256,256]{2,1,0:T(8,128)(2,1)S(1)}, bf16[2,256,256]{2,1,0:T(8,128)(2,1)S(1)}, u32[]{:S(2)}, u32[]{:S(2)}) collective-permute-start(bf16[2,256,256]{2,1,0:T(8,128)(2,1)S(1)} %get-tuple-element.122), channel_id=1, source_target_pairs={{0,48},{8,56},{16,0},{24,8},{32,16},{40,24},{48,32},{56,40},{64,11... | collective-permute-start | bytes 786440 | tf_op jit(solution)/shard_map/ppermute | solution.py:211
  24.1 30.7 %collective-permute-start.10 = (bf16[4,2,256,256]{3,2,1,0:T(8,128)(2,1)S(1)}, bf16[4,2,256,256]{3,2,1,0:T(8,128)(2,1)S(1)}, u32[]{:S(2)}, u32[]{:S(2)}) collective-permute-start(bf16[4,2,256,256]{3,2,1,0:T(8,128)(2,1)S(1)} %pad_maximum_fusion.refs_4_), channel_id=1, source_target_pairs={{0,64},{1,65},{2,66},{3,67},{4,68},{5,69},{6,70},{7,71},{8,72},{9,... | collective-permute-start | bytes 3145736 | tf_op jit(solution)/shard_map/ppermute | solution.py:203
  25.3 3.6 %collective-permute-start = (s32[129]{0:T(256)S(1)}, s32[129]{0:T(256)S(1)}, u32[]{:S(2)}, u32[]{:S(2)}) collective-permute-start(s32[129]{0:T(256)S(1)} %pad_add_fusion.ids), channel_id=1, source_target_pairs={{0,8},{8,0},{16,24},{24,16},{32,40},{40,32},{48,56},{56,48},{64,72... | collective-permute-start | bytes 1556 | tf_op jit(solution)/shard_map/ppermute | solution.py:198
  25.3 25.8 %collective-permute-start.9 = (bf16[2,2,256,256]{3,2,1,0:T(8,128)(2,1)S(1)}, bf16[2,2,256,256]{3,2,1,0:T(8,128)(2,1)S(1)}, u32[]{:S(2)}, u32[]{:S(2)}) collective-permute-start(bf16[2,2,256,256]{3,2,1,0:T(8,128)(2,1)S(1)} %pad_maximum_fusion.3.refs_0_), channel_id=1, source_target_pairs={{0,48},{8,56},{16,0},{24,8},{32,16},{40,24},{48,32},{56,40},{64,11... | collective-permute-start | bytes 1572872 | tf_op jit(solution)/shard_map/ppermute | solution.py:211
  28.0 23.1 %collective-permute-start.8 = (bf16[2,2,256,256]{3,2,1,0:T(8,128)(2,1)S(1)}, bf16[2,2,256,256]{3,2,1,0:T(8,128)(2,1)S(1)}, u32[]{:S(2)}, u32[]{:S(2)}) collective-permute-start(bf16[2,2,256,256]{3,2,1,0:T(8,128)(2,1)S(1)} %pad_maximum_fusion.3.refs_0_), channel_id=1, source_target_pairs={{0,32},{8,40},{16,48},{24,56},{32,0},{40,8},{48,16},{56,24},{64,96... | collective-permute-start | bytes 1572872 | tf_op jit(solution)/shard_map/ppermute | solution.py:211
  28.9 25.8 %collective-permute-start.7 = (bf16[2,2,256,256]{3,2,1,0:T(8,128)(2,1)S(1)}, bf16[2,2,256,256]{3,2,1,0:T(8,128)(2,1)S(1)}, u32[]{:S(2)}, u32[]{:S(2)}) collective-permute-start(bf16[2,2,256,256]{3,2,1,0:T(8,128)(2,1)S(1)} %pad_maximum_fusion.3.refs_0_), channel_id=1, source_target_pairs={{0,16},{8,24},{16,32},{24,40},{32,48},{40,56},{48,0},{56,8},{64,80... | collective-permute-start | bytes 1572872 | tf_op jit(solution)/shard_map/ppermute | solution.py:211
  54.8 6.3 %copy-start.1 = (bf16[64,128,128]{2,1,0:T(8,128)(2,1)}, bf16[64,128,128]{2,1,0:T(8,128)(2,1)S(1)}, u32[]{:S(2)}) copy-start(bf16[64,128,128]{2,1,0:T(8,128)(2,1)S(1)} %collective-permute-done.1.other_tiles) | copy-start | bytes 6291460
  61.1 30.2 %collective-permute-start.11 = (bf16[4,2,256,256]{3,2,1,0:T(8,128)(2,1)S(1)}, bf16[4,2,256,256]{3,2,1,0:T(8,128)(2,1)S(1)}, u32[]{:S(2)}, u32[]{:S(2)}) collective-permute-start(bf16[4,2,256,256]{3,2,1,0:T(8,128)(2,1)S(1)} %get-tuple-element.59), channel_id=1, source_target_pairs={{0,1},{1,0},{2,3},{3,2},{4,5},{5,4},{6,7},{7,6},{8,9},{9,8},{10,11... | collective-permute-start | bytes 3145736 | tf_op jit(solution)/shard_map/ppermute | solution.py:203
  62.7 15.9 %collective-permute-start.12 = (bf16[2,2,256,256]{3,2,1,0:T(8,128)(2,1)S(1)}, bf16[2,2,256,256]{3,2,1,0:T(8,128)(2,1)S(1)}, u32[]{:S(2)}, u32[]{:S(2)}) collective-permute-start(bf16[2,2,256,256]{3,2,1,0:T(8,128)(2,1)S(1)} %get-tuple-element.61), channel_id=1, source_target_pairs={{0,2},{1,3},{2,4},{3,5},{4,6},{5,7},{6,0},{7,1},{8,10},{9,11},{10,... | collective-permute-start | bytes 1572872 | tf_op jit(solution)/shard_map/ppermute | solution.py:211
  63.8 27.2 %collective-permute-start.13 = (bf16[2,2,256,256]{3,2,1,0:T(8,128)(2,1)S(1)}, bf16[2,2,256,256]{3,2,1,0:T(8,128)(2,1)S(1)}, u32[]{:S(2)}, u32[]{:S(2)}) collective-permute-start(bf16[2,2,256,256]{3,2,1,0:T(8,128)(2,1)S(1)} %get-tuple-element.62), channel_id=1, source_target_pairs={{0,4},{1,5},{2,6},{3,7},{4,0},{5,1},{6,2},{7,3},{8,12},{9,13},{10,... | collective-permute-start | bytes 1572872 | tf_op jit(solution)/shard_map/ppermute | solution.py:211
  68.2 22.8 %collective-permute-start.14 = (bf16[2,2,256,256]{3,2,1,0:T(8,128)(2,1)S(1)}, bf16[2,2,256,256]{3,2,1,0:T(8,128)(2,1)S(1)}, u32[]{:S(2)}, u32[]{:S(2)}) collective-permute-start(bf16[2,2,256,256]{3,2,1,0:T(8,128)(2,1)S(1)} %get-tuple-element.63), channel_id=1, source_target_pairs={{0,6},{1,7},{2,0},{3,1},{4,2},{5,3},{6,4},{7,5},{8,14},{9,15},{10,... | collective-permute-start | bytes 1572872 | tf_op jit(solution)/shard_map/ppermute | solution.py:211
  91.5 17.5 %copy-start.8 = (bf16[512,512]{1,0:T(8,128)(2,1)S(1)}, bf16[512,512]{1,0:T(8,128)(2,1)}, u32[]{:S(2)}) copy-start(bf16[512,512]{1,0:T(8,128)(2,1)} %weight.1) | copy-start | bytes 1572868
  91.5 17.5 %copy-start.9 = (bf16[512,512]{1,0:T(8,128)(2,1)S(1)}, bf16[512,512]{1,0:T(8,128)(2,1)}, u32[]{:S(2)}) copy-start(bf16[512,512]{1,0:T(8,128)(2,1)} %cotangent.1) | copy-start | bytes 1572868
  91.5 17.5 %copy-start.10 = (f32[512]{0:T(512)S(1)}, f32[512]{0:T(512)}, u32[]{:S(2)}) copy-start(f32[512]{0:T(512)} %param.10) | copy-start | bytes 6148
  91.6 7.1 %collective-permute-start.18 = (bf16[2,256,256]{2,1,0:T(8,128)(2,1)S(1)}, bf16[2,256,256]{2,1,0:T(8,128)(2,1)S(1)}, u32[]{:S(2)}, u32[]{:S(2)}) collective-permute-start(bf16[2,256,256]{2,1,0:T(8,128)(2,1)S(1)} %get-tuple-element.69), channel_id=1, source_target_pairs={{0,1},{1,0},{2,3},{3,2},{4,5},{5,4},{6,7},{7,6},{8,9},{9,8},{10,11... | collective-permute-start | bytes 786440 | tf_op jit(solution)/shard_map/ppermute | solution.py:203
  92.1 8.3 %collective-permute-start.15 = (bf16[2,256,256]{2,1,0:T(8,128)(2,1)S(1)}, bf16[2,256,256]{2,1,0:T(8,128)(2,1)S(1)}, u32[]{:S(2)}, u32[]{:S(2)}) collective-permute-start(bf16[2,256,256]{2,1,0:T(8,128)(2,1)S(1)} %get-tuple-element.65), channel_id=1, source_target_pairs={{0,2},{1,3},{2,4},{3,5},{4,6},{5,7},{6,0},{7,1},{8,10},{9,11},{10,... | collective-permute-start | bytes 786440 | tf_op jit(solution)/shard_map/ppermute | solution.py:211
  93.3 13.9 %collective-permute-start.16 = (bf16[2,256,256]{2,1,0:T(8,128)(2,1)S(1)}, bf16[2,256,256]{2,1,0:T(8,128)(2,1)S(1)}, u32[]{:S(2)}, u32[]{:S(2)}) collective-permute-start(bf16[2,256,256]{2,1,0:T(8,128)(2,1)S(1)} %get-tuple-element.66), channel_id=1, source_target_pairs={{0,4},{1,5},{2,6},{3,7},{4,0},{5,1},{6,2},{7,3},{8,12},{9,13},{10,... | collective-permute-start | bytes 786440 | tf_op jit(solution)/shard_map/ppermute | solution.py:211
  95.7 11.5 %collective-permute-start.17 = (bf16[2,256,256]{2,1,0:T(8,128)(2,1)S(1)}, bf16[2,256,256]{2,1,0:T(8,128)(2,1)S(1)}, u32[]{:S(2)}, u32[]{:S(2)}) collective-permute-start(bf16[2,256,256]{2,1,0:T(8,128)(2,1)S(1)} %get-tuple-element.67), channel_id=1, source_target_pairs={{0,6},{1,7},{2,0},{3,1},{4,2},{5,3},{6,4},{7,5},{8,14},{9,15},{10,... | collective-permute-start | bytes 786440 | tf_op jit(solution)/shard_map/ppermute | solution.py:211
  107.4 1.6 collective-permute-start.19
  112.2 1.5 collective-permute-start.21
  113.8 13.1 %collective-permute-start.24 = (bf16[2,256,256]{2,1,0:T(8,128)(2,1)S(1)}, bf16[2,256,256]{2,1,0:T(8,128)(2,1)S(1)}, u32[]{:S(2)}, u32[]{:S(2)}) collective-permute-start(bf16[2,256,256]{2,1,0:T(8,128)(2,1)S(1)} %get-tuple-element.118), channel_id=1, source_target_pairs={{0,4},{1,5},{2,6},{3,7},{4,0},{5,1},{6,2},{7,3},{8,12},{9,13},{10,... | collective-permute-start | bytes 786440 | tf_op jit(solution)/shard_map/ppermute | solution.py:211
  115.3 14.1 %collective-permute-start.23 = (bf16[2,256,256]{2,1,0:T(8,128)(2,1)S(1)}, bf16[2,256,256]{2,1,0:T(8,128)(2,1)S(1)}, u32[]{:S(2)}, u32[]{:S(2)}) collective-permute-start(bf16[2,256,256]{2,1,0:T(8,128)(2,1)S(1)} %get-tuple-element.118), channel_id=1, source_target_pairs={{0,2},{1,3},{2,4},{3,5},{4,6},{5,7},{6,0},{7,1},{8,10},{9,11},{10,... | collective-permute-start | bytes 786440 | tf_op jit(solution)/shard_map/ppermute | solution.py:211
  116.8 12.5 %collective-permute-start.25 = (bf16[2,256,256]{2,1,0:T(8,128)(2,1)S(1)}, bf16[2,256,256]{2,1,0:T(8,128)(2,1)S(1)}, u32[]{:S(2)}, u32[]{:S(2)}) collective-permute-start(bf16[2,256,256]{2,1,0:T(8,128)(2,1)S(1)} %get-tuple-element.118), channel_id=1, source_target_pairs={{0,6},{1,7},{2,0},{3,1},{4,2},{5,3},{6,4},{7,5},{8,14},{9,15},{10,... | collective-permute-start | bytes 786440 | tf_op jit(solution)/shard_map/ppermute | solution.py:211
  118.5 7.5 %collective-permute-start.22 = (bf16[2,256,256]{2,1,0:T(8,128)(2,1)S(1)}, bf16[2,256,256]{2,1,0:T(8,128)(2,1)S(1)}, u32[]{:S(2)}, u32[]{:S(2)}) collective-permute-start(bf16[2,256,256]{2,1,0:T(8,128)(2,1)S(1)} %get-tuple-element.119), channel_id=1, source_target_pairs={{0,1},{1,0},{2,3},{3,2},{4,5},{5,4},{6,7},{7,6},{8,9},{9,8},{10,11... | collective-permute-start | bytes 786440 | tf_op jit(solution)/shard_map/ppermute | solution.py:203
  120.1 11.0 %collective-permute-start.20 = (bf16[4,2,48,512]{3,2,1,0:T(8,128)(2,1)S(1)}, bf16[4,2,48,512]{3,2,1,0:T(8,128)(2,1)S(1)}, u32[]{:S(2)}, u32[]{:S(2)}) collective-permute-start(bf16[4,2,48,512]{3,2,1,0:T(8,128)(2,1)S(1)} %slice_bitcast_fusion), channel_id=1, source_target_pairs={{0,8},{8,0},{16,24},{24,16},{32,40},{40,32},{48,56},{56,48},{64,72... | collective-permute-start | bytes 1179656 | tf_op jit(solution)/shard_map/ppermute | solution.py:198
  129.5 34.4 %collective-permute-start.29 = (bf16[4,2,256,256]{3,2,1,0:T(8,128)(2,1)S(1)}, bf16[4,2,256,256]{3,2,1,0:T(8,128)(2,1)}, u32[]{:S(2)}, u32[]{:S(2)}) collective-permute-start(bf16[4,2,256,256]{3,2,1,0:T(8,128)(2,1)S(1)} %pad_maximum_fusion.1.refs_4_), channel_id=1, source_target_pairs={{0,1},{1,0},{2,3},{3,2},{4,5},{5,4},{6,7},{7,6},{8,9},{9,8},{10,11... | collective-permute-start | bytes 3145736 | tf_op jit(solution)/shard_map/ppermute | solution.py:203
  132.0 11.7 %all-to-all-start = ((bf16[4,2,48,512]{3,2,1,0:T(8,128)(2,1)}), bf16[4,2,48,512]{3,2,1,0:T(8,128)(2,1)S(1)}, u32[]{:S(2)}, u32[]{:S(2)}) async-start(bf16[4,2,48,512]{3,2,1,0:T(8,128)(2,1)} %fusion), calls=%async_computation | async-start | bytes 786432 | tf_op jit(solution)/shard_map/all_to_all | solution.py:223
  135.5 25.9 %collective-permute-start.28 = (bf16[2,2,256,256]{3,2,1,0:T(8,128)(2,1)}, bf16[2,2,256,256]{3,2,1,0:T(8,128)(2,1)}, u32[]{:S(2)}, u32[]{:S(2)}) collective-permute-start(bf16[2,2,256,256]{3,2,1,0:T(8,128)(2,1)} %pad_maximum_fusion.4.refs_0_), channel_id=1, source_target_pairs={{0,6},{1,7},{2,0},{3,1},{4,2},{5,3},{6,4},{7,5},{8,14},{9,15},{10,... | collective-permute-start | bytes 1572872 | tf_op jit(solution)/shard_map/ppermute | solution.py:211
  137.6 23.8 %collective-permute-start.27 = (bf16[2,2,256,256]{3,2,1,0:T(8,128)(2,1)}, bf16[2,2,256,256]{3,2,1,0:T(8,128)(2,1)}, u32[]{:S(2)}, u32[]{:S(2)}) collective-permute-start(bf16[2,2,256,256]{3,2,1,0:T(8,128)(2,1)} %pad_maximum_fusion.4.refs_0_), channel_id=1, source_target_pairs={{0,4},{1,5},{2,6},{3,7},{4,0},{5,1},{6,2},{7,3},{8,12},{9,13},{10,... | collective-permute-start | bytes 1572872 | tf_op jit(solution)/shard_map/ppermute | solution.py:211
  138.4 25.6 %collective-permute-start.26 = (bf16[2,2,256,256]{3,2,1,0:T(8,128)(2,1)}, bf16[2,2,256,256]{3,2,1,0:T(8,128)(2,1)}, u32[]{:S(2)}, u32[]{:S(2)}) collective-permute-start(bf16[2,2,256,256]{3,2,1,0:T(8,128)(2,1)} %pad_maximum_fusion.4.refs_0_), channel_id=1, source_target_pairs={{0,2},{1,3},{2,4},{3,5},{4,6},{5,7},{6,0},{7,1},{8,10},{9,11},{10,... | collective-permute-start | bytes 1572872 | tf_op jit(solution)/shard_map/ppermute | solution.py:211
  143.7 24.8 %copy-start.2 = (bf16[64,128,128]{2,1,0:T(8,128)(2,1)S(1)}, bf16[64,128,128]{2,1,0:T(8,128)(2,1)}, u32[]{:S(2)}) copy-start(bf16[64,128,128]{2,1,0:T(8,128)(2,1)} %copy-done.1) | copy-start | bytes 6291460
  163.9 14.6 %collective-permute-start.32 = (bf16[2,48,512]{2,1,0:T(8,128)(2,1)S(1)}, bf16[2,48,512]{2,1,0:T(8,128)(2,1)S(1)}, u32[]{:S(2)}, u32[]{:S(2)}) collective-permute-start(bf16[2,48,512]{2,1,0:T(8,128)(2,1)S(1)} %fusion.23), channel_id=1, source_target_pairs={{0,48},{8,56},{16,0},{24,8},{32,16},{40,24},{48,32},{56,40},{64,11... | collective-permute-start | bytes 294920 | tf_op jit(solution)/shard_map/ppermute | solution.py:211
  166.8 11.8 %collective-permute-start.31 = (bf16[2,48,512]{2,1,0:T(8,128)(2,1)S(1)}, bf16[2,48,512]{2,1,0:T(8,128)(2,1)S(1)}, u32[]{:S(2)}, u32[]{:S(2)}) collective-permute-start(bf16[2,48,512]{2,1,0:T(8,128)(2,1)S(1)} %fusion.23), channel_id=1, source_target_pairs={{0,32},{8,40},{16,48},{24,56},{32,0},{40,8},{48,16},{56,24},{64,96... | collective-permute-start | bytes 294920 | tf_op jit(solution)/shard_map/ppermute | solution.py:211
  167.6 10.9 %collective-permute-start.30 = (bf16[2,48,512]{2,1,0:T(8,128)(2,1)S(1)}, bf16[2,48,512]{2,1,0:T(8,128)(2,1)S(1)}, u32[]{:S(2)}, u32[]{:S(2)}) collective-permute-start(bf16[2,48,512]{2,1,0:T(8,128)(2,1)S(1)} %fusion.23), channel_id=1, source_target_pairs={{0,16},{8,24},{16,32},{24,40},{32,48},{40,56},{48,0},{56,8},{64,80... | collective-permute-start | bytes 294920 | tf_op jit(solution)/shard_map/ppermute | solution.py:211
  168.5 1.0 copy-start.3
  177.6 1.0 copy-start.4
  178.6 9.2 %copy-start.6 = (bf16[2,2,256,256]{3,2,1,0:T(8,128)(2,1)}, bf16[2,2,256,256]{3,2,1,0:T(8,128)(2,1)S(1)}, u32[]{:S(2)}) copy-start(bf16[2,2,256,256]{3,2,1,0:T(8,128)(2,1)S(1)} %get-tuple-element.91) | copy-start | bytes 1572868
  178.6 33.2 %collective-permute-start.33 = (bf16[4,2,256,256]{3,2,1,0:T(8,128)(2,1)}, bf16[4,2,256,256]{3,2,1,0:T(8,128)(2,1)S(1)}, u32[]{:S(2)}, u32[]{:S(2)}) collective-permute-start(bf16[4,2,256,256]{3,2,1,0:T(8,128)(2,1)} %get-tuple-element.90), channel_id=1, source_target_pairs={{0,64},{1,65},{2,66},{3,67},{4,68},{5,69},{6,70},{7,71},{8,72},{9,... | collective-permute-start | bytes 3145736 | tf_op jit(solution)/shard_map/ppermute | solution.py:203
  181.6 5.2 %collective-permute-start.42 = (bf16[4,2,48,512]{3,2,1,0:T(8,128)(2,1)S(1)}, bf16[4,2,48,512]{3,2,1,0:T(8,128)(2,1)S(1)}, u32[]{:S(2)}, u32[]{:S(2)}) collective-permute-start(bf16[4,2,48,512]{3,2,1,0:T(8,128)(2,1)S(1)} %pad_maximum_fusion.5), channel_id=1, source_target_pairs={{0,8},{8,0},{16,24},{24,16},{32,40},{40,32},{48,56},{56,48},{64,72... | collective-permute-start | bytes 1179656 | tf_op jit(solution)/shard_map/ppermute | solution.py:198
  181.6 27.0 %collective-permute-start.34 = (bf16[2,2,256,256]{3,2,1,0:T(8,128)(2,1)}, bf16[2,2,256,256]{3,2,1,0:T(8,128)(2,1)S(1)}, u32[]{:S(2)}, u32[]{:S(2)}) collective-permute-start(bf16[2,2,256,256]{3,2,1,0:T(8,128)(2,1)} %get-tuple-element.92), channel_id=1, source_target_pairs={{0,16},{8,24},{16,32},{24,40},{32,48},{40,56},{48,0},{56,8},{64,80... | collective-permute-start | bytes 1572872 | tf_op jit(solution)/shard_map/ppermute | solution.py:211
  184.1 24.5 %collective-permute-start.35 = (bf16[2,2,256,256]{3,2,1,0:T(8,128)(2,1)}, bf16[2,2,256,256]{3,2,1,0:T(8,128)(2,1)}, u32[]{:S(2)}, u32[]{:S(2)}) collective-permute-start(bf16[2,2,256,256]{3,2,1,0:T(8,128)(2,1)} %get-tuple-element.93), channel_id=1, source_target_pairs={{0,32},{8,40},{16,48},{24,56},{32,0},{40,8},{48,16},{56,24},{64,96... | collective-permute-start | bytes 1572872 | tf_op jit(solution)/shard_map/ppermute | solution.py:211
  184.7 24.7 %collective-permute-start.36 = (bf16[2,2,256,256]{3,2,1,0:T(8,128)(2,1)}, bf16[2,2,256,256]{3,2,1,0:T(8,128)(2,1)}, u32[]{:S(2)}, u32[]{:S(2)}) collective-permute-start(bf16[2,2,256,256]{3,2,1,0:T(8,128)(2,1)} %get-tuple-element.94), channel_id=1, source_target_pairs={{0,48},{8,56},{16,0},{24,8},{32,16},{40,24},{48,32},{56,40},{64,11... | collective-permute-start | bytes 1572872 | tf_op jit(solution)/shard_map/ppermute | solution.py:211
  187.8 24.1 %copy-start.5 = (bf16[4,2,256,256]{3,2,1,0:T(8,128)(2,1)S(1)}, bf16[4,2,256,256]{3,2,1,0:T(8,128)(2,1)}, u32[]{:S(2)}) copy-start(bf16[4,2,256,256]{3,2,1,0:T(8,128)(2,1)} %copy-done.4) | copy-start | bytes 3145732
  187.8 30.6 %all-to-all-start.2 = ((bf16[4,4,48,512]{3,2,1,0:T(8,128)(2,1)}), bf16[4,4,48,512]{3,2,1,0:T(8,128)(2,1)S(1)}, u32[]{:S(2)}, u32[]{:S(2)}) async-start(bf16[4,4,48,512]{3,2,1,0:T(8,128)(2,1)} %bitcast.47), calls=%async_computation.2 | async-start | bytes 1572864 | tf_op jit(solution)/shard_map/all_to_all | solution.py:261
  208.6 0.8 copy-start.11
  212.9 10.1 %collective-permute-start.37 = (bf16[2,256,256]{2,1,0:T(8,128)(2,1)}, bf16[2,256,256]{2,1,0:T(8,128)(2,1)S(1)}, u32[]{:S(2)}, u32[]{:S(2)}) collective-permute-start(bf16[2,256,256]{2,1,0:T(8,128)(2,1)} %get-tuple-element.96), channel_id=1, source_target_pairs={{0,16},{8,24},{16,32},{24,40},{32,48},{40,56},{48,0},{56,8},{64,80... | collective-permute-start | bytes 786440 | tf_op jit(solution)/shard_map/ppermute | solution.py:211
  214.7 14.3 %collective-permute-start.38 = (bf16[2,256,256]{2,1,0:T(8,128)(2,1)}, bf16[2,256,256]{2,1,0:T(8,128)(2,1)S(1)}, u32[]{:S(2)}, u32[]{:S(2)}) collective-permute-start(bf16[2,256,256]{2,1,0:T(8,128)(2,1)} %get-tuple-element.97), channel_id=1, source_target_pairs={{0,32},{8,40},{16,48},{24,56},{32,0},{40,8},{48,16},{56,24},{64,96... | collective-permute-start | bytes 786440 | tf_op jit(solution)/shard_map/ppermute | solution.py:211
  216.9 12.1 %collective-permute-start.39 = (bf16[2,256,256]{2,1,0:T(8,128)(2,1)}, bf16[2,256,256]{2,1,0:T(8,128)(2,1)S(1)}, u32[]{:S(2)}, u32[]{:S(2)}) collective-permute-start(bf16[2,256,256]{2,1,0:T(8,128)(2,1)} %get-tuple-element.98), channel_id=1, source_target_pairs={{0,48},{8,56},{16,0},{24,8},{32,16},{40,24},{48,32},{56,40},{64,11... | collective-permute-start | bytes 786440 | tf_op jit(solution)/shard_map/ppermute | solution.py:211
  218.3 10.8 %collective-permute-start.40 = (bf16[2,256,256]{2,1,0:T(8,128)(2,1)}, bf16[2,256,256]{2,1,0:T(8,128)(2,1)S(1)}, u32[]{:S(2)}, u32[]{:S(2)}) collective-permute-start(bf16[2,256,256]{2,1,0:T(8,128)(2,1)} %get-tuple-element.100), channel_id=1, source_target_pairs={{0,64},{1,65},{2,66},{3,67},{4,68},{5,69},{6,70},{7,71},{8,72},{9,... | collective-permute-start | bytes 786440 | tf_op jit(solution)/shard_map/ppermute | solution.py:203
  219.5 15.0 %all-to-all-start.3 = ((bf16[4,4,48,512]{3,2,1,0:T(8,128)(2,1)}), bf16[4,4,48,512]{3,2,1,0:T(8,128)(2,1)S(1)}, u32[]{:S(2)}, u32[]{:S(2)}) async-start(bf16[4,4,48,512]{3,2,1,0:T(8,128)(2,1)} %broadcast_in_dim.19), calls=%async_computation.3 | async-start | bytes 1572864 | tf_op jit(solution)/shard_map/all_to_all | solution.py:262
  229.2 6.3 %collective-permute-start.41 = (bf16[512,256]{1,0:T(8,128)(2,1)S(1)}, bf16[512,256]{1,0:T(8,128)(2,1)S(1)}, u32[]{:S(2)}, u32[]{:S(2)}) collective-permute-start(bf16[512,256]{1,0:T(8,128)(2,1)S(1)} %get-tuple-element.116), channel_id=1, source_target_pairs={{0,8},{8,0},{16,24},{24,16},{32,40},{40,32},{48,56},{56,48},{64,72... | collective-permute-start | bytes 786440 | tf_op jit(solution)/shard_map/ppermute | solution.py:198

commit v5 on v4

--- a/solution.py
+++ b/solution.py
@@ -10,8 +10,8 @@
 
 BF = jnp.bfloat16
 F32 = jnp.float32
-VMEM_LIMIT = 26 * 2**20
 UNROLL = 16
+TILES_VMEM = 18 * 2**20
 HALF = 256
 FIRST = 256
 SHARE = 32
@@ -59,13 +59,6 @@
     first, second = features[:, :HALF], features[:, HALF:]
     mine[...] = jnp.where(left, first, second)
     other[...] = jnp.where(left, second, first)
-
-
-def route_loads(pieces, source):
-    own, ring_1, ring_2, ring_3, near, far = pieces
-    low, high = pl.ds(0, FIRST), pl.ds(FIRST, 512 - FIRST)
-    loads = [(piece, source.at[d, :, :, low]) for d, piece in enumerate((own, ring_1, ring_2, ring_3))]
-    return loads + [(near, source.at[:, 0, :, high]), (far, source.at[:, 1, :, high])]
 
 
 def store_parts(acc, outs):
@@ -101,8 +94,8 @@
 
 
 def tiles_kernel(transposed, ids, other_ids, tiles, other_tiles, *refs):
-    pieces, outs, (source, vals, acc, sems) = refs[:6], refs[6:12], refs[12:]
-    start_loads([(tiles, vals.at[0]), (other_tiles, vals.at[1]), *route_loads(pieces, source)], acc, sems)
+    source, outs, (vals, acc, sems) = refs[0], refs[1:7], refs[7:]
+    start_loads([(tiles, vals.at[0]), (other_tiles, vals.at[1])], acc, sems)
     for side, table in enumerate((ids, other_ids)):
 
         @functools.partial(tile_loop, table[128], acc)
@@ -119,31 +112,33 @@
     store_parts(acc, outs)
 
 
-def dense_kernel(
-    scale, mine, other, weight, bias, cotangent, output, grad_mine, grad_other, chunks, agg, grad_pre, product
-):
+def dense_kernel(start, mine, other, weight, bias, cotangent, output, grad_mine, grad_other, agg, grad_pre):
+    left = lax.rem(lax.axis_index("row"), 2) == 0
     size = 128
-    core = lax.rem(lax.axis_index("row"), 2)
-    left = core == 0
-
-    def body(i, bias_sum):
-        at = pl.ds(pl.multiple_of(i * size, size), size)
+    for i in range(mine.shape[0] // size):
+        at = slice(i * size, (i + 1) * size)
         a, b = mine[at, :], other[at, :]
         agg[at, :HALF] = jnp.where(left, a, b)
         agg[at, HALF:] = jnp.where(left, b, a)
         pre = jnp.dot(agg[at, :], weight[...], preferred_element_type=F32) + bias[...]
         s = jax.nn.sigmoid(pre)
         output[at, :] = (pre * s).astype(BF)
-        grad = (cotangent[at, :].astype(F32) * s * (1.0 + pre * (1.0 - s))).astype(BF)
+        given = cotangent[start + i * size : start + (i + 1) * size, :].astype(F32)
+        grad = (given * s * (1.0 + pre * (1.0 - s))).astype(BF)
         grad_pre[at, :] = grad
         back = lax.dot_general(grad, weight[...], (((1,), (1,)), ((), ())), preferred_element_type=F32).astype(BF)
         grad_mine[at, :] = jnp.where(left, back[:, :HALF], back[:, HALF:])
         grad_other[at, :] = jnp.where(left, back[:, HALF:], back[:, :HALF])
-        return bias_sum + jnp.sum(grad.astype(F32), axis=0, keepdims=True)
-
-    bias_sum = lax.fori_loop(0, agg.shape[0] // size, body, jnp.zeros((1, agg.shape[1]), F32)) * scale
-    product[...] = lax.dot_general(agg[...], grad_pre[...], (((0,), (0,)), ((), ())), preferred_element_type=F32)
-    tail = jnp.broadcast_to(bias_sum, (TAIL, agg.shape[1])).astype(BF)
+
+
+def weight_kernel(scale, agg_1, agg_2, grad_1, grad_2, chunks, product):
+    core = lax.rem(lax.axis_index("row"), 2)
+    both = (((0,), (0,)), ((), ()))
+    product[...] = lax.dot_general(agg_1[...], grad_1[...], both, preferred_element_type=F32)
+    product[...] += lax.dot_general(agg_2[...], grad_2[...], both, preferred_element_type=F32)
+    bias_sum = jnp.sum(grad_1[...].astype(F32), axis=0, keepdims=True)
+    bias_sum = (bias_sum + jnp.sum(grad_2[...].astype(F32), axis=0, keepdims=True)) * scale
+    tail = jnp.broadcast_to(bias_sum, (TAIL, bias_sum.shape[1])).astype(BF)
     for far in range(2):
         for x in range(4):
             for y in range(2):
@@ -163,11 +158,12 @@
     bias_grad[...] = chunks[0, 0, SHARE : SHARE + 1, :].astype(F32)
 
 
-def final_kernel(mine, other, out):
+def final_kernel(first_mine, first_other, rest_mine, rest_other, out):
     left = lax.axis_index("row") % 2 == 0
-    a, b = mine[...], other[...]
-    out[:, :HALF] = jnp.where(left, a, b)
-    out[:, HALF:] = jnp.where(left, b, a)
+    for rows, mine, other in ((slice(0, FIRST), first_mine, first_other), (slice(FIRST, 512), rest_mine, rest_other)):
+        a, b = mine[...], other[...]
+        out[rows, :HALF] = jnp.where(left, a, b)
+        out[rows, HALF:] = jnp.where(left, b, a)
 
 
 def any_spec():
@@ -178,18 +174,18 @@
     return pl.BlockSpec(memory_space=pltpu.VMEM)
 
 
-def call(kernel, args, out_shape, ids=(), in_specs=None, out_specs=None, scratch=(), flops=0, moved=4 * 2**20):
+def call(kernel, args, out_shape, ids=(), in_specs=None, scratch=(), flops=0, moved=4 * 2**20, vmem=8 * 2**20):
     shapes = [jax.ShapeDtypeStruct(s, d) for s, d in out_shape]
     return pl.pallas_call(
         kernel,
         grid_spec=pltpu.PrefetchScalarGridSpec(
             num_scalar_prefetch=len(ids),
             in_specs=in_specs or [vmem_spec() for _ in args],
-            out_specs=out_specs or [vmem_spec() for _ in shapes],
+            out_specs=[vmem_spec() for _ in shapes],
             scratch_shapes=scratch,
         ),
         out_shape=shapes,
-        compiler_params=pltpu.CompilerParams(vmem_limit_bytes=VMEM_LIMIT),
+        compiler_params=pltpu.CompilerParams(vmem_limit_bytes=vmem),
         cost_estimate=pl.CostEstimate(flops=flops, bytes_accessed=moved, transcendentals=0),
     )(*ids, *args)
 
@@ -232,14 +228,13 @@
     return (part, *(shift(part, axis, d) for d in range(1, 4)))
 
 
-def two_way_gather(mine, other, axis):
-    pair = jnp.stack([mine, other])
+def two_way_gather(first, rest, axis):
     high, low = (1, 0) if axis == "row" else (0, 1)
-    first, rest = pair[:, :FIRST], pair[:, FIRST:]
     near = jnp.stack(ring(rest, axis))
     first = jnp.stack([first, swap_y(first, high, low)])
     first, near = lax.optimization_barrier((first, near))
-    return (*ring(first, axis), near, swap_y(near, high, low))
+    far = swap_y(near, high, low)
+    return jnp.concatenate([jnp.stack(ring(first, axis)), jnp.stack([near, far], axis=1)], axis=3)
 
 
 def two_way_scatter(parts, axis):
@@ -252,8 +247,7 @@
     first, rest = lax.optimization_barrier((first, rest))
     first = add(first[0], *(shift(first[d], axis, d) for d in range(1, 4)))
     rest = add(rest[0], swap_y(rest[1], high, low))
-    total = jnp.concatenate([first, rest], axis=1)
-    return total[0], core_swap(total[1])
+    return (first[0], core_swap(first[1])), (rest[0], core_swap(rest[1]))
 
 
 def z_sum(chunks):
@@ -268,43 +262,57 @@
     other_tiles, other_ids = core_swap(tiles), core_swap(ids)
     scale = 1.0 / math.sqrt(65536)
     tables = (ids, other_ids)
-    def multiply(transposed, pieces):
-        rest, whole = 512 - FIRST, (4, 2, 2, 512, HALF)
+    def multiply(transposed, source):
+        rest = 512 - FIRST
         return call(
             functools.partial(tiles_kernel, transposed),
-            (tiles, other_tiles, *pieces),
+            (tiles, other_tiles, source),
             [((4, 2, FIRST, HALF), BF)] * 2 + [((2, 2, rest, HALF), BF)] * 4,
             ids=tables,
-            in_specs=[any_spec()] * 8,
+            in_specs=[any_spec(), any_spec(), vmem_spec()],
             scratch=[
-                pltpu.VMEM(whole, BF),
                 pltpu.VMEM((2, 64, 128, 128), BF),
                 pltpu.VMEM((65, 128, HALF), F32),
-                pltpu.SemaphoreType.DMA((8,)),
+                pltpu.SemaphoreType.DMA((2,)),
             ],
             flops=2 * 64 * 128 * 128 * 512,
             moved=16 * 2**20,
+            vmem=TILES_VMEM,
         )
 
+    def dense(start, halves):
+        rows = halves[0].shape[0]
+        return call(
+            functools.partial(dense_kernel, start),
+            (*halves, weight, bias.reshape(1, 512), cotangent),
+            [((rows, 512), BF), ((rows, HALF), BF), ((rows, HALF), BF), ((rows, 512), BF), ((rows, 512), BF)],
+            flops=4 * rows * 512**2,
+        )
+
     mine, other = call(halves_kernel, (features,), [((512, HALF), BF)] * 2)
-    pieces = two_way_gather(mine, core_swap(other), "row")
-    mine, other = two_way_scatter(multiply(False, pieces), "col")
-    output, mine, other, chunks = call(
-        functools.partial(dense_kernel, scale),
-        (mine, other, weight, bias.reshape(1, 512), cotangent),
-        [((512, 512), BF), ((512, HALF), BF), ((512, HALF), BF), ((2, 4, 2, SHARE + TAIL, 512), BF)],
-        scratch=[pltpu.VMEM((512, 512), BF), pltpu.VMEM((512, 512), BF), pltpu.VMEM((512, 512), F32)],
-        flops=6 * 512**3,
-        moved=8 * 2**20,
+    pair = jnp.stack([mine, core_swap(other)])
+    source = two_way_gather(pair[:, :FIRST], pair[:, FIRST:], "row")
+    first, rest = two_way_scatter(multiply(False, source), "col")
+    rest_output, mine, other, rest_agg, rest_grad = dense(FIRST, rest)
+    rest = jnp.stack([mine, core_swap(other)])
+    first_output, mine, other, first_agg, first_grad = dense(0, first)
+    first = jnp.stack([mine, core_swap(other)])
+    output = jnp.concatenate([first_output, rest_output])
+    source = two_way_gather(first, rest, "col")
+    (chunks,) = call(
+        functools.partial(weight_kernel, scale),
+        (first_agg, rest_agg, first_grad, rest_grad),
+        [((2, 4, 2, SHARE + TAIL, 512), BF)],
+        scratch=[pltpu.VMEM((512, 512), F32)],
+        flops=2 * 512**3,
     )
-    pieces = two_way_gather(mine, core_swap(other), "col")
-    chunks, pieces = lax.optimization_barrier((plane_sum(chunks), pieces))
-    parts = multiply(True, pieces)
+    chunks, source = lax.optimization_barrier((plane_sum(chunks), source))
+    parts = multiply(True, source)
     chunks, parts = lax.optimization_barrier((jnp.stack(ring(chunks, "row")), parts))
-    mine, other = two_way_scatter(parts, "row")
+    first, rest = two_way_scatter(parts, "row")
     chunks = jnp.stack([chunks, core_swap(chunks)])
     weight_grad, bias_grad = call(place_kernel, (z_sum(chunks),), [((512, 512), F32), ((1, 512), F32)])
-    (feature_grad,) = call(final_kernel, (mine, other), [((512, 512), BF)])
+    (feature_grad,) = call(final_kernel, (*first, *rest), [((512, 512), BF)])
     return (output, feature_grad, weight_grad, bias_grad.reshape(512))
 
 

time: 237 us -> 233 us (0.983)
  waiting for transfers between devices: 118 us -> 111 us
  other arithmetic: 7.87 us -> 13.1 us
  Pallas kernels: 19.4 us -> 17 us
    all_to_all x1, waiting for transfers between devices: 5.13 us -> 0.52 us  [z_sum(): lax.all_to_all(fourfold(part), 'col', 0, 0, tiled=True, axis_index_groups...]
    ppermute x8 -> x11, waiting for transfers between devices: 5.77 us -> 2.04 us  [core_swap(): return lax.ppermute(value, 'row', [(i, i ^ 1) for i in range(16)])]
    concatenate x0 -> x3, other arithmetic: none -> 3.26 us  [the longest x2 2.43 us: two_way_gather(): jnp.concatenate([jnp.stack(ring(first, axis)), jnp.stack([near, far], axi...]
    ppermute x8, starting transfers between devices: 12.3 us -> 15 us  [swap_y(): return lax.ppermute(value, ('row', 'col'), to)]
    pallas_call x6 -> x8, Pallas kernels: 19.4 us -> 17 us  [call(): pl.pallas_call(kernel, grid_spec=pltpu.PrefetchScalarGridSpec(num_scalar_...]
  transfers between devices with their start and end apart: 46 -> 49, of which waited for: 21 -> 22; matrix products, arithmetic and copies ran while one was open for 4% -> 5% of each run, Pallas kernels for 4% -> 4%
where the time goes in v5:
time: 233 us; the launch traced here: 232 us
  waiting for transfers between devices  111 us (48%)
  starting transfers between devices  69.1 us (30%)
  Pallas kernels  17 us (7%)
  blocking collectives  16 us (7%)
  other arithmetic  13.1 us (6%)
  local copies, waits for them, and re-layouts  4.24 us (2%)
    ppermute x27, waiting for transfers between devices, shift(): return lax.ppermute(value, axis, to)  93.8 us
    ppermute x27, starting transfers between devices, shift(): return lax.ppermute(value, axis, to)  41.6 us
    pallas_call x8, Pallas kernels, call(): pl.pallas_call(kernel, grid_spec=pltpu.PrefetchScalarGridSpec(num_scalar_...  17 us
    all_to_all x1, blocking collectives, plane_sum(): lax.all_to_all(fourfold(part), ('row', 'col'), 0, 0, tiled=True, axis_ind...  16 us
    ppermute x8, starting transfers between devices, swap_y(): return lax.ppermute(value, ('row', 'col'), to)  15 us
    ppermute x8, waiting for transfers between devices, swap_y(): return lax.ppermute(value, ('row', 'col'), to)  9.27 us
    all_to_all x1, waiting for transfers between devices, plane_sum(): lax.all_to_all(part, 'row', 0, 0, tiled=True, axis_index_groups=X_LINES)  5.06 us
  transfers between devices with their start and end apart: 49, of which 22 were waited for; matrix products, arithmetic and copies ran while one was open for 5% of the time, Pallas kernels for 4%

profile of v5, /device:TPU:0, one launch (start us, length us, event | category | flops | bytes accessed | tf_op | source)
XLA Modules:
  0.0 231.9 jit_solution(2657117040507678819)
XLA Ops:
  0.6 1.0 copy-done.7
  1.8 1.5 collective-permute-done.2
  3.4 3.4 %collective-permute-start.3 = (bf16[2,256,256]{2,1,0:T(8,128)(2,1)S(1)}, bf16[2,256,256]{2,1,0:T(8,128)(2,1)S(1)}, u32[]{:S(2)}, u32[]{:S(2)}) collective-permute-start(bf16[2,256,256]{2,1,0:T(8,128)(2,1)S(1)} %get-tuple-element.119), channel_id=1, source_target_pairs={{0,64},{1,65},{2,66},{3,67},{4,68},{5,69},{6,70},{7,71},{8,72},{9,... | collective-permute-start | bytes 786440 | tf_op jit(solution)/shard_map/ppermute | solution.py:199
  6.8 3.0 %collective-permute-start.5 = (bf16[2,256,256]{2,1,0:T(8,128)(2,1)S(1)}, bf16[2,256,256]{2,1,0:T(8,128)(2,1)S(1)}, u32[]{:S(2)}, u32[]{:S(2)}) collective-permute-start(bf16[2,256,256]{2,1,0:T(8,128)(2,1)S(1)} %get-tuple-element.118), channel_id=1, source_target_pairs={{0,32},{8,40},{16,48},{24,56},{32,0},{40,8},{48,16},{56,24},{64,96... | collective-permute-start | bytes 786440 | tf_op jit(solution)/shard_map/ppermute | solution.py:207
  10.4 2.6 %collective-permute-start.6 = (bf16[2,256,256]{2,1,0:T(8,128)(2,1)S(1)}, bf16[2,256,256]{2,1,0:T(8,128)(2,1)S(1)}, u32[]{:S(2)}, u32[]{:S(2)}) collective-permute-start(bf16[2,256,256]{2,1,0:T(8,128)(2,1)S(1)} %get-tuple-element.118), channel_id=1, source_target_pairs={{0,48},{8,56},{16,0},{24,8},{32,16},{40,24},{48,32},{56,40},{64,11... | collective-permute-start | bytes 786440 | tf_op jit(solution)/shard_map/ppermute | solution.py:207
  13.4 4.0 %collective-permute-done.5 = bf16[2,256,256]{2,1,0:T(8,128)(2,1)S(1)} collective-permute-done((bf16[2,256,256]{2,1,0:T(8,128)(2,1)S(1)}, bf16[2,256,256]{2,1,0:T(8,128)(2,1)S(1)}, u32[]{:S(2)}, u32[]{:S(2)}) %collective-permute-start.5) | collective-permute-done | bytes 262176 | tf_op jit(solution)/shard_map/ppermute | solution.py:207
  17.4 5.2 %collective-permute-done.4 = bf16[2,256,256]{2,1,0:T(8,128)(2,1)S(1)} collective-permute-done((bf16[2,256,256]{2,1,0:T(8,128)(2,1)S(1)}, bf16[2,256,256]{2,1,0:T(8,128)(2,1)S(1)}, u32[]{:S(2)}, u32[]{:S(2)}) %collective-permute-start.4) | collective-permute-done | bytes 262176 | tf_op jit(solution)/shard_map/ppermute | solution.py:207
  23.3 2.6 %collective-permute-start.9 = (bf16[2,2,256,256]{3,2,1,0:T(8,128)(2,1)S(1)}, bf16[2,2,256,256]{3,2,1,0:T(8,128)(2,1)S(1)}, u32[]{:S(2)}, u32[]{:S(2)}) collective-permute-start(bf16[2,2,256,256]{3,2,1,0:T(8,128)(2,1)S(1)} %pad_maximum_fusion.3), channel_id=1, source_target_pairs={{0,48},{8,56},{16,0},{24,8},{32,16},{40,24},{48,32},{56,40},{64,11... | collective-permute-start | bytes 1572872 | tf_op jit(solution)/shard_map/ppermute | solution.py:207
  25.9 0.9 collective-permute-start.8
  27.5 20.7 %collective-permute-done.9 = bf16[2,2,256,256]{3,2,1,0:T(8,128)(2,1)S(1)} collective-permute-done((bf16[2,2,256,256]{3,2,1,0:T(8,128)(2,1)S(1)}, bf16[2,2,256,256]{3,2,1,0:T(8,128)(2,1)S(1)}, u32[]{:S(2)}, u32[]{:S(2)}) %collective-permute-start.9) | collective-permute-done | bytes 524320 | tf_op jit(solution)/shard_map/ppermute | solution.py:207
  48.3 3.7 %collective-permute-done.7 = bf16[2,2,256,256]{3,2,1,0:T(8,128)(2,1)S(1)} collective-permute-done((bf16[2,2,256,256]{3,2,1,0:T(8,128)(2,1)S(1)}, bf16[2,2,256,256]{3,2,1,0:T(8,128)(2,1)S(1)}, u32[]{:S(2)}, u32[]{:S(2)}) %collective-permute-start.7) | collective-permute-done | bytes 524320 | tf_op jit(solution)/shard_map/ppermute | solution.py:207
  52.3 1.3 copy-done
  53.6 5.9 %shard_map.112 = (bf16[4,2,256,256]{3,2,1,0:T(8,128)(2,1)S(1)}, bf16[4,2,256,256]{3,2,1,0:T(8,128)(2,1)S(1)}, bf16[2,2,256,256]{3,2,1,0:T(8,128)(2,1)S(1)}, bf16...) custom-call(s32[129]{0:T(256)S(1)} %pad_add_fusion.ids, ...), custom_call_target="tpu_custom_call" | custom-call | flops 1073741824 | bytes 16777216 | tf_op jit(solution)/shard_map/pallas_call | solution.py:179
  59.5 2.4 %collective-permute-start.11 = (bf16[4,2,256,256]{3,2,1,0:T(8,128)(2,1)S(1)}, bf16[4,2,256,256]{3,2,1,0:T(8,128)(2,1)S(1)}, u32[]{:S(2)}, u32[]{:S(2)}) collective-permute-start(bf16[4,2,256,256]{3,2,1,0:T(8,128)(2,1)S(1)} %get-tuple-element.60), channel_id=1, source_target_pairs={{0,1},{1,0},{2,3},{3,2},{4,5},{5,4},{6,7},{7,6},{8,9},{9,8},{10,11... | collective-permute-start | bytes 3145736 | tf_op jit(solution)/shard_map/ppermute | solution.py:199
  62.4 3.6 %collective-permute-start.13 = (bf16[2,2,256,256]{3,2,1,0:T(8,128)(2,1)S(1)}, bf16[2,2,256,256]{3,2,1,0:T(8,128)(2,1)S(1)}, u32[]{:S(2)}, u32[]{:S(2)}) collective-permute-start(bf16[2,2,256,256]{3,2,1,0:T(8,128)(2,1)S(1)} %get-tuple-element.63), channel_id=1, source_target_pairs={{0,4},{1,5},{2,6},{3,7},{4,0},{5,1},{6,2},{7,3},{8,12},{9,13},{10,... | collective-permute-start | bytes 1572872 | tf_op jit(solution)/shard_map/ppermute | solution.py:207
  66.0 2.5 %collective-permute-start.14 = (bf16[2,2,256,256]{3,2,1,0:T(8,128)(2,1)S(1)}, bf16[2,2,256,256]{3,2,1,0:T(8,128)(2,1)S(1)}, u32[]{:S(2)}, u32[]{:S(2)}) collective-permute-start(bf16[2,2,256,256]{3,2,1,0:T(8,128)(2,1)S(1)} %get-tuple-element.64), channel_id=1, source_target_pairs={{0,6},{1,7},{2,0},{3,1},{4,2},{5,3},{6,4},{7,5},{8,14},{9,15},{10,... | collective-permute-start | bytes 1572872 | tf_op jit(solution)/shard_map/ppermute | solution.py:207
  68.5 8.3 %collective-permute-done.12 = bf16[2,2,256,256]{3,2,1,0:T(8,128)(2,1)S(1)} collective-permute-done((bf16[2,2,256,256]{3,2,1,0:T(8,128)(2,1)S(1)}, bf16[2,2,256,256]{3,2,1,0:T(8,128)(2,1)S(1)}, u32[]{:S(2)}, u32[]{:S(2)}) %collective-permute-start.12) | collective-permute-done | bytes 524320 | tf_op jit(solution)/shard_map/ppermute | solution.py:207
  76.8 12.3 %collective-permute-done.13 = bf16[2,2,256,256]{3,2,1,0:T(8,128)(2,1)S(1)} collective-permute-done((bf16[2,2,256,256]{3,2,1,0:T(8,128)(2,1)S(1)}, bf16[2,2,256,256]{3,2,1,0:T(8,128)(2,1)S(1)}, u32[]{:S(2)}, u32[]{:S(2)}) %collective-permute-start.13) | collective-permute-done | bytes 524320 | tf_op jit(solution)/shard_map/ppermute | solution.py:207
  89.6 1.7 collective-permute-start.19
  91.4 1.1 collective-permute-start.15
  92.5 2.4 %collective-permute-start.16 = (bf16[2,256,256]{2,1,0:T(8,128)(2,1)S(1)}, bf16[2,256,256]{2,1,0:T(8,128)(2,1)S(1)}, u32[]{:S(2)}, u32[]{:S(2)}) collective-permute-start(bf16[2,256,256]{2,1,0:T(8,128)(2,1)S(1)} %get-tuple-element.67), channel_id=1, source_target_pairs={{0,4},{1,5},{2,6},{3,7},{4,0},{5,1},{6,2},{7,3},{8,12},{9,13},{10,... | collective-permute-start | bytes 786440 | tf_op jit(solution)/shard_map/ppermute | solution.py:207
  94.9 1.2 collective-permute-start.17
  96.1 1.0 collective-permute-done.19
  97.3 2.4 %collective-permute-done.15 = bf16[2,256,256]{2,1,0:T(8,128)(2,1)S(1)} collective-permute-done((bf16[2,256,256]{2,1,0:T(8,128)(2,1)S(1)}, bf16[2,256,256]{2,1,0:T(8,128)(2,1)S(1)}, u32[]{:S(2)}, u32[]{:S(2)}) %collective-permute-start.15) | collective-permute-done | bytes 262176 | tf_op jit(solution)/shard_map/ppermute | solution.py:207
  99.7 6.7 %collective-permute-done.16 = bf16[2,256,256]{2,1,0:T(8,128)(2,1)S(1)} collective-permute-done((bf16[2,256,256]{2,1,0:T(8,128)(2,1)S(1)}, bf16[2,256,256]{2,1,0:T(8,128)(2,1)S(1)}, u32[]{:S(2)}, u32[]{:S(2)}) %collective-permute-start.16) | collective-permute-done | bytes 262176 | tf_op jit(solution)/shard_map/ppermute | solution.py:207
  106.7 0.8 shard_map.114
  109.9 1.5 collective-permute-start.26
  111.4 1.5 collective-permute-start.25
  112.9 1.7 collective-permute-start.27
  114.7 1.4 collective-permute-start.23
  116.2 6.4 %collective-permute-done.23 = bf16[2,256,256]{2,1,0:T(8,128)(2,1)S(1)} collective-permute-done((bf16[2,256,256]{2,1,0:T(8,128)(2,1)S(1)}, bf16[2,256,256]{2,1,0:T(8,128)(2,1)S(1)}, u32[]{:S(2)}, u32[]{:S(2)}) %collective-permute-start.23) | collective-permute-done | bytes 262176 | tf_op jit(solution)/shard_map/ppermute | solution.py:199
  122.6 0.8 pad_maximum_fusion.5
  123.4 2.4 %collective-permute-done.25 = bf16[2,256,256]{2,1,0:T(8,128)(2,1)S(1)} collective-permute-done((bf16[2,256,256]{2,1,0:T(8,128)(2,1)S(1)}, bf16[2,256,256]{2,1,0:T(8,128)(2,1)S(1)}, u32[]{:S(2)}, u32[]{:S(2)}) %collective-permute-start.25) | collective-permute-done | bytes 262176 | tf_op jit(solution)/shard_map/ppermute | solution.py:207
  126.5 0.9 fusion
  127.4 4.1 %all-to-all-start = ((bf16[4,2,48,512]{3,2,1,0:T(8,128)(2,1)}), bf16[4,2,48,512]{3,2,1,0:T(8,128)(2,1)}, u32[]{:S(2)}, u32[]{:S(2)}) async-start(bf16[4,2,48,512]{3,2,1,0:T(8,128)(2,1)} %fusion), calls=%async_computation | async-start | bytes 786432 | tf_op jit(solution)/shard_map/all_to_all | solution.py:219
  131.5 2.1 collective-permute-start.30
  133.6 1.1 collective-permute-start.29
  134.8 5.1 %all-to-all-done = bf16[4,2,48,512]{3,2,1,0:T(8,128)(2,1)} async-done(((bf16[4,2,48,512]{3,2,1,0:T(8,128)(2,1)}), bf16[4,2,48,512]{3,2,1,0:T(8,128)(2,1)}, u32[]{:S(2)}, u32[]{:S(2)}) %all-to-all-start) | async-done | bytes 393248 | tf_op jit(solution)/shard_map/all_to_all | solution.py:219
  139.8 1.1 fusion.15
  141.0 16.0 %all_to_all.20 = bf16[4,2,48,512]{3,2,1,0:T(8,128)(2,1)S(1)} all-to-all(bf16[4,2,48,512]{3,2,1,0:T(8,128)(2,1)S(1)} %broadcast_in_dim.17), channel_id=1, replica_groups={{0,1,64,65},{2,3,66,67},{4,5,68,69},{6,7,70,71},{8,9,72,73},{10,11,74,7..., dimensions={0} | all-to-all | bytes 786432 | tf_op jit(solution)/shard_map/all_to_all | solution.py:220
  157.0 2.9 %collective-permute-done.28 = bf16[2,2,256,256]{3,2,1,0:T(8,128)(2,1)} collective-permute-done((bf16[2,2,256,256]{3,2,1,0:T(8,128)(2,1)}, bf16[2,2,256,256]{3,2,1,0:T(8,128)(2,1)}, u32[]{:S(2)}, u32[]{:S(2)}) %collective-permute-start.28) | collective-permute-done | bytes 524320 | tf_op jit(solution)/shard_map/ppermute | solution.py:207
  160.0 2.1 maximum_maximum_fusion.1.refs_0_
  162.1 2.9 %collective-permute-start.34 = (bf16[2,48,512]{2,1,0:T(8,128)(2,1)S(1)}, bf16[2,48,512]{2,1,0:T(8,128)(2,1)S(1)}, u32[]{:S(2)}, u32[]{:S(2)}) collective-permute-start(bf16[2,48,512]{2,1,0:T(8,128)(2,1)S(1)} %fusion.16), channel_id=1, source_target_pairs={{0,48},{8,56},{16,0},{24,8},{32,16},{40,24},{48,32},{56,40},{64,11... | collective-permute-start | bytes 294920 | tf_op jit(solution)/shard_map/ppermute | solution.py:207
  165.0 0.9 collective-permute-start.33
  165.9 0.9 collective-permute-start.32
  166.7 6.9 %shard_map.116 = (bf16[4,2,256,256]{3,2,1,0:T(8,128)(2,1)S(1)}, bf16[4,2,256,256]{3,2,1,0:T(8,128)(2,1)}, bf16[2,2,256,256]{3,2,1,0:T(8,128)(2,1)S(1)}, bf16[2,2...) custom-call(s32[129]{0:T(256)S(1)} %pad_add_fusion.ids, ...), custom_call_target="tpu_custom_call" | custom-call | flops 1073741824 | bytes 16777216 | tf_op jit(solution)/shard_map/pallas_call | solution.py:179
  174.5 3.2 %collective-permute-start.35 = (bf16[4,2,256,256]{3,2,1,0:T(8,128)(2,1)}, bf16[4,2,256,256]{3,2,1,0:T(8,128)(2,1)}, u32[]{:S(2)}, u32[]{:S(2)}) collective-permute-start(bf16[4,2,256,256]{3,2,1,0:T(8,128)(2,1)} %get-tuple-element.92), channel_id=1, source_target_pairs={{0,64},{1,65},{2,66},{3,67},{4,68},{5,69},{6,70},{7,71},{8,72},{9,... | collective-permute-start | bytes 3145736 | tf_op jit(solution)/shard_map/ppermute | solution.py:199
  177.8 1.0 collective-permute-start.36
  178.8 2.9 %collective-permute-start.37 = (bf16[2,2,256,256]{3,2,1,0:T(8,128)(2,1)}, bf16[2,2,256,256]{3,2,1,0:T(8,128)(2,1)}, u32[]{:S(2)}, u32[]{:S(2)}) collective-permute-start(bf16[2,2,256,256]{3,2,1,0:T(8,128)(2,1)} %get-tuple-element.95), channel_id=1, source_target_pairs={{0,32},{8,40},{16,48},{24,56},{32,0},{40,8},{48,16},{56,24},{64,96... | collective-permute-start | bytes 1572872 | tf_op jit(solution)/shard_map/ppermute | solution.py:207
  181.6 1.0 pad_maximum_fusion.2
  182.6 3.5 %all-to-all-start.2 = ((bf16[4,4,48,512]{3,2,1,0:T(8,128)(2,1)}), bf16[4,4,48,512]{3,2,1,0:T(8,128)(2,1)S(1)}, u32[]{:S(2)}, u32[]{:S(2)}) async-start(bf16[4,4,48,512]{3,2,1,0:T(8,128)(2,1)} %bitcast.67), calls=%async_computation.2 | async-start | bytes 1572864 | tf_op jit(solution)/shard_map/all_to_all | solution.py:255
  186.1 7.4 %collective-permute-done.36 = bf16[2,2,256,256]{3,2,1,0:T(8,128)(2,1)S(1)} collective-permute-done((bf16[2,2,256,256]{3,2,1,0:T(8,128)(2,1)}, bf16[2,2,256,256]{3,2,1,0:T(8,128)(2,1)S(1)}, u32[]{:S(2)}, u32[]{:S(2)}) %collective-permute-start.36) | collective-permute-done | bytes 524320 | tf_op jit(solution)/shard_map/ppermute | solution.py:207
  193.5 11.9 %collective-permute-done.37 = bf16[2,2,256,256]{3,2,1,0:T(8,128)(2,1)} collective-permute-done((bf16[2,2,256,256]{3,2,1,0:T(8,128)(2,1)}, bf16[2,2,256,256]{3,2,1,0:T(8,128)(2,1)}, u32[]{:S(2)}, u32[]{:S(2)}) %collective-permute-start.37) | collective-permute-done | bytes 524320 | tf_op jit(solution)/shard_map/ppermute | solution.py:207
  205.5 2.1 fusion.12
  207.7 2.3 %fusion.10 = (bf16[2,256,256]{2,1,0:T(8,128)(2,1)}, bf16[2,256,256]{2,1,0:T(8,128)(2,1)}, bf16[2,256,256]{2,1,0:T(8,128)(2,1)}, bf16[2,256,256]{2,1,0:T(8,128)(2,1)S(1)}) fusion(bf16[4,2,256,256]{3,2,1,0:T(8,128)(2,1)} %collective-permute-done.35, bf16[4,2,256,256]{3,2,1,0:T(8,128)(2,1)S(1)} %get-tuple-element.91), kind=kLoop, calls=%fused_computation.41 | loop fusion | flops 2097152 | bytes 3145728 | tf_op jit(solution)/shard_map/convert_element_type | solution.py:214
  210.7 3.4 %collective-permute-start.40 = (bf16[2,256,256]{2,1,0:T(8,128)(2,1)}, bf16[2,256,256]{2,1,0:T(8,128)(2,1)S(1)}, u32[]{:S(2)}, u32[]{:S(2)}) collective-permute-start(bf16[2,256,256]{2,1,0:T(8,128)(2,1)} %get-tuple-element.99), channel_id=1, source_target_pairs={{0,32},{8,40},{16,48},{24,56},{32,0},{40,8},{48,16},{56,24},{64,96... | collective-permute-start | bytes 786440 | tf_op jit(solution)/shard_map/ppermute | solution.py:207
  214.2 1.0 broadcast_in_dim.19
  215.1 3.5 %all-to-all-start.3 = ((bf16[4,4,48,512]{3,2,1,0:T(8,128)(2,1)}), bf16[4,4,48,512]{3,2,1,0:T(8,128)(2,1)S(1)}, u32[]{:S(2)}, u32[]{:S(2)}) async-start(bf16[4,4,48,512]{3,2,1,0:T(8,128)(2,1)} %broadcast_in_dim.19), calls=%async_computation.3 | async-start | bytes 1572864 | tf_op jit(solution)/shard_map/all_to_all | solution.py:256
  218.7 1.9 collective-permute-start.43
  220.5 5.6 %collective-permute-done.40 = bf16[2,256,256]{2,1,0:T(8,128)(2,1)S(1)} collective-permute-done((bf16[2,256,256]{2,1,0:T(8,128)(2,1)}, bf16[2,256,256]{2,1,0:T(8,128)(2,1)S(1)}, u32[]{:S(2)}, u32[]{:S(2)}) %collective-permute-start.40) | collective-permute-done | bytes 262176 | tf_op jit(solution)/shard_map/ppermute | solution.py:207
  226.4 1.5 collective-permute-done.43
  228.1 0.8 pad_maximum_fusion.4
  229.5 0.8 shard_map.117
  230.8 1.0 shard_map.118
  (103 shorter events, 10.0 us)
Async XLA Ops:
  0.6 1.0 copy-start.7
  1.7 25.8 %copy-start.12 = (s32[1,1,64]{2,1,0:T(1,128)S(1)}, s32[1,1,64]{2,1,0:T(1,128)}, u32[]{:S(2)}) copy-start(s32[1,1,64]{2,1,0:T(1,128)} %param.13) | copy-start | bytes 772
  1.7 25.8 %copy-start.13 = (s32[1,1,64]{2,1,0:T(1,128)S(1)}, s32[1,1,64]{2,1,0:T(1,128)}, u32[]{:S(2)}) copy-start(s32[1,1,64]{2,1,0:T(1,128)} %param.14) | copy-start | bytes 772
  1.7 1.6 collective-permute-start.2
  3.4 10.0 %collective-permute-start.3 = (bf16[2,256,256]{2,1,0:T(8,128)(2,1)S(1)}, bf16[2,256,256]{2,1,0:T(8,128)(2,1)S(1)}, u32[]{:S(2)}, u32[]{:S(2)}) collective-permute-start(bf16[2,256,256]{2,1,0:T(8,128)(2,1)S(1)} %get-tuple-element.119), channel_id=1, source_target_pairs={{0,64},{1,65},{2,66},{3,67},{4,68},{5,69},{6,70},{7,71},{8,72},{9,... | collective-permute-start | bytes 786440 | tf_op jit(solution)/shard_map/ppermute | solution.py:199
  6.8 45.5 %collective-permute-start.1 = (bf16[64,128,128]{2,1,0:T(8,128)(2,1)}, bf16[64,128,128]{2,1,0:T(8,128)(2,1)S(1)}, u32[]{:S(2)}, u32[]{:S(2)}) collective-permute-start(bf16[64,128,128]{2,1,0:T(8,128)(2,1)} %bitcast.103), channel_id=1, source_target_pairs={{0,8},{8,0},{16,24},{24,16},{32,40},{40,32},{48,56},{56,48},{64,72... | collective-permute-start | bytes 6291464 | tf_op jit(solution)/shard_map/ppermute | solution.py:194
  6.8 10.7 %collective-permute-start.5 = (bf16[2,256,256]{2,1,0:T(8,128)(2,1)S(1)}, bf16[2,256,256]{2,1,0:T(8,128)(2,1)S(1)}, u32[]{:S(2)}, u32[]{:S(2)}) collective-permute-start(bf16[2,256,256]{2,1,0:T(8,128)(2,1)S(1)} %get-tuple-element.118), channel_id=1, source_target_pairs={{0,32},{8,40},{16,48},{24,56},{32,0},{40,8},{48,16},{56,24},{64,96... | collective-permute-start | bytes 786440 | tf_op jit(solution)/shard_map/ppermute | solution.py:207
  9.8 12.8 %collective-permute-start.4 = (bf16[2,256,256]{2,1,0:T(8,128)(2,1)S(1)}, bf16[2,256,256]{2,1,0:T(8,128)(2,1)S(1)}, u32[]{:S(2)}, u32[]{:S(2)}) collective-permute-start(bf16[2,256,256]{2,1,0:T(8,128)(2,1)S(1)} %get-tuple-element.118), channel_id=1, source_target_pairs={{0,16},{8,24},{16,32},{24,40},{32,48},{40,56},{48,0},{56,8},{64,80... | collective-permute-start | bytes 786440 | tf_op jit(solution)/shard_map/ppermute | solution.py:207
  10.4 12.4 %collective-permute-start.6 = (bf16[2,256,256]{2,1,0:T(8,128)(2,1)S(1)}, bf16[2,256,256]{2,1,0:T(8,128)(2,1)S(1)}, u32[]{:S(2)}, u32[]{:S(2)}) collective-permute-start(bf16[2,256,256]{2,1,0:T(8,128)(2,1)S(1)} %get-tuple-element.118), channel_id=1, source_target_pairs={{0,48},{8,56},{16,0},{24,8},{32,16},{40,24},{48,32},{56,40},{64,11... | collective-permute-start | bytes 786440 | tf_op jit(solution)/shard_map/ppermute | solution.py:207
  22.9 29.1 %collective-permute-start.10 = (bf16[4,2,256,256]{3,2,1,0:T(8,128)(2,1)S(1)}, bf16[4,2,256,256]{3,2,1,0:T(8,128)(2,1)S(1)}, u32[]{:S(2)}, u32[]{:S(2)}) collective-permute-start(bf16[4,2,256,256]{3,2,1,0:T(8,128)(2,1)S(1)} %pad_maximum_fusion), channel_id=1, source_target_pairs={{0,64},{1,65},{2,66},{3,67},{4,68},{5,69},{6,70},{7,71},{8,72},{9,... | collective-permute-start | bytes 3145736 | tf_op jit(solution)/shard_map/ppermute | solution.py:199
  23.3 25.0 %collective-permute-start.9 = (bf16[2,2,256,256]{3,2,1,0:T(8,128)(2,1)S(1)}, bf16[2,2,256,256]{3,2,1,0:T(8,128)(2,1)S(1)}, u32[]{:S(2)}, u32[]{:S(2)}) collective-permute-start(bf16[2,2,256,256]{3,2,1,0:T(8,128)(2,1)S(1)} %pad_maximum_fusion.3), channel_id=1, source_target_pairs={{0,48},{8,56},{16,0},{24,8},{32,16},{40,24},{48,32},{56,40},{64,11... | collective-permute-start | bytes 1572872 | tf_op jit(solution)/shard_map/ppermute | solution.py:207
  25.9 22.4 %collective-permute-start.8 = (bf16[2,2,256,256]{3,2,1,0:T(8,128)(2,1)S(1)}, bf16[2,2,256,256]{3,2,1,0:T(8,128)(2,1)S(1)}, u32[]{:S(2)}, u32[]{:S(2)}) collective-permute-start(bf16[2,2,256,256]{3,2,1,0:T(8,128)(2,1)S(1)} %pad_maximum_fusion.3), channel_id=1, source_target_pairs={{0,32},{8,40},{16,48},{24,56},{32,0},{40,8},{48,16},{56,24},{64,96... | collective-permute-start | bytes 1572872 | tf_op jit(solution)/shard_map/ppermute | solution.py:207
  26.8 25.2 %collective-permute-start.7 = (bf16[2,2,256,256]{3,2,1,0:T(8,128)(2,1)S(1)}, bf16[2,2,256,256]{3,2,1,0:T(8,128)(2,1)S(1)}, u32[]{:S(2)}, u32[]{:S(2)}) collective-permute-start(bf16[2,2,256,256]{3,2,1,0:T(8,128)(2,1)S(1)} %pad_maximum_fusion.3), channel_id=1, source_target_pairs={{0,16},{8,24},{16,32},{24,40},{32,48},{40,56},{48,0},{56,8},{64,80... | collective-permute-start | bytes 1572872 | tf_op jit(solution)/shard_map/ppermute | solution.py:207
  48.3 4.0 %collective-permute-start = (s32[129]{0:T(256)S(1)}, s32[129]{0:T(256)S(1)}, u32[]{:S(2)}, u32[]{:S(2)}) collective-permute-start(s32[129]{0:T(256)S(1)} %pad_add_fusion.ids), channel_id=1, source_target_pairs={{0,8},{8,0},{16,24},{24,16},{32,40},{40,32},{48,56},{56,48},{64,72... | collective-permute-start | bytes 1556 | tf_op jit(solution)/shard_map/ppermute | solution.py:194
  52.0 1.6 copy-start
  53.6 6.0 %copy-start.1 = (bf16[64,128,128]{2,1,0:T(8,128)(2,1)}, bf16[64,128,128]{2,1,0:T(8,128)(2,1)S(1)}, u32[]{:S(2)}) copy-start(bf16[64,128,128]{2,1,0:T(8,128)(2,1)S(1)} %collective-permute-done.1.other_tiles) | copy-start | bytes 6291460
  59.5 29.8 %collective-permute-start.11 = (bf16[4,2,256,256]{3,2,1,0:T(8,128)(2,1)S(1)}, bf16[4,2,256,256]{3,2,1,0:T(8,128)(2,1)S(1)}, u32[]{:S(2)}, u32[]{:S(2)}) collective-permute-start(bf16[4,2,256,256]{3,2,1,0:T(8,128)(2,1)S(1)} %get-tuple-element.60), channel_id=1, source_target_pairs={{0,1},{1,0},{2,3},{3,2},{4,5},{5,4},{6,7},{7,6},{8,9},{9,8},{10,11... | collective-permute-start | bytes 3145736 | tf_op jit(solution)/shard_map/ppermute | solution.py:199
  62.0 14.8 %collective-permute-start.12 = (bf16[2,2,256,256]{3,2,1,0:T(8,128)(2,1)S(1)}, bf16[2,2,256,256]{3,2,1,0:T(8,128)(2,1)S(1)}, u32[]{:S(2)}, u32[]{:S(2)}) collective-permute-start(bf16[2,2,256,256]{3,2,1,0:T(8,128)(2,1)S(1)} %get-tuple-element.62), channel_id=1, source_target_pairs={{0,2},{1,3},{2,4},{3,5},{4,6},{5,7},{6,0},{7,1},{8,10},{9,11},{10,... | collective-permute-start | bytes 1572872 | tf_op jit(solution)/shard_map/ppermute | solution.py:207
  62.4 26.6 %collective-permute-start.13 = (bf16[2,2,256,256]{3,2,1,0:T(8,128)(2,1)S(1)}, bf16[2,2,256,256]{3,2,1,0:T(8,128)(2,1)S(1)}, u32[]{:S(2)}, u32[]{:S(2)}) collective-permute-start(bf16[2,2,256,256]{3,2,1,0:T(8,128)(2,1)S(1)} %get-tuple-element.63), channel_id=1, source_target_pairs={{0,4},{1,5},{2,6},{3,7},{4,0},{5,1},{6,2},{7,3},{8,12},{9,13},{10,... | collective-permute-start | bytes 1572872 | tf_op jit(solution)/shard_map/ppermute | solution.py:207
  66.0 23.1 %collective-permute-start.14 = (bf16[2,2,256,256]{3,2,1,0:T(8,128)(2,1)S(1)}, bf16[2,2,256,256]{3,2,1,0:T(8,128)(2,1)S(1)}, u32[]{:S(2)}, u32[]{:S(2)}) collective-permute-start(bf16[2,2,256,256]{3,2,1,0:T(8,128)(2,1)S(1)} %get-tuple-element.64), channel_id=1, source_target_pairs={{0,6},{1,7},{2,0},{3,1},{4,2},{5,3},{6,4},{7,5},{8,14},{9,15},{10,... | collective-permute-start | bytes 1572872 | tf_op jit(solution)/shard_map/ppermute | solution.py:207
  89.1 17.6 %copy-start.3 = (bf16[512,512]{1,0:T(8,128)(2,1)S(1)}, bf16[512,512]{1,0:T(8,128)(2,1)}, u32[]{:S(2)}) copy-start(bf16[512,512]{1,0:T(8,128)(2,1)} %weight.3) | copy-start | bytes 1572868
  89.1 17.6 %copy-start.4 = (bf16[512,512]{1,0:T(8,128)(2,1)S(1)}, bf16[512,512]{1,0:T(8,128)(2,1)}, u32[]{:S(2)}) copy-start(bf16[512,512]{1,0:T(8,128)(2,1)} %cotangent.3) | copy-start | bytes 1572868
  89.1 17.7 %copy-start.10 = (f32[512]{0:T(512)S(1)}, f32[512]{0:T(512)}, u32[]{:S(2)}) copy-start(f32[512]{0:T(512)} %param.10) | copy-start | bytes 6148
  89.6 7.5 %collective-permute-start.19 = (bf16[2,256,256]{2,1,0:T(8,128)(2,1)S(1)}, bf16[2,256,256]{2,1,0:T(8,128)(2,1)S(1)}, u32[]{:S(2)}, u32[]{:S(2)}) collective-permute-start(bf16[2,256,256]{2,1,0:T(8,128)(2,1)S(1)} %get-tuple-element.71), channel_id=1, source_target_pairs={{0,1},{1,0},{2,3},{3,2},{4,5},{5,4},{6,7},{7,6},{8,9},{9,8},{10,11... | collective-permute-start | bytes 786440 | tf_op jit(solution)/shard_map/ppermute | solution.py:199
  91.4 8.3 %collective-permute-start.15 = (bf16[2,256,256]{2,1,0:T(8,128)(2,1)S(1)}, bf16[2,256,256]{2,1,0:T(8,128)(2,1)S(1)}, u32[]{:S(2)}, u32[]{:S(2)}) collective-permute-start(bf16[2,256,256]{2,1,0:T(8,128)(2,1)S(1)} %get-tuple-element.66), channel_id=1, source_target_pairs={{0,2},{1,3},{2,4},{3,5},{4,6},{5,7},{6,0},{7,1},{8,10},{9,11},{10,... | collective-permute-start | bytes 786440 | tf_op jit(solution)/shard_map/ppermute | solution.py:207
  92.5 13.9 %collective-permute-start.16 = (bf16[2,256,256]{2,1,0:T(8,128)(2,1)S(1)}, bf16[2,256,256]{2,1,0:T(8,128)(2,1)S(1)}, u32[]{:S(2)}, u32[]{:S(2)}) collective-permute-start(bf16[2,256,256]{2,1,0:T(8,128)(2,1)S(1)} %get-tuple-element.67), channel_id=1, source_target_pairs={{0,4},{1,5},{2,6},{3,7},{4,0},{5,1},{6,2},{7,3},{8,12},{9,13},{10,... | collective-permute-start | bytes 786440 | tf_op jit(solution)/shard_map/ppermute | solution.py:207
  94.9 11.5 %collective-permute-start.17 = (bf16[2,256,256]{2,1,0:T(8,128)(2,1)S(1)}, bf16[2,256,256]{2,1,0:T(8,128)(2,1)S(1)}, u32[]{:S(2)}, u32[]{:S(2)}) collective-permute-start(bf16[2,256,256]{2,1,0:T(8,128)(2,1)S(1)} %get-tuple-element.68), channel_id=1, source_target_pairs={{0,6},{1,7},{2,0},{3,1},{4,2},{5,3},{6,4},{7,5},{8,14},{9,15},{10,... | collective-permute-start | bytes 786440 | tf_op jit(solution)/shard_map/ppermute | solution.py:207
  97.2 9.5 %collective-permute-start.20 = (bf16[256,256]{1,0:T(8,128)(2,1)S(1)}, bf16[256,256]{1,0:T(8,128)(2,1)S(1)}, u32[]{:S(2)}, u32[]{:S(2)}) collective-permute-start(bf16[256,256]{1,0:T(8,128)(2,1)S(1)} %get-tuple-element.130), channel_id=1, source_target_pairs={{0,8},{8,0},{16,24},{24,16},{32,40},{40,32},{48,56},{56,48},{64,72... | collective-permute-start | bytes 393224 | tf_op jit(solution)/shard_map/ppermute | solution.py:194
  106.6 1.5 collective-permute-start.18
  107.6 2.3 collective-permute-start.24
  108.9 0.9 copy-start.8
  109.0 5.7 %collective-permute-start.22 = (bf16[256,256]{1,0:T(8,128)(2,1)S(1)}, bf16[256,256]{1,0:T(8,128)(2,1)S(1)}, u32[]{:S(2)}, u32[]{:S(2)}) collective-permute-start(bf16[256,256]{1,0:T(8,128)(2,1)S(1)} %get-tuple-element.78), channel_id=1, source_target_pairs={{0,8},{8,0},{16,24},{24,16},{32,40},{40,32},{48,56},{56,48},{64,72... | collective-permute-start | bytes 393224 | tf_op jit(solution)/shard_map/ppermute | solution.py:194
  109.9 13.5 %collective-permute-start.26 = (bf16[2,256,256]{2,1,0:T(8,128)(2,1)S(1)}, bf16[2,256,256]{2,1,0:T(8,128)(2,1)S(1)}, u32[]{:S(2)}, u32[]{:S(2)}) collective-permute-start(bf16[2,256,256]{2,1,0:T(8,128)(2,1)S(1)} %get-tuple-element.125), channel_id=1, source_target_pairs={{0,4},{1,5},{2,6},{3,7},{4,0},{5,1},{6,2},{7,3},{8,12},{9,13},{10,... | collective-permute-start | bytes 786440 | tf_op jit(solution)/shard_map/ppermute | solution.py:207
  111.4 14.4 %collective-permute-start.25 = (bf16[2,256,256]{2,1,0:T(8,128)(2,1)S(1)}, bf16[2,256,256]{2,1,0:T(8,128)(2,1)S(1)}, u32[]{:S(2)}, u32[]{:S(2)}) collective-permute-start(bf16[2,256,256]{2,1,0:T(8,128)(2,1)S(1)} %get-tuple-element.125), channel_id=1, source_target_pairs={{0,2},{1,3},{2,4},{3,5},{4,6},{5,7},{6,0},{7,1},{8,10},{9,11},{10,... | collective-permute-start | bytes 786440 | tf_op jit(solution)/shard_map/ppermute | solution.py:207
  112.9 12.9 %collective-permute-start.27 = (bf16[2,256,256]{2,1,0:T(8,128)(2,1)S(1)}, bf16[2,256,256]{2,1,0:T(8,128)(2,1)S(1)}, u32[]{:S(2)}, u32[]{:S(2)}) collective-permute-start(bf16[2,256,256]{2,1,0:T(8,128)(2,1)S(1)} %get-tuple-element.125), channel_id=1, source_target_pairs={{0,6},{1,7},{2,0},{3,1},{4,2},{5,3},{6,4},{7,5},{8,14},{9,15},{10,... | collective-permute-start | bytes 786440 | tf_op jit(solution)/shard_map/ppermute | solution.py:207
  114.7 7.9 %collective-permute-start.23 = (bf16[2,256,256]{2,1,0:T(8,128)(2,1)S(1)}, bf16[2,256,256]{2,1,0:T(8,128)(2,1)S(1)}, u32[]{:S(2)}, u32[]{:S(2)}) collective-permute-start(bf16[2,256,256]{2,1,0:T(8,128)(2,1)S(1)} %get-tuple-element.127), channel_id=1, source_target_pairs={{0,1},{1,0},{2,3},{3,2},{4,5},{5,4},{6,7},{7,6},{8,9},{9,8},{10,11... | collective-permute-start | bytes 786440 | tf_op jit(solution)/shard_map/ppermute | solution.py:199
  116.1 10.4 %collective-permute-start.21 = (bf16[4,2,48,512]{3,2,1,0:T(8,128)(2,1)S(1)}, bf16[4,2,48,512]{3,2,1,0:T(8,128)(2,1)S(1)}, u32[]{:S(2)}, u32[]{:S(2)}) collective-permute-start(bf16[4,2,48,512]{3,2,1,0:T(8,128)(2,1)S(1)} %slice_bitcast_fusion), channel_id=1, source_target_pairs={{0,8},{8,0},{16,24},{24,16},{32,40},{40,32},{48,56},{56,48},{64,72... | collective-permute-start | bytes 1179656 | tf_op jit(solution)/shard_map/ppermute | solution.py:194
  126.0 34.0 %collective-permute-start.31 = (bf16[4,2,256,256]{3,2,1,0:T(8,128)(2,1)S(1)}, bf16[4,2,256,256]{3,2,1,0:T(8,128)(2,1)}, u32[]{:S(2)}, u32[]{:S(2)}) collective-permute-start(bf16[4,2,256,256]{3,2,1,0:T(8,128)(2,1)S(1)} %pad_maximum_fusion.1), channel_id=1, source_target_pairs={{0,1},{1,0},{2,3},{3,2},{4,5},{5,4},{6,7},{7,6},{8,9},{9,8},{10,11... | collective-permute-start | bytes 3145736 | tf_op jit(solution)/shard_map/ppermute | solution.py:199
  127.4 12.5 %all-to-all-start = ((bf16[4,2,48,512]{3,2,1,0:T(8,128)(2,1)}), bf16[4,2,48,512]{3,2,1,0:T(8,128)(2,1)}, u32[]{:S(2)}, u32[]{:S(2)}) async-start(bf16[4,2,48,512]{3,2,1,0:T(8,128)(2,1)} %fusion), calls=%async_computation | async-start | bytes 786432 | tf_op jit(solution)/shard_map/all_to_all | solution.py:219
  131.5 25.5 %collective-permute-start.30 = (bf16[2,2,256,256]{3,2,1,0:T(8,128)(2,1)}, bf16[2,2,256,256]{3,2,1,0:T(8,128)(2,1)}, u32[]{:S(2)}, u32[]{:S(2)}) collective-permute-start(bf16[2,2,256,256]{3,2,1,0:T(8,128)(2,1)} %pad_maximum_fusion.5), channel_id=1, source_target_pairs={{0,6},{1,7},{2,0},{3,1},{4,2},{5,3},{6,4},{7,5},{8,14},{9,15},{10,... | collective-permute-start | bytes 1572872 | tf_op jit(solution)/shard_map/ppermute | solution.py:207
  133.6 23.4 %collective-permute-start.29 = (bf16[2,2,256,256]{3,2,1,0:T(8,128)(2,1)}, bf16[2,2,256,256]{3,2,1,0:T(8,128)(2,1)}, u32[]{:S(2)}, u32[]{:S(2)}) collective-permute-start(bf16[2,2,256,256]{3,2,1,0:T(8,128)(2,1)} %pad_maximum_fusion.5), channel_id=1, source_target_pairs={{0,4},{1,5},{2,6},{3,7},{4,0},{5,1},{6,2},{7,3},{8,12},{9,13},{10,... | collective-permute-start | bytes 1572872 | tf_op jit(solution)/shard_map/ppermute | solution.py:207
  134.8 25.2 %collective-permute-start.28 = (bf16[2,2,256,256]{3,2,1,0:T(8,128)(2,1)}, bf16[2,2,256,256]{3,2,1,0:T(8,128)(2,1)}, u32[]{:S(2)}, u32[]{:S(2)}) collective-permute-start(bf16[2,2,256,256]{3,2,1,0:T(8,128)(2,1)} %pad_maximum_fusion.5), channel_id=1, source_target_pairs={{0,2},{1,3},{2,4},{3,5},{4,6},{5,7},{6,0},{7,1},{8,10},{9,11},{10,... | collective-permute-start | bytes 1572872 | tf_op jit(solution)/shard_map/ppermute | solution.py:207
  160.0 6.8 %copy-start.2 = (bf16[64,128,128]{2,1,0:T(8,128)(2,1)S(1)}, bf16[64,128,128]{2,1,0:T(8,128)(2,1)}, u32[]{:S(2)}) copy-start(bf16[64,128,128]{2,1,0:T(8,128)(2,1)} %copy-done.1) | copy-start | bytes 6291460
  162.1 12.3 %collective-permute-start.34 = (bf16[2,48,512]{2,1,0:T(8,128)(2,1)S(1)}, bf16[2,48,512]{2,1,0:T(8,128)(2,1)S(1)}, u32[]{:S(2)}, u32[]{:S(2)}) collective-permute-start(bf16[2,48,512]{2,1,0:T(8,128)(2,1)S(1)} %fusion.16), channel_id=1, source_target_pairs={{0,48},{8,56},{16,0},{24,8},{32,16},{40,24},{48,32},{56,40},{64,11... | collective-permute-start | bytes 294920 | tf_op jit(solution)/shard_map/ppermute | solution.py:207
  165.0 9.4 %collective-permute-start.33 = (bf16[2,48,512]{2,1,0:T(8,128)(2,1)S(1)}, bf16[2,48,512]{2,1,0:T(8,128)(2,1)S(1)}, u32[]{:S(2)}, u32[]{:S(2)}) collective-permute-start(bf16[2,48,512]{2,1,0:T(8,128)(2,1)S(1)} %fusion.16), channel_id=1, source_target_pairs={{0,32},{8,40},{16,48},{24,56},{32,0},{40,8},{48,16},{56,24},{64,96... | collective-permute-start | bytes 294920 | tf_op jit(solution)/shard_map/ppermute | solution.py:207
  165.9 8.6 %collective-permute-start.32 = (bf16[2,48,512]{2,1,0:T(8,128)(2,1)S(1)}, bf16[2,48,512]{2,1,0:T(8,128)(2,1)S(1)}, u32[]{:S(2)}, u32[]{:S(2)}) collective-permute-start(bf16[2,48,512]{2,1,0:T(8,128)(2,1)S(1)} %fusion.16), channel_id=1, source_target_pairs={{0,16},{8,24},{16,32},{24,40},{32,48},{40,56},{48,0},{56,8},{64,80... | collective-permute-start | bytes 294920 | tf_op jit(solution)/shard_map/ppermute | solution.py:207
  173.6 0.8 copy-start.5
  174.5 31.0 %copy-start.6 = (bf16[2,2,256,256]{3,2,1,0:T(8,128)(2,1)S(1)}, bf16[2,2,256,256]{3,2,1,0:T(8,128)(2,1)}, u32[]{:S(2)}) copy-start(bf16[2,2,256,256]{3,2,1,0:T(8,128)(2,1)} %copy-done.5) | copy-start | bytes 1572868
  174.5 33.1 %collective-permute-start.35 = (bf16[4,2,256,256]{3,2,1,0:T(8,128)(2,1)}, bf16[4,2,256,256]{3,2,1,0:T(8,128)(2,1)}, u32[]{:S(2)}, u32[]{:S(2)}) collective-permute-start(bf16[4,2,256,256]{3,2,1,0:T(8,128)(2,1)} %get-tuple-element.92), channel_id=1, source_target_pairs={{0,64},{1,65},{2,66},{3,67},{4,68},{5,69},{6,70},{7,71},{8,72},{9,... | collective-permute-start | bytes 3145736 | tf_op jit(solution)/shard_map/ppermute | solution.py:199
  177.8 3.9 %collective-permute-start.45 = (bf16[4,2,48,512]{3,2,1,0:T(8,128)(2,1)S(1)}, bf16[4,2,48,512]{3,2,1,0:T(8,128)(2,1)S(1)}, u32[]{:S(2)}, u32[]{:S(2)}) collective-permute-start(bf16[4,2,48,512]{3,2,1,0:T(8,128)(2,1)S(1)} %pad_maximum_fusion.6), channel_id=1, source_target_pairs={{0,8},{8,0},{16,24},{24,16},{32,40},{40,32},{48,56},{56,48},{64,72... | collective-permute-start | bytes 1179656 | tf_op jit(solution)/shard_map/ppermute | solution.py:194
  177.8 15.8 %collective-permute-start.36 = (bf16[2,2,256,256]{3,2,1,0:T(8,128)(2,1)}, bf16[2,2,256,256]{3,2,1,0:T(8,128)(2,1)S(1)}, u32[]{:S(2)}, u32[]{:S(2)}) collective-permute-start(bf16[2,2,256,256]{3,2,1,0:T(8,128)(2,1)} %get-tuple-element.94), channel_id=1, source_target_pairs={{0,16},{8,24},{16,32},{24,40},{32,48},{40,56},{48,0},{56,8},{64,80... | collective-permute-start | bytes 1572872 | tf_op jit(solution)/shard_map/ppermute | solution.py:207
  178.8 26.7 %collective-permute-start.37 = (bf16[2,2,256,256]{3,2,1,0:T(8,128)(2,1)}, bf16[2,2,256,256]{3,2,1,0:T(8,128)(2,1)}, u32[]{:S(2)}, u32[]{:S(2)}) collective-permute-start(bf16[2,2,256,256]{3,2,1,0:T(8,128)(2,1)} %get-tuple-element.95), channel_id=1, source_target_pairs={{0,32},{8,40},{16,48},{24,56},{32,0},{40,8},{48,16},{56,24},{64,96... | collective-permute-start | bytes 1572872 | tf_op jit(solution)/shard_map/ppermute | solution.py:207
  181.6 23.9 %collective-permute-start.38 = (bf16[2,2,256,256]{3,2,1,0:T(8,128)(2,1)}, bf16[2,2,256,256]{3,2,1,0:T(8,128)(2,1)}, u32[]{:S(2)}, u32[]{:S(2)}) collective-permute-start(bf16[2,2,256,256]{3,2,1,0:T(8,128)(2,1)} %get-tuple-element.96), channel_id=1, source_target_pairs={{0,48},{8,56},{16,0},{24,8},{32,16},{40,24},{48,32},{56,40},{64,11... | collective-permute-start | bytes 1572872 | tf_op jit(solution)/shard_map/ppermute | solution.py:207
  182.6 31.5 %all-to-all-start.2 = ((bf16[4,4,48,512]{3,2,1,0:T(8,128)(2,1)}), bf16[4,4,48,512]{3,2,1,0:T(8,128)(2,1)S(1)}, u32[]{:S(2)}, u32[]{:S(2)}) async-start(bf16[4,4,48,512]{3,2,1,0:T(8,128)(2,1)} %bitcast.67), calls=%async_computation.2 | async-start | bytes 1572864 | tf_op jit(solution)/shard_map/all_to_all | solution.py:255
  207.6 11.0 %copy-start.11 = (bf16[2,256,256]{2,1,0:T(8,128)(2,1)S(1)}, bf16[2,256,256]{2,1,0:T(8,128)(2,1)}, u32[]{:S(2)}) copy-start(bf16[2,256,256]{2,1,0:T(8,128)(2,1)} %get-tuple-element.102) | copy-start | bytes 786436
  207.6 20.5 %copy-start.9 = (bf16[256,512]{1,0:T(8,128)(2,1)S(1)}, bf16[256,512]{1,0:T(8,128)(2,1)}, u32[]{:S(2)}) copy-start(bf16[256,512]{1,0:T(8,128)(2,1)} %copy-done.8) | copy-start | bytes 786436
  210.0 10.5 %collective-permute-start.39 = (bf16[2,256,256]{2,1,0:T(8,128)(2,1)}, bf16[2,256,256]{2,1,0:T(8,128)(2,1)S(1)}, u32[]{:S(2)}, u32[]{:S(2)}) collective-permute-start(bf16[2,256,256]{2,1,0:T(8,128)(2,1)} %get-tuple-element.98), channel_id=1, source_target_pairs={{0,16},{8,24},{16,32},{24,40},{32,48},{40,56},{48,0},{56,8},{64,80... | collective-permute-start | bytes 786440 | tf_op jit(solution)/shard_map/ppermute | solution.py:207
  210.7 15.5 %collective-permute-start.40 = (bf16[2,256,256]{2,1,0:T(8,128)(2,1)}, bf16[2,256,256]{2,1,0:T(8,128)(2,1)S(1)}, u32[]{:S(2)}, u32[]{:S(2)}) collective-permute-start(bf16[2,256,256]{2,1,0:T(8,128)(2,1)} %get-tuple-element.99), channel_id=1, source_target_pairs={{0,32},{8,40},{16,48},{24,56},{32,0},{40,8},{48,16},{56,24},{64,96... | collective-permute-start | bytes 786440 | tf_op jit(solution)/shard_map/ppermute | solution.py:207
  214.1 12.1 %collective-permute-start.41 = (bf16[2,256,256]{2,1,0:T(8,128)(2,1)}, bf16[2,256,256]{2,1,0:T(8,128)(2,1)S(1)}, u32[]{:S(2)}, u32[]{:S(2)}) collective-permute-start(bf16[2,256,256]{2,1,0:T(8,128)(2,1)} %get-tuple-element.100), channel_id=1, source_target_pairs={{0,48},{8,56},{16,0},{24,8},{32,16},{40,24},{48,32},{56,40},{64,11... | collective-permute-start | bytes 786440 | tf_op jit(solution)/shard_map/ppermute | solution.py:207
  215.1 15.7 %all-to-all-start.3 = ((bf16[4,4,48,512]{3,2,1,0:T(8,128)(2,1)}), bf16[4,4,48,512]{3,2,1,0:T(8,128)(2,1)S(1)}, u32[]{:S(2)}, u32[]{:S(2)}) async-start(bf16[4,4,48,512]{3,2,1,0:T(8,128)(2,1)} %broadcast_in_dim.19), calls=%async_computation.3 | async-start | bytes 1572864 | tf_op jit(solution)/shard_map/all_to_all | solution.py:256
  218.7 9.3 %collective-permute-start.43 = (bf16[2,256,256]{2,1,0:T(8,128)(2,1)S(1)}, bf16[2,256,256]{2,1,0:T(8,128)(2,1)S(1)}, u32[]{:S(2)}, u32[]{:S(2)}) collective-permute-start(bf16[2,256,256]{2,1,0:T(8,128)(2,1)S(1)} %copy-done.11), channel_id=1, source_target_pairs={{0,64},{1,65},{2,66},{3,67},{4,68},{5,69},{6,70},{7,71},{8,72},{9,... | collective-permute-start | bytes 786440 | tf_op jit(solution)/shard_map/ppermute | solution.py:199
  226.3 2.7 %collective-permute-start.42 = (bf16[256,256]{1,0:T(8,128)(2,1)S(1)}, bf16[256,256]{1,0:T(8,128)(2,1)S(1)}, u32[]{:S(2)}, u32[]{:S(2)}) collective-permute-start(bf16[256,256]{1,0:T(8,128)(2,1)S(1)} %get-tuple-element.122), channel_id=1, source_target_pairs={{0,8},{8,0},{16,24},{24,16},{32,40},{40,32},{48,56},{56,48},{64,72... | collective-permute-start | bytes 393224 | tf_op jit(solution)/shard_map/ppermute | solution.py:194
  228.0 1.4 collective-permute-start.44

commit v6 on v5

--- a/solution.py
+++ b/solution.py
@@ -16,11 +16,7 @@
 FIRST = 256
 SHARE = 32
 TAIL = 16
-X_LINES = [[y * 8 + x * 2 + core for x in range(4)] for y in range(2) for core in range(2)]
-Z_LINES = [[z * 2 + y for z in range(4)] for y in range(2)]
-Y_LINES = [
-    [(high * 8 + line) * 8 + z * 2 + low for high in range(2) for low in range(2)] for line in range(8) for z in range(4)
-]
+CHUNK = 2 * SHARE + TAIL
 
 
 def tile_loop(count, acc, step):
@@ -133,29 +129,39 @@
 
 def weight_kernel(scale, agg_1, agg_2, grad_1, grad_2, chunks, product):
     core = lax.rem(lax.axis_index("row"), 2)
+    col = lax.axis_index("col")
     both = (((0,), (0,)), ((), ()))
     product[...] = lax.dot_general(agg_1[...], grad_1[...], both, preferred_element_type=F32)
     product[...] += lax.dot_general(agg_2[...], grad_2[...], both, preferred_element_type=F32)
     bias_sum = jnp.sum(grad_1[...].astype(F32), axis=0, keepdims=True)
     bias_sum = (bias_sum + jnp.sum(grad_2[...].astype(F32), axis=0, keepdims=True)) * scale
-    tail = jnp.broadcast_to(bias_sum, (TAIL, bias_sum.shape[1])).astype(BF)
+    row = lax.broadcasted_iota(jnp.int32, (TAIL, HALF), 0)
+    tail = jnp.where(row == 0, bias_sum[:, :HALF], jnp.where(row == 1, bias_sum[:, HALF:], 0.0)).astype(BF)
     for far in range(2):
-        for x in range(4):
+        for d in range(4):
             for y in range(2):
-                owner = y * 8 + x * 2 + lax.rem(core + far, 2)
-                rows = product[pl.ds(pl.multiple_of(owner * SHARE, SHARE), SHARE), :]
-                chunks[far, x, y, :SHARE, :] = (rows * scale).astype(BF)
-                chunks[far, x, y, SHARE:, :] = tail
-
-
-def place_kernel(chunks, weight_grad, bias_grad):
-    me = lax.axis_index("row")
-    for flat in range(16):
-        far, x, y = flat // 8, flat // 2 % 4, flat % 2
-        owner = y * 8 + lax.rem(lax.rem(me // 2, 4) + 4 - x, 4) * 2 + lax.rem(me + far, 2)
-        at = pl.ds(pl.multiple_of(owner * SHARE, SHARE), SHARE)
-        weight_grad[at, :] = chunks[flat // 4, flat % 4, :SHARE, :].astype(F32)
-    bias_grad[...] = chunks[0, 0, SHARE : SHARE + 1, :].astype(F32)
+                rows = product[share_rows(lax.rem(core + far, 2), lax.rem(col // 2 + d, 4), lax.rem(col + y, 2)), :]
+                rows = (rows * scale).astype(BF)
+                chunks[far, d, y, :SHARE, :] = rows[:, :HALF]
+                chunks[far, d, y, SHARE : 2 * SHARE, :] = rows[:, HALF:]
+                chunks[far, d, y, 2 * SHARE :, :] = tail
+
+
+def share_rows(core, z, y):
+    return pl.ds(pl.multiple_of((core * 8 + z * 2 + y) * SHARE, SHARE), SHARE)
+
+
+def place_kernel(own, moved_1, moved_2, moved_3, weight_grad, bias_grad):
+    core = lax.rem(lax.axis_index("row"), 2)
+    col = lax.axis_index("col")
+    for d, piece in enumerate((own, moved_1, moved_2, moved_3)):
+        for y in range(2):
+            for far in range(2):
+                at = share_rows(lax.rem(core + far, 2), lax.rem(col // 2 + 4 - d, 4), lax.rem(col + y, 2))
+                weight_grad[at, :HALF] = piece[y, far, :SHARE, :].astype(F32)
+                weight_grad[at, HALF:] = piece[y, far, SHARE : 2 * SHARE, :].astype(F32)
+    bias_grad[:, :HALF] = own[0, 0, 2 * SHARE : 2 * SHARE + 1, :].astype(F32)
+    bias_grad[:, HALF:] = own[0, 0, 2 * SHARE + 1 : 2 * SHARE + 2, :].astype(F32)
 
 
 def final_kernel(first_mine, first_other, rest_mine, rest_other, out):
@@ -214,46 +220,51 @@
     return total.astype(BF)
 
 
-def plane_sum(chunks):
-    part = add(chunks[0], core_swap(chunks[1]))
-    part = add(*lax.all_to_all(part, "row", 0, 0, tiled=True, axis_index_groups=X_LINES))
-    return add(*lax.all_to_all(fourfold(part), ("row", "col"), 0, 0, tiled=True, axis_index_groups=Y_LINES))
-
-
-def fourfold(value):
-    return jnp.broadcast_to(value[None], (4, *value.shape))
-
-
 def ring(part, axis):
     return (part, *(shift(part, axis, d) for d in range(1, 4)))
 
 
-def two_way_gather(first, rest, axis):
+def two_way_gather(first, rest, axis, chunks=None):
     high, low = (1, 0) if axis == "row" else (0, 1)
     near = jnp.stack(ring(rest, axis))
-    first = jnp.stack([first, swap_y(first, high, low)])
-    first, near = lax.optimization_barrier((first, near))
+    if chunks is None:
+        other = swap_y(first, high, low)
+    else:
+        moved = swap_y(jnp.concatenate([first, chunks[:, 1].reshape(2, 2 * CHUNK, HALF)], axis=1), high, low)
+        other = moved[:, :FIRST]
+        chunks = add(chunks[:, 0], moved[:, FIRST:].reshape(4, CHUNK, HALF))
+    first = jnp.stack([first, other])
+    first, near, chunks = lax.optimization_barrier((first, near, chunks))
     far = swap_y(near, high, low)
-    return jnp.concatenate([jnp.stack(ring(first, axis)), jnp.stack([near, far], axis=1)], axis=3)
-
-
-def two_way_scatter(parts, axis):
+    if chunks is None:
+        pieces = ring(first, axis)
+    else:
+        flat = first.reshape(-1, HALF)
+        size = flat.shape[0]
+        moved = [shift(jnp.concatenate([flat, chunks[d]]), axis, d) for d in range(1, 4)]
+        pieces = (first, *(part[:size].reshape(first.shape) for part in moved))
+        chunks = add(chunks[0], *(part[size:] for part in moved))
+    return jnp.concatenate([jnp.stack(pieces), jnp.stack([near, far], axis=1)], axis=3), chunks
+
+
+def two_way_scatter(parts, axis, chunk=None):
     stay_first, over_y, stay_rest, *ahead = parts
     high, low = (1, 0) if axis == "row" else (0, 1)
-    from_y = swap_y(over_y, high, low)
+    if chunk is None:
+        from_y = swap_y(over_y, high, low)
+    else:
+        flat = over_y.reshape(-1, HALF)
+        size = flat.shape[0]
+        moved = swap_y(jnp.concatenate([flat, chunk]), high, low)
+        from_y = moved[:size].reshape(over_y.shape)
+        chunk = add(chunk, moved[size:])
     moved = [shift(part, axis, d + 1) for d, part in enumerate(ahead)]
     rest = [add(stay_rest[y], *(part[y] for part in moved)) for y in range(2)]
     first = [add(stay_first[d], from_y[d]) for d in range(4)]
     first, rest = lax.optimization_barrier((first, rest))
     first = add(first[0], *(shift(first[d], axis, d) for d in range(1, 4)))
     rest = add(rest[0], swap_y(rest[1], high, low))
-    return (first[0], core_swap(first[1])), (rest[0], core_swap(rest[1]))
-
-
-def z_sum(chunks):
-    parts = chunks.reshape(4, 4, *chunks.shape[-2:])
-    part = add(*lax.all_to_all(parts, "col", 0, 0, tiled=True, axis_index_groups=Z_LINES))
-    return lax.all_to_all(fourfold(part), "col", 0, 0, tiled=True, axis_index_groups=Z_LINES)
+    return (first[0], core_swap(first[1])), (rest[0], core_swap(rest[1])), chunk
 
 
 def on_device(features, weight, bias, cotangent, tile_values, tile_rows, tile_cols, tile_counts):
@@ -291,27 +302,29 @@
 
     mine, other = call(halves_kernel, (features,), [((512, HALF), BF)] * 2)
     pair = jnp.stack([mine, core_swap(other)])
-    source = two_way_gather(pair[:, :FIRST], pair[:, FIRST:], "row")
-    first, rest = two_way_scatter(multiply(False, source), "col")
+    source, _ = two_way_gather(pair[:, :FIRST], pair[:, FIRST:], "row")
+    first, rest, _ = two_way_scatter(multiply(False, source), "col")
     rest_output, mine, other, rest_agg, rest_grad = dense(FIRST, rest)
     rest = jnp.stack([mine, core_swap(other)])
     first_output, mine, other, first_agg, first_grad = dense(0, first)
     first = jnp.stack([mine, core_swap(other)])
     output = jnp.concatenate([first_output, rest_output])
-    source = two_way_gather(first, rest, "col")
     (chunks,) = call(
         functools.partial(weight_kernel, scale),
         (first_agg, rest_agg, first_grad, rest_grad),
-        [((2, 4, 2, SHARE + TAIL, 512), BF)],
+        [((2, 4, 2, CHUNK, HALF), BF)],
         scratch=[pltpu.VMEM((512, 512), F32)],
         flops=2 * 512**3,
     )
-    chunks, source = lax.optimization_barrier((plane_sum(chunks), source))
+    chunks = add(chunks[0], core_swap(chunks[1]))
+    source, chunk = two_way_gather(first, rest, "col", chunks)
+    source, chunk = lax.optimization_barrier((source, chunk))
     parts = multiply(True, source)
-    chunks, parts = lax.optimization_barrier((jnp.stack(ring(chunks, "row")), parts))
-    first, rest = two_way_scatter(parts, "row")
-    chunks = jnp.stack([chunks, core_swap(chunks)])
-    weight_grad, bias_grad = call(place_kernel, (z_sum(chunks),), [((512, 512), F32), ((1, 512), F32)])
+    chunk, parts = lax.optimization_barrier((add(*ring(chunk, "row")), parts))
+    first, rest, chunk = two_way_scatter(parts, "row", chunk)
+    chunks = jnp.stack([chunk, core_swap(chunk)])
+    chunks = jnp.stack([chunks, swap_y(chunks, 0, 1)])
+    weight_grad, bias_grad = call(place_kernel, ring(chunks, "col"), [((512, 512), F32), ((1, 512), F32)])
     (feature_grad,) = call(final_kernel, (*first, *rest), [((512, 512), BF)])
     return (output, feature_grad, weight_grad, bias_grad.reshape(512))
 

time: 233 us -> 224 us (0.961)
  waiting for transfers between devices: 111 us -> 131 us
  blocking collectives: 16 us -> 0 us
  other arithmetic: 13.1 us -> 4.01 us
  Pallas kernels: 17 us -> 14.3 us
    ppermute x27 -> x30, waiting for transfers between devices: 93.8 us -> 123 us  [shift(): return lax.ppermute(value, axis, to)]
    all_to_all x1 -> x0, blocking collectives: 16 us -> none  [plane_sum(): lax.all_to_all(fourfold(part), ('row', 'col'), 0, 0, tiled=True, axis_ind...]
    all_to_all x3 -> x0, starting transfers between devices: 11.1 us -> none  [the longest x1 4.12 us: plane_sum(): lax.all_to_all(part, 'row', 0, 0, tiled=True, axis_index_groups=X_LINES)]
    ppermute x27 -> x30, starting transfers between devices: 41.6 us -> 51.9 us  [shift(): return lax.ppermute(value, axis, to)]
    all_to_all x3 -> x0, waiting for transfers between devices: 5.58 us -> none  [the longest x1 5.06 us: plane_sum(): lax.all_to_all(part, 'row', 0, 0, tiled=True, axis_index_groups=X_LINES)]
    ppermute x8 -> x9, waiting for transfers between devices: 9.27 us -> 5.02 us  [swap_y(): return lax.ppermute(value, ('row', 'col'), to)]
    pallas_call x8, Pallas kernels: 17 us -> 14.3 us  [call(): pl.pallas_call(kernel, grid_spec=pltpu.PrefetchScalarGridSpec(num_scalar_...]
    convert_element_type x7 -> x11, other arithmetic: 3.85 us -> 1.21 us  [add(): return total.astype(BF)]
  transfers between devices with their start and end apart: 49 -> 50, of which waited for: 22 -> 27; matrix products, arithmetic and copies ran while one was open for 5% -> 2% of each run, Pallas kernels for 4% -> 3%
where the time goes in v6:
time: 224 us
  waiting for transfers between devices  131 us (58%)
  starting transfers between devices  70.1 us (31%)
  Pallas kernels  14.3 us (6%)
  other arithmetic  4.01 us (2%)
  local copies, waits for them, and re-layouts  2.69 us (1%)
    ppermute x30, waiting for transfers between devices, shift(): return lax.ppermute(value, axis, to)  123 us
    ppermute x30, starting transfers between devices, shift(): return lax.ppermute(value, axis, to)  51.9 us
    ppermute x9, starting transfers between devices, swap_y(): return lax.ppermute(value, ('row', 'col'), to)  16.3 us
    pallas_call x8, Pallas kernels, call(): pl.pallas_call(kernel, grid_spec=pltpu.PrefetchScalarGridSpec(num_scalar_...  14.3 us
    ppermute x9, waiting for transfers between devices, swap_y(): return lax.ppermute(value, ('row', 'col'), to)  5.02 us
  transfers between devices with their start and end apart: 50, of which 27 were waited for; matrix products, arithmetic and copies ran while one was open for 2% of the time, Pallas kernels for 3%

profile of v6, /device:TPU:0, one launch (start us, length us, event | category | flops | bytes accessed | tf_op | source)
XLA Modules:
  0.0 223.8 jit_solution(11854142437452423419)
XLA Ops:
  0.6 1.0 copy-done.3
  1.8 1.5 collective-permute-done.2
  3.4 3.4 %collective-permute-start.3 = (bf16[2,256,256]{2,1,0:T(8,128)(2,1)S(1)}, bf16[2,256,256]{2,1,0:T(8,128)(2,1)S(1)}, u32[]{:S(2)}, u32[]{:S(2)}) collective-permute-start(bf16[2,256,256]{2,1,0:T(8,128)(2,1)S(1)} %get-tuple-element.130), channel_id=1, source_target_pairs={{0,64},{1,65},{2,66},{3,67},{4,68},{5,69},{6,70},{7,71},{8,72},{9,... | collective-permute-start | bytes 786440 | tf_op jit(solution)/shard_map/ppermute | solution.py:205
  6.8 3.0 %collective-permute-start.5 = (bf16[2,256,256]{2,1,0:T(8,128)(2,1)S(1)}, bf16[2,256,256]{2,1,0:T(8,128)(2,1)S(1)}, u32[]{:S(2)}, u32[]{:S(2)}) collective-permute-start(bf16[2,256,256]{2,1,0:T(8,128)(2,1)S(1)} %get-tuple-element.129), channel_id=1, source_target_pairs={{0,32},{8,40},{16,48},{24,56},{32,0},{40,8},{48,16},{56,24},{64,96... | collective-permute-start | bytes 786440 | tf_op jit(solution)/shard_map/ppermute | solution.py:213
  9.8 0.6 collective-permute-start.4
  10.4 2.6 %collective-permute-start.6 = (bf16[2,256,256]{2,1,0:T(8,128)(2,1)S(1)}, bf16[2,256,256]{2,1,0:T(8,128)(2,1)S(1)}, u32[]{:S(2)}, u32[]{:S(2)}) collective-permute-start(bf16[2,256,256]{2,1,0:T(8,128)(2,1)S(1)} %get-tuple-element.129), channel_id=1, source_target_pairs={{0,48},{8,56},{16,0},{24,8},{32,16},{40,24},{48,32},{56,40},{64,11... | collective-permute-start | bytes 786440 | tf_op jit(solution)/shard_map/ppermute | solution.py:213
  13.4 4.0 %collective-permute-done.5 = bf16[2,256,256]{2,1,0:T(8,128)(2,1)S(1)} collective-permute-done((bf16[2,256,256]{2,1,0:T(8,128)(2,1)S(1)}, bf16[2,256,256]{2,1,0:T(8,128)(2,1)S(1)}, u32[]{:S(2)}, u32[]{:S(2)}) %collective-permute-start.5) | collective-permute-done | bytes 262176 | tf_op jit(solution)/shard_map/ppermute | solution.py:213
  17.4 5.2 %collective-permute-done.4 = bf16[2,256,256]{2,1,0:T(8,128)(2,1)S(1)} collective-permute-done((bf16[2,256,256]{2,1,0:T(8,128)(2,1)S(1)}, bf16[2,256,256]{2,1,0:T(8,128)(2,1)S(1)}, u32[]{:S(2)}, u32[]{:S(2)}) %collective-permute-start.4) | collective-permute-done | bytes 262176 | tf_op jit(solution)/shard_map/ppermute | solution.py:213
  23.3 2.6 %collective-permute-start.9 = (bf16[2,2,256,256]{3,2,1,0:T(8,128)(2,1)S(1)}, bf16[2,2,256,256]{3,2,1,0:T(8,128)(2,1)S(1)}, u32[]{:S(2)}, u32[]{:S(2)}) collective-permute-start(bf16[2,2,256,256]{3,2,1,0:T(8,128)(2,1)S(1)} %pad_maximum_fusion.6), channel_id=1, source_target_pairs={{0,48},{8,56},{16,0},{24,8},{32,16},{40,24},{48,32},{56,40},{64,11... | collective-permute-start | bytes 1572872 | tf_op jit(solution)/shard_map/ppermute | solution.py:213
  25.9 0.9 collective-permute-start.8
  27.5 20.7 %collective-permute-done.9 = bf16[2,2,256,256]{3,2,1,0:T(8,128)(2,1)S(1)} collective-permute-done((bf16[2,2,256,256]{3,2,1,0:T(8,128)(2,1)S(1)}, bf16[2,2,256,256]{3,2,1,0:T(8,128)(2,1)S(1)}, u32[]{:S(2)}, u32[]{:S(2)}) %collective-permute-start.9) | collective-permute-done | bytes 524320 | tf_op jit(solution)/shard_map/ppermute | solution.py:213
  48.3 3.7 %collective-permute-done.7 = bf16[2,2,256,256]{3,2,1,0:T(8,128)(2,1)S(1)} collective-permute-done((bf16[2,2,256,256]{3,2,1,0:T(8,128)(2,1)S(1)}, bf16[2,2,256,256]{3,2,1,0:T(8,128)(2,1)S(1)}, u32[]{:S(2)}, u32[]{:S(2)}) %collective-permute-start.7) | collective-permute-done | bytes 524320 | tf_op jit(solution)/shard_map/ppermute | solution.py:213
  52.3 1.3 copy-done
  53.6 5.2 %shard_map.112 = (bf16[4,2,256,256]{3,2,1,0:T(8,128)(2,1)S(1)}, bf16[4,2,256,256]{3,2,1,0:T(8,128)(2,1)S(1)}, bf16[2,2,256,256]{3,2,1,0:T(8,128)(2,1)S(1)}, bf16...) custom-call(s32[129]{0:T(256)S(1)} %pad_add_fusion.ids, ...), custom_call_target="tpu_custom_call" | custom-call | flops 1073741824 | bytes 16777216 | tf_op jit(solution)/shard_map/pallas_call | solution.py:185
  58.7 2.4 %collective-permute-start.11 = (bf16[4,2,256,256]{3,2,1,0:T(8,128)(2,1)S(1)}, bf16[4,2,256,256]{3,2,1,0:T(8,128)(2,1)S(1)}, u32[]{:S(2)}, u32[]{:S(2)}) collective-permute-start(bf16[4,2,256,256]{3,2,1,0:T(8,128)(2,1)S(1)} %get-tuple-element.61), channel_id=1, source_target_pairs={{0,1},{1,0},{2,3},{3,2},{4,5},{5,4},{6,7},{7,6},{8,9},{9,8},{10,11... | collective-permute-start | bytes 3145736 | tf_op jit(solution)/shard_map/ppermute | solution.py:205
  61.2 2.7 %collective-permute-start.12 = (bf16[2,2,256,256]{3,2,1,0:T(8,128)(2,1)S(1)}, bf16[2,2,256,256]{3,2,1,0:T(8,128)(2,1)S(1)}, u32[]{:S(2)}, u32[]{:S(2)}) collective-permute-start(bf16[2,2,256,256]{3,2,1,0:T(8,128)(2,1)S(1)} %get-tuple-element.63), channel_id=1, source_target_pairs={{0,2},{1,3},{2,4},{3,5},{4,6},{5,7},{6,0},{7,1},{8,10},{9,11},{10,... | collective-permute-start | bytes 1572872 | tf_op jit(solution)/shard_map/ppermute | solution.py:213
  63.9 3.6 %collective-permute-start.13 = (bf16[2,2,256,256]{3,2,1,0:T(8,128)(2,1)S(1)}, bf16[2,2,256,256]{3,2,1,0:T(8,128)(2,1)S(1)}, u32[]{:S(2)}, u32[]{:S(2)}) collective-permute-start(bf16[2,2,256,256]{3,2,1,0:T(8,128)(2,1)S(1)} %get-tuple-element.64), channel_id=1, source_target_pairs={{0,4},{1,5},{2,6},{3,7},{4,0},{5,1},{6,2},{7,3},{8,12},{9,13},{10,... | collective-permute-start | bytes 1572872 | tf_op jit(solution)/shard_map/ppermute | solution.py:213
  67.5 1.0 collective-permute-start.14
  68.5 9.4 %collective-permute-done.12 = bf16[2,2,256,256]{3,2,1,0:T(8,128)(2,1)S(1)} collective-permute-done((bf16[2,2,256,256]{3,2,1,0:T(8,128)(2,1)S(1)}, bf16[2,2,256,256]{3,2,1,0:T(8,128)(2,1)S(1)}, u32[]{:S(2)}, u32[]{:S(2)}) %collective-permute-start.12) | collective-permute-done | bytes 524320 | tf_op jit(solution)/shard_map/ppermute | solution.py:213
  77.9 12.3 %collective-permute-done.13 = bf16[2,2,256,256]{3,2,1,0:T(8,128)(2,1)S(1)} collective-permute-done((bf16[2,2,256,256]{3,2,1,0:T(8,128)(2,1)S(1)}, bf16[2,2,256,256]{3,2,1,0:T(8,128)(2,1)S(1)}, u32[]{:S(2)}, u32[]{:S(2)}) %collective-permute-start.13) | collective-permute-done | bytes 524320 | tf_op jit(solution)/shard_map/ppermute | solution.py:213
  91.3 1.2 collective-permute-start.15
  92.5 2.4 %collective-permute-start.16 = (bf16[2,256,256]{2,1,0:T(8,128)(2,1)S(1)}, bf16[2,256,256]{2,1,0:T(8,128)(2,1)S(1)}, u32[]{:S(2)}, u32[]{:S(2)}) collective-permute-start(bf16[2,256,256]{2,1,0:T(8,128)(2,1)S(1)} %get-tuple-element.68), channel_id=1, source_target_pairs={{0,4},{1,5},{2,6},{3,7},{4,0},{5,1},{6,2},{7,3},{8,12},{9,13},{10,... | collective-permute-start | bytes 786440 | tf_op jit(solution)/shard_map/ppermute | solution.py:213
  94.9 1.2 collective-permute-start.17
  96.2 1.8 collective-permute-done.19
  98.2 1.5 collective-permute-done.15
  99.7 6.7 %collective-permute-done.16 = bf16[2,256,256]{2,1,0:T(8,128)(2,1)S(1)} collective-permute-done((bf16[2,256,256]{2,1,0:T(8,128)(2,1)S(1)}, bf16[2,256,256]{2,1,0:T(8,128)(2,1)S(1)}, u32[]{:S(2)}, u32[]{:S(2)}) %collective-permute-start.16) | collective-permute-done | bytes 262176 | tf_op jit(solution)/shard_map/ppermute | solution.py:213
  106.8 0.8 shard_map.114
  108.1 0.8 shard_map.113
  108.9 0.6 shard_map.115
  110.5 1.0 collective-permute-done.22
  111.9 1.6 collective-permute-start.23
  113.6 1.4 collective-permute-start.26
  114.9 1.6 collective-permute-start.25
  116.6 1.6 collective-permute-start.27
  118.2 6.2 %collective-permute-done.26 = bf16[2,256,256]{2,1,0:T(8,128)(2,1)S(1)} collective-permute-done((bf16[2,256,256]{2,1,0:T(8,128)(2,1)S(1)}, bf16[2,256,256]{2,1,0:T(8,128)(2,1)S(1)}, u32[]{:S(2)}, u32[]{:S(2)}) %collective-permute-start.26) | collective-permute-done | bytes 262176 | tf_op jit(solution)/shard_map/ppermute | solution.py:213
  124.4 4.5 %collective-permute-done.25 = bf16[2,256,256]{2,1,0:T(8,128)(2,1)S(1)} collective-permute-done((bf16[2,256,256]{2,1,0:T(8,128)(2,1)S(1)}, bf16[2,256,256]{2,1,0:T(8,128)(2,1)S(1)}, u32[]{:S(2)}, u32[]{:S(2)}) %collective-permute-start.25) | collective-permute-done | bytes 262176 | tf_op jit(solution)/shard_map/ppermute | solution.py:213
  129.2 0.5 collective-permute-start.31
  129.8 0.8 collective-permute-start.28
  130.6 2.8 %collective-permute-start.29 = (bf16[1104,256]{1,0:T(8,128)(2,1)S(1)}, bf16[1104,256]{1,0:T(8,128)(2,1)S(1)}, u32[]{:S(2)}, u32[]{:S(2)}) collective-permute-start(bf16[1104,256]{1,0:T(8,128)(2,1)S(1)} %get-tuple-element.127), channel_id=1, source_target_pairs={{0,4},{1,5},{2,6},{3,7},{4,0},{5,1},{6,2},{7,3},{8,12},{9,13},{10,... | collective-permute-start | bytes 1695752 | tf_op jit(solution)/shard_map/ppermute | solution.py:213
  133.4 0.5 collective-permute-start.30
  133.9 12.6 %collective-permute-done.28 = bf16[1104,256]{1,0:T(8,128)(2,1)S(1)} collective-permute-done((bf16[1104,256]{1,0:T(8,128)(2,1)S(1)}, bf16[1104,256]{1,0:T(8,128)(2,1)S(1)}, u32[]{:S(2)}, u32[]{:S(2)}) %collective-permute-start.28) | collective-permute-done | bytes 565280 | tf_op jit(solution)/shard_map/ppermute | solution.py:213
  146.6 11.4 %collective-permute-done.29 = bf16[1104,256]{1,0:T(8,128)(2,1)S(1)} collective-permute-done((bf16[1104,256]{1,0:T(8,128)(2,1)S(1)}, bf16[1104,256]{1,0:T(8,128)(2,1)S(1)}, u32[]{:S(2)}, u32[]{:S(2)}) %collective-permute-start.29) | collective-permute-done | bytes 565280 | tf_op jit(solution)/shard_map/ppermute | solution.py:213
  158.9 1.9 collective-permute-start.32
  160.8 5.0 %shard_map.116 = (bf16[4,2,256,256]{3,2,1,0:T(8,128)(2,1)S(1)}, bf16[4,2,256,256]{3,2,1,0:T(8,128)(2,1)S(1)}, bf16[2,2,256,256]{3,2,1,0:T(8,128)(2,1)S(1)}, bf16...) custom-call(s32[129]{0:T(256)S(1)} %pad_add_fusion.ids, ...), custom_call_target="tpu_custom_call" | custom-call | flops 1073741824 | bytes 16777216 | tf_op jit(solution)/shard_map/pallas_call | solution.py:185
  165.9 4.8 %collective-permute-start.35 = (bf16[2128,256]{1,0:T(8,128)(2,1)S(1)}, bf16[2128,256]{1,0:T(8,128)(2,1)S(1)}, u32[]{:S(2)}, u32[]{:S(2)}) collective-permute-start(bf16[2128,256]{1,0:T(8,128)(2,1)S(1)} %pad_maximum_fusion), channel_id=1, source_target_pairs={{0,64},{1,65},{2,66},{3,67},{4,68},{5,69},{6,70},{7,71},{8,72},{9,... | collective-permute-start | bytes 3268616 | tf_op jit(solution)/shard_map/ppermute | solution.py:205
  170.7 0.8 collective-permute-start.36
  171.5 2.6 %collective-permute-start.37 = (bf16[2,2,256,256]{3,2,1,0:T(8,128)(2,1)S(1)}, bf16[2,2,256,256]{3,2,1,0:T(8,128)(2,1)S(1)}, u32[]{:S(2)}, u32[]{:S(2)}) collective-permute-start(bf16[2,2,256,256]{3,2,1,0:T(8,128)(2,1)S(1)} %get-tuple-element.98), channel_id=1, source_target_pairs={{0,32},{8,40},{16,48},{24,56},{32,0},{40,8},{48,16},{56,24},{64,96... | collective-permute-start | bytes 1572872 | tf_op jit(solution)/shard_map/ppermute | solution.py:213
  174.1 2.6 %collective-permute-start.38 = (bf16[2,2,256,256]{3,2,1,0:T(8,128)(2,1)S(1)}, bf16[2,2,256,256]{3,2,1,0:T(8,128)(2,1)S(1)}, u32[]{:S(2)}, u32[]{:S(2)}) collective-permute-start(bf16[2,2,256,256]{3,2,1,0:T(8,128)(2,1)S(1)} %get-tuple-element.99), channel_id=1, source_target_pairs={{0,48},{8,56},{16,0},{24,8},{32,16},{40,24},{48,32},{56,40},{64,11... | collective-permute-start | bytes 1572872 | tf_op jit(solution)/shard_map/ppermute | solution.py:213
  176.7 10.0 %collective-permute-done.36 = bf16[2,2,256,256]{3,2,1,0:T(8,128)(2,1)S(1)} collective-permute-done((bf16[2,2,256,256]{3,2,1,0:T(8,128)(2,1)S(1)}, bf16[2,2,256,256]{3,2,1,0:T(8,128)(2,1)S(1)}, u32[]{:S(2)}, u32[]{:S(2)}) %collective-permute-start.36) | collective-permute-done | bytes 524320 | tf_op jit(solution)/shard_map/ppermute | solution.py:213
  186.7 8.6 %collective-permute-done.37 = bf16[2,2,256,256]{3,2,1,0:T(8,128)(2,1)S(1)} collective-permute-done((bf16[2,2,256,256]{3,2,1,0:T(8,128)(2,1)S(1)}, bf16[2,2,256,256]{3,2,1,0:T(8,128)(2,1)S(1)}, u32[]{:S(2)}, u32[]{:S(2)}) %collective-permute-start.37) | collective-permute-done | bytes 524320 | tf_op jit(solution)/shard_map/ppermute | solution.py:213
  196.5 1.8 collective-permute-start.39
  198.3 2.4 %collective-permute-start.40 = (bf16[2,256,256]{2,1,0:T(8,128)(2,1)S(1)}, bf16[2,256,256]{2,1,0:T(8,128)(2,1)S(1)}, u32[]{:S(2)}, u32[]{:S(2)}) collective-permute-start(bf16[2,256,256]{2,1,0:T(8,128)(2,1)S(1)} %get-tuple-element.102), channel_id=1, source_target_pairs={{0,32},{8,40},{16,48},{24,56},{32,0},{40,8},{48,16},{56,24},{64,96... | collective-permute-start | bytes 786440 | tf_op jit(solution)/shard_map/ppermute | solution.py:213
  200.7 1.6 collective-permute-start.41
  202.4 2.5 %collective-permute-start.43 = (bf16[2,256,256]{2,1,0:T(8,128)(2,1)S(1)}, bf16[2,256,256]{2,1,0:T(8,128)(2,1)S(1)}, u32[]{:S(2)}, u32[]{:S(2)}) collective-permute-start(bf16[2,256,256]{2,1,0:T(8,128)(2,1)S(1)} %get-tuple-element.105), channel_id=1, source_target_pairs={{0,64},{1,65},{2,66},{3,67},{4,68},{5,69},{6,70},{7,71},{8,72},{9,... | collective-permute-start | bytes 786440 | tf_op jit(solution)/shard_map/ppermute | solution.py:205
  204.9 2.8 %collective-permute-done.46 = bf16[2,80,256]{2,1,0:T(8,128)(2,1)S(1)} collective-permute-done((bf16[2,80,256]{2,1,0:T(8,128)(2,1)S(1)}, bf16[2,80,256]{2,1,0:T(8,128)(2,1)S(1)}, u32[]{:S(2)}, u32[]{:S(2)}) %collective-permute-start.46) | collective-permute-done | bytes 81952 | tf_op jit(solution)/shard_map/ppermute | solution.py:205
  207.8 3.8 %collective-permute-start.49 = (bf16[2,2,80,256]{3,2,1,0:T(8,128)(2,1)S(1)}, bf16[2,2,80,256]{3,2,1,0:T(8,128)(2,1)S(1)}, u32[]{:S(2)}, u32[]{:S(2)}) collective-permute-start(bf16[2,2,80,256]{3,2,1,0:T(8,128)(2,1)S(1)} %pad_maximum_fusion.12.own), channel_id=1, source_target_pairs={{0,6},{1,7},{2,0},{3,1},{4,2},{5,3},{6,4},{7,5},{8,14},{9,15},{10,... | collective-permute-start | bytes 491528 | tf_op jit(solution)/shard_map/ppermute | solution.py:213
  211.5 1.4 collective-permute-start.48
  213.0 2.3 %collective-permute-start.47 = (bf16[2,2,80,256]{3,2,1,0:T(8,128)(2,1)S(1)}, bf16[2,2,80,256]{3,2,1,0:T(8,128)(2,1)S(1)}, u32[]{:S(2)}, u32[]{:S(2)}) collective-permute-start(bf16[2,2,80,256]{3,2,1,0:T(8,128)(2,1)S(1)} %pad_maximum_fusion.12.own), channel_id=1, source_target_pairs={{0,2},{1,3},{2,4},{3,5},{4,6},{5,7},{6,0},{7,1},{8,10},{9,11},{10,... | collective-permute-start | bytes 491528 | tf_op jit(solution)/shard_map/ppermute | solution.py:213
  215.6 0.6 collective-permute-start.44
  216.2 0.8 pad_maximum_fusion.7
  217.0 1.5 collective-permute-done.48.moved_2
  218.5 3.4 %collective-permute-done.47.moved_1 = bf16[2,2,80,256]{3,2,1,0:T(8,128)(2,1)S(1)} collective-permute-done((bf16[2,2,80,256]{3,2,1,0:T(8,128)(2,1)S(1)}, bf16[2,2,80,256]{3,2,1,0:T(8,128)(2,1)S(1)}, u32[]{:S(2)}, u32[]{:S(2)}) %collective-permute-start.47) | collective-permute-done | bytes 163872 | tf_op jit(solution)/shard_map/ppermute | solution.py:213
  221.9 1.0 shard_map.118
  222.9 0.8 shard_map.117
  (101 shorter events, 8.2 us)
Async XLA Ops:
  0.6 1.0 copy-start.3
  1.7 25.8 %copy-start.5 = (s32[1,1,64]{2,1,0:T(1,128)S(1)}, s32[1,1,64]{2,1,0:T(1,128)}, u32[]{:S(2)}) copy-start(s32[1,1,64]{2,1,0:T(1,128)} %param.13) | copy-start | bytes 772
  1.7 25.8 %copy-start.6 = (s32[1,1,64]{2,1,0:T(1,128)S(1)}, s32[1,1,64]{2,1,0:T(1,128)}, u32[]{:S(2)}) copy-start(s32[1,1,64]{2,1,0:T(1,128)} %param.14) | copy-start | bytes 772
  1.7 1.6 collective-permute-start.2
  3.4 10.0 %collective-permute-start.3 = (bf16[2,256,256]{2,1,0:T(8,128)(2,1)S(1)}, bf16[2,256,256]{2,1,0:T(8,128)(2,1)S(1)}, u32[]{:S(2)}, u32[]{:S(2)}) collective-permute-start(bf16[2,256,256]{2,1,0:T(8,128)(2,1)S(1)} %get-tuple-element.130), channel_id=1, source_target_pairs={{0,64},{1,65},{2,66},{3,67},{4,68},{5,69},{6,70},{7,71},{8,72},{9,... | collective-permute-start | bytes 786440 | tf_op jit(solution)/shard_map/ppermute | solution.py:205
  6.8 45.5 %collective-permute-start.1 = (bf16[64,128,128]{2,1,0:T(8,128)(2,1)}, bf16[64,128,128]{2,1,0:T(8,128)(2,1)S(1)}, u32[]{:S(2)}, u32[]{:S(2)}) collective-permute-start(bf16[64,128,128]{2,1,0:T(8,128)(2,1)} %bitcast.128), channel_id=1, source_target_pairs={{0,8},{8,0},{16,24},{24,16},{32,40},{40,32},{48,56},{56,48},{64,72... | collective-permute-start | bytes 6291464 | tf_op jit(solution)/shard_map/ppermute | solution.py:200
  6.8 10.7 %collective-permute-start.5 = (bf16[2,256,256]{2,1,0:T(8,128)(2,1)S(1)}, bf16[2,256,256]{2,1,0:T(8,128)(2,1)S(1)}, u32[]{:S(2)}, u32[]{:S(2)}) collective-permute-start(bf16[2,256,256]{2,1,0:T(8,128)(2,1)S(1)} %get-tuple-element.129), channel_id=1, source_target_pairs={{0,32},{8,40},{16,48},{24,56},{32,0},{40,8},{48,16},{56,24},{64,96... | collective-permute-start | bytes 786440 | tf_op jit(solution)/shard_map/ppermute | solution.py:213
  9.8 12.8 %collective-permute-start.4 = (bf16[2,256,256]{2,1,0:T(8,128)(2,1)S(1)}, bf16[2,256,256]{2,1,0:T(8,128)(2,1)S(1)}, u32[]{:S(2)}, u32[]{:S(2)}) collective-permute-start(bf16[2,256,256]{2,1,0:T(8,128)(2,1)S(1)} %get-tuple-element.129), channel_id=1, source_target_pairs={{0,16},{8,24},{16,32},{24,40},{32,48},{40,56},{48,0},{56,8},{64,80... | collective-permute-start | bytes 786440 | tf_op jit(solution)/shard_map/ppermute | solution.py:213
  10.4 12.4 %collective-permute-start.6 = (bf16[2,256,256]{2,1,0:T(8,128)(2,1)S(1)}, bf16[2,256,256]{2,1,0:T(8,128)(2,1)S(1)}, u32[]{:S(2)}, u32[]{:S(2)}) collective-permute-start(bf16[2,256,256]{2,1,0:T(8,128)(2,1)S(1)} %get-tuple-element.129), channel_id=1, source_target_pairs={{0,48},{8,56},{16,0},{24,8},{32,16},{40,24},{48,32},{56,40},{64,11... | collective-permute-start | bytes 786440 | tf_op jit(solution)/shard_map/ppermute | solution.py:213
  22.9 29.1 %collective-permute-start.10 = (bf16[4,2,256,256]{3,2,1,0:T(8,128)(2,1)S(1)}, bf16[4,2,256,256]{3,2,1,0:T(8,128)(2,1)S(1)}, u32[]{:S(2)}, u32[]{:S(2)}) collective-permute-start(bf16[4,2,256,256]{3,2,1,0:T(8,128)(2,1)S(1)} %pad_maximum_fusion.1), channel_id=1, source_target_pairs={{0,64},{1,65},{2,66},{3,67},{4,68},{5,69},{6,70},{7,71},{8,72},{9,... | collective-permute-start | bytes 3145736 | tf_op jit(solution)/shard_map/ppermute | solution.py:205
  23.3 25.0 %collective-permute-start.9 = (bf16[2,2,256,256]{3,2,1,0:T(8,128)(2,1)S(1)}, bf16[2,2,256,256]{3,2,1,0:T(8,128)(2,1)S(1)}, u32[]{:S(2)}, u32[]{:S(2)}) collective-permute-start(bf16[2,2,256,256]{3,2,1,0:T(8,128)(2,1)S(1)} %pad_maximum_fusion.6), channel_id=1, source_target_pairs={{0,48},{8,56},{16,0},{24,8},{32,16},{40,24},{48,32},{56,40},{64,11... | collective-permute-start | bytes 1572872 | tf_op jit(solution)/shard_map/ppermute | solution.py:213
  25.9 22.4 %collective-permute-start.8 = (bf16[2,2,256,256]{3,2,1,0:T(8,128)(2,1)S(1)}, bf16[2,2,256,256]{3,2,1,0:T(8,128)(2,1)S(1)}, u32[]{:S(2)}, u32[]{:S(2)}) collective-permute-start(bf16[2,2,256,256]{3,2,1,0:T(8,128)(2,1)S(1)} %pad_maximum_fusion.6), channel_id=1, source_target_pairs={{0,32},{8,40},{16,48},{24,56},{32,0},{40,8},{48,16},{56,24},{64,96... | collective-permute-start | bytes 1572872 | tf_op jit(solution)/shard_map/ppermute | solution.py:213
  26.8 25.2 %collective-permute-start.7 = (bf16[2,2,256,256]{3,2,1,0:T(8,128)(2,1)S(1)}, bf16[2,2,256,256]{3,2,1,0:T(8,128)(2,1)S(1)}, u32[]{:S(2)}, u32[]{:S(2)}) collective-permute-start(bf16[2,2,256,256]{3,2,1,0:T(8,128)(2,1)S(1)} %pad_maximum_fusion.6), channel_id=1, source_target_pairs={{0,16},{8,24},{16,32},{24,40},{32,48},{40,56},{48,0},{56,8},{64,80... | collective-permute-start | bytes 1572872 | tf_op jit(solution)/shard_map/ppermute | solution.py:213
  48.3 4.0 %collective-permute-start = (s32[129]{0:T(256)S(1)}, s32[129]{0:T(256)S(1)}, u32[]{:S(2)}, u32[]{:S(2)}) collective-permute-start(s32[129]{0:T(256)S(1)} %pad_add_fusion.ids), channel_id=1, source_target_pairs={{0,8},{8,0},{16,24},{24,16},{32,40},{40,32},{48,56},{56,48},{64,72... | collective-permute-start | bytes 1556 | tf_op jit(solution)/shard_map/ppermute | solution.py:200
  52.0 1.6 copy-start
  58.7 31.8 %collective-permute-start.11 = (bf16[4,2,256,256]{3,2,1,0:T(8,128)(2,1)S(1)}, bf16[4,2,256,256]{3,2,1,0:T(8,128)(2,1)S(1)}, u32[]{:S(2)}, u32[]{:S(2)}) collective-permute-start(bf16[4,2,256,256]{3,2,1,0:T(8,128)(2,1)S(1)} %get-tuple-element.61), channel_id=1, source_target_pairs={{0,1},{1,0},{2,3},{3,2},{4,5},{5,4},{6,7},{7,6},{8,9},{9,8},{10,11... | collective-permute-start | bytes 3145736 | tf_op jit(solution)/shard_map/ppermute | solution.py:205
  61.2 16.7 %collective-permute-start.12 = (bf16[2,2,256,256]{3,2,1,0:T(8,128)(2,1)S(1)}, bf16[2,2,256,256]{3,2,1,0:T(8,128)(2,1)S(1)}, u32[]{:S(2)}, u32[]{:S(2)}) collective-permute-start(bf16[2,2,256,256]{3,2,1,0:T(8,128)(2,1)S(1)} %get-tuple-element.63), channel_id=1, source_target_pairs={{0,2},{1,3},{2,4},{3,5},{4,6},{5,7},{6,0},{7,1},{8,10},{9,11},{10,... | collective-permute-start | bytes 1572872 | tf_op jit(solution)/shard_map/ppermute | solution.py:213
  63.9 26.4 %collective-permute-start.13 = (bf16[2,2,256,256]{3,2,1,0:T(8,128)(2,1)S(1)}, bf16[2,2,256,256]{3,2,1,0:T(8,128)(2,1)S(1)}, u32[]{:S(2)}, u32[]{:S(2)}) collective-permute-start(bf16[2,2,256,256]{3,2,1,0:T(8,128)(2,1)S(1)} %get-tuple-element.64), channel_id=1, source_target_pairs={{0,4},{1,5},{2,6},{3,7},{4,0},{5,1},{6,2},{7,3},{8,12},{9,13},{10,... | collective-permute-start | bytes 1572872 | tf_op jit(solution)/shard_map/ppermute | solution.py:213
  67.5 22.8 %collective-permute-start.14 = (bf16[2,2,256,256]{3,2,1,0:T(8,128)(2,1)S(1)}, bf16[2,2,256,256]{3,2,1,0:T(8,128)(2,1)S(1)}, u32[]{:S(2)}, u32[]{:S(2)}) collective-permute-start(bf16[2,2,256,256]{3,2,1,0:T(8,128)(2,1)S(1)} %get-tuple-element.65), channel_id=1, source_target_pairs={{0,6},{1,7},{2,0},{3,1},{4,2},{5,3},{6,4},{7,5},{8,14},{9,15},{10,... | collective-permute-start | bytes 1572872 | tf_op jit(solution)/shard_map/ppermute | solution.py:213
  90.3 16.5 %copy-start.1 = (bf16[512,512]{1,0:T(8,128)(2,1)S(1)}, bf16[512,512]{1,0:T(8,128)(2,1)}, u32[]{:S(2)}) copy-start(bf16[512,512]{1,0:T(8,128)(2,1)} %weight.3) | copy-start | bytes 1572868
  90.3 16.5 %copy-start.2 = (bf16[512,512]{1,0:T(8,128)(2,1)S(1)}, bf16[512,512]{1,0:T(8,128)(2,1)}, u32[]{:S(2)}) copy-start(bf16[512,512]{1,0:T(8,128)(2,1)} %cotangent.3) | copy-start | bytes 1572868
  90.3 16.5 %copy-start.4 = (f32[512]{0:T(512)S(1)}, f32[512]{0:T(512)}, u32[]{:S(2)}) copy-start(f32[512]{0:T(512)} %param.10) | copy-start | bytes 6148
  90.9 7.1 %collective-permute-start.19 = (bf16[2,256,256]{2,1,0:T(8,128)(2,1)S(1)}, bf16[2,256,256]{2,1,0:T(8,128)(2,1)S(1)}, u32[]{:S(2)}, u32[]{:S(2)}) collective-permute-start(bf16[2,256,256]{2,1,0:T(8,128)(2,1)S(1)} %get-tuple-element.72), channel_id=1, source_target_pairs={{0,1},{1,0},{2,3},{3,2},{4,5},{5,4},{6,7},{7,6},{8,9},{9,8},{10,11... | collective-permute-start | bytes 786440 | tf_op jit(solution)/shard_map/ppermute | solution.py:205
  91.3 8.4 %collective-permute-start.15 = (bf16[2,256,256]{2,1,0:T(8,128)(2,1)S(1)}, bf16[2,256,256]{2,1,0:T(8,128)(2,1)S(1)}, u32[]{:S(2)}, u32[]{:S(2)}) collective-permute-start(bf16[2,256,256]{2,1,0:T(8,128)(2,1)S(1)} %get-tuple-element.67), channel_id=1, source_target_pairs={{0,2},{1,3},{2,4},{3,5},{4,6},{5,7},{6,0},{7,1},{8,10},{9,11},{10,... | collective-permute-start | bytes 786440 | tf_op jit(solution)/shard_map/ppermute | solution.py:213
  92.5 13.9 %collective-permute-start.16 = (bf16[2,256,256]{2,1,0:T(8,128)(2,1)S(1)}, bf16[2,256,256]{2,1,0:T(8,128)(2,1)S(1)}, u32[]{:S(2)}, u32[]{:S(2)}) collective-permute-start(bf16[2,256,256]{2,1,0:T(8,128)(2,1)S(1)} %get-tuple-element.68), channel_id=1, source_target_pairs={{0,4},{1,5},{2,6},{3,7},{4,0},{5,1},{6,2},{7,3},{8,12},{9,13},{10,... | collective-permute-start | bytes 786440 | tf_op jit(solution)/shard_map/ppermute | solution.py:213
  94.9 11.5 %collective-permute-start.17 = (bf16[2,256,256]{2,1,0:T(8,128)(2,1)S(1)}, bf16[2,256,256]{2,1,0:T(8,128)(2,1)S(1)}, u32[]{:S(2)}, u32[]{:S(2)}) collective-permute-start(bf16[2,256,256]{2,1,0:T(8,128)(2,1)S(1)} %get-tuple-element.69), channel_id=1, source_target_pairs={{0,6},{1,7},{2,0},{3,1},{4,2},{5,3},{6,4},{7,5},{8,14},{9,15},{10,... | collective-permute-start | bytes 786440 | tf_op jit(solution)/shard_map/ppermute | solution.py:213
  98.1 8.6 %collective-permute-start.20 = (bf16[256,256]{1,0:T(8,128)(2,1)S(1)}, bf16[256,256]{1,0:T(8,128)(2,1)S(1)}, u32[]{:S(2)}, u32[]{:S(2)}) collective-permute-start(bf16[256,256]{1,0:T(8,128)(2,1)S(1)} %get-tuple-element.139), channel_id=1, source_target_pairs={{0,8},{8,0},{16,24},{24,16},{32,40},{40,32},{48,56},{56,48},{64,72... | collective-permute-start | bytes 393224 | tf_op jit(solution)/shard_map/ppermute | solution.py:200
  106.6 1.4 collective-permute-start.18
  109.6 1.9 collective-permute-start.22
  110.0 3.5 %collective-permute-start.24 = (bf16[256,256]{1,0:T(8,128)(2,1)S(1)}, bf16[256,256]{1,0:T(8,128)(2,1)S(1)}, u32[]{:S(2)}, u32[]{:S(2)}) collective-permute-start(bf16[256,256]{1,0:T(8,128)(2,1)S(1)} %get-tuple-element.81), channel_id=1, source_target_pairs={{0,8},{8,0},{16,24},{24,16},{32,40},{40,32},{48,56},{56,48},{64,72... | collective-permute-start | bytes 393224 | tf_op jit(solution)/shard_map/ppermute | solution.py:200
  110.3 1.5 collective-permute-start.21
  111.9 17.1 %collective-permute-start.23 = (bf16[2,416,256]{2,1,0:T(8,128)(2,1)S(1)}, bf16[2,416,256]{2,1,0:T(8,128)(2,1)S(1)}, u32[]{:S(2)}, u32[]{:S(2)}) collective-permute-start(bf16[2,416,256]{2,1,0:T(8,128)(2,1)S(1)} %pad_maximum_fusion.9), channel_id=1, source_target_pairs={{0,1},{1,0},{2,3},{3,2},{4,5},{5,4},{6,7},{7,6},{8,9},{9,8},{10,11... | collective-permute-start | bytes 1277960 | tf_op jit(solution)/shard_map/ppermute | solution.py:205
  113.6 10.8 %collective-permute-start.26 = (bf16[2,256,256]{2,1,0:T(8,128)(2,1)S(1)}, bf16[2,256,256]{2,1,0:T(8,128)(2,1)S(1)}, u32[]{:S(2)}, u32[]{:S(2)}) collective-permute-start(bf16[2,256,256]{2,1,0:T(8,128)(2,1)S(1)} %get-tuple-element.136), channel_id=1, source_target_pairs={{0,4},{1,5},{2,6},{3,7},{4,0},{5,1},{6,2},{7,3},{8,12},{9,13},{10,... | collective-permute-start | bytes 786440 | tf_op jit(solution)/shard_map/ppermute | solution.py:213
  114.9 13.9 %collective-permute-start.25 = (bf16[2,256,256]{2,1,0:T(8,128)(2,1)S(1)}, bf16[2,256,256]{2,1,0:T(8,128)(2,1)S(1)}, u32[]{:S(2)}, u32[]{:S(2)}) collective-permute-start(bf16[2,256,256]{2,1,0:T(8,128)(2,1)S(1)} %get-tuple-element.136), channel_id=1, source_target_pairs={{0,2},{1,3},{2,4},{3,5},{4,6},{5,7},{6,0},{7,1},{8,10},{9,11},{10,... | collective-permute-start | bytes 786440 | tf_op jit(solution)/shard_map/ppermute | solution.py:213
  116.6 12.3 %collective-permute-start.27 = (bf16[2,256,256]{2,1,0:T(8,128)(2,1)S(1)}, bf16[2,256,256]{2,1,0:T(8,128)(2,1)S(1)}, u32[]{:S(2)}, u32[]{:S(2)}) collective-permute-start(bf16[2,256,256]{2,1,0:T(8,128)(2,1)S(1)} %get-tuple-element.136), channel_id=1, source_target_pairs={{0,6},{1,7},{2,0},{3,1},{4,2},{5,3},{6,4},{7,5},{8,14},{9,15},{10,... | collective-permute-start | bytes 786440 | tf_op jit(solution)/shard_map/ppermute | solution.py:213
  129.2 29.2 %collective-permute-start.31 = (bf16[4,2,256,256]{3,2,1,0:T(8,128)(2,1)S(1)}, bf16[4,2,256,256]{3,2,1,0:T(8,128)(2,1)S(1)}, u32[]{:S(2)}, u32[]{:S(2)}) collective-permute-start(bf16[4,2,256,256]{3,2,1,0:T(8,128)(2,1)S(1)} %pad_maximum_fusion.2), channel_id=1, source_target_pairs={{0,1},{1,0},{2,3},{3,2},{4,5},{5,4},{6,7},{7,6},{8,9},{9,8},{10,11... | collective-permute-start | bytes 3145736 | tf_op jit(solution)/shard_map/ppermute | solution.py:205
  129.8 16.7 %collective-permute-start.28 = (bf16[1104,256]{1,0:T(8,128)(2,1)S(1)}, bf16[1104,256]{1,0:T(8,128)(2,1)S(1)}, u32[]{:S(2)}, u32[]{:S(2)}) collective-permute-start(bf16[1104,256]{1,0:T(8,128)(2,1)S(1)} %get-tuple-element.126), channel_id=1, source_target_pairs={{0,2},{1,3},{2,4},{3,5},{4,6},{5,7},{6,0},{7,1},{8,10},{9,11},{10,... | collective-permute-start | bytes 1695752 | tf_op jit(solution)/shard_map/ppermute | solution.py:213
  130.6 27.3 %collective-permute-start.29 = (bf16[1104,256]{1,0:T(8,128)(2,1)S(1)}, bf16[1104,256]{1,0:T(8,128)(2,1)S(1)}, u32[]{:S(2)}, u32[]{:S(2)}) collective-permute-start(bf16[1104,256]{1,0:T(8,128)(2,1)S(1)} %get-tuple-element.127), channel_id=1, source_target_pairs={{0,4},{1,5},{2,6},{3,7},{4,0},{5,1},{6,2},{7,3},{8,12},{9,13},{10,... | collective-permute-start | bytes 1695752 | tf_op jit(solution)/shard_map/ppermute | solution.py:213
  133.4 24.9 %collective-permute-start.30 = (bf16[1104,256]{1,0:T(8,128)(2,1)S(1)}, bf16[1104,256]{1,0:T(8,128)(2,1)S(1)}, u32[]{:S(2)}, u32[]{:S(2)}) collective-permute-start(bf16[1104,256]{1,0:T(8,128)(2,1)S(1)} %get-tuple-element.128), channel_id=1, source_target_pairs={{0,6},{1,7},{2,0},{3,1},{4,2},{5,3},{6,4},{7,5},{8,14},{9,15},{10,... | collective-permute-start | bytes 1695752 | tf_op jit(solution)/shard_map/ppermute | solution.py:213
  158.7 7.1 %collective-permute-start.34 = (bf16[80,256]{1,0:T(8,128)(2,1)S(1)}, bf16[80,256]{1,0:T(8,128)(2,1)S(1)}, u32[]{:S(2)}, u32[]{:S(2)}) collective-permute-start(bf16[80,256]{1,0:T(8,128)(2,1)S(1)} %fusion.17), channel_id=1, source_target_pairs={{0,48},{8,56},{16,0},{24,8},{32,16},{40,24},{48,32},{56,40},{64,11... | collective-permute-start | bytes 122888 | tf_op jit(solution)/shard_map/ppermute | solution.py:213
  158.8 7.0 %collective-permute-start.33 = (bf16[80,256]{1,0:T(8,128)(2,1)S(1)}, bf16[80,256]{1,0:T(8,128)(2,1)S(1)}, u32[]{:S(2)}, u32[]{:S(2)}) collective-permute-start(bf16[80,256]{1,0:T(8,128)(2,1)S(1)} %fusion.17), channel_id=1, source_target_pairs={{0,32},{8,40},{16,48},{24,56},{32,0},{40,8},{48,16},{56,24},{64,96... | collective-permute-start | bytes 122888 | tf_op jit(solution)/shard_map/ppermute | solution.py:213
  158.9 6.9 %collective-permute-start.32 = (bf16[80,256]{1,0:T(8,128)(2,1)S(1)}, bf16[80,256]{1,0:T(8,128)(2,1)S(1)}, u32[]{:S(2)}, u32[]{:S(2)}) collective-permute-start(bf16[80,256]{1,0:T(8,128)(2,1)S(1)} %fusion.17), channel_id=1, source_target_pairs={{0,16},{8,24},{16,32},{24,40},{32,48},{40,56},{48,0},{56,8},{64,80... | collective-permute-start | bytes 122888 | tf_op jit(solution)/shard_map/ppermute | solution.py:213
  165.9 30.1 %collective-permute-start.35 = (bf16[2128,256]{1,0:T(8,128)(2,1)S(1)}, bf16[2128,256]{1,0:T(8,128)(2,1)S(1)}, u32[]{:S(2)}, u32[]{:S(2)}) collective-permute-start(bf16[2128,256]{1,0:T(8,128)(2,1)S(1)} %pad_maximum_fusion), channel_id=1, source_target_pairs={{0,64},{1,65},{2,66},{3,67},{4,68},{5,69},{6,70},{7,71},{8,72},{9,... | collective-permute-start | bytes 3268616 | tf_op jit(solution)/shard_map/ppermute | solution.py:205
  170.7 16.0 %collective-permute-start.36 = (bf16[2,2,256,256]{3,2,1,0:T(8,128)(2,1)S(1)}, bf16[2,2,256,256]{3,2,1,0:T(8,128)(2,1)S(1)}, u32[]{:S(2)}, u32[]{:S(2)}) collective-permute-start(bf16[2,2,256,256]{3,2,1,0:T(8,128)(2,1)S(1)} %get-tuple-element.97), channel_id=1, source_target_pairs={{0,16},{8,24},{16,32},{24,40},{32,48},{40,56},{48,0},{56,8},{64,80... | collective-permute-start | bytes 1572872 | tf_op jit(solution)/shard_map/ppermute | solution.py:213
  171.5 23.7 %collective-permute-start.37 = (bf16[2,2,256,256]{3,2,1,0:T(8,128)(2,1)S(1)}, bf16[2,2,256,256]{3,2,1,0:T(8,128)(2,1)S(1)}, u32[]{:S(2)}, u32[]{:S(2)}) collective-permute-start(bf16[2,2,256,256]{3,2,1,0:T(8,128)(2,1)S(1)} %get-tuple-element.98), channel_id=1, source_target_pairs={{0,32},{8,40},{16,48},{24,56},{32,0},{40,8},{48,16},{56,24},{64,96... | collective-permute-start | bytes 1572872 | tf_op jit(solution)/shard_map/ppermute | solution.py:213
  174.1 21.6 %collective-permute-start.38 = (bf16[2,2,256,256]{3,2,1,0:T(8,128)(2,1)S(1)}, bf16[2,2,256,256]{3,2,1,0:T(8,128)(2,1)S(1)}, u32[]{:S(2)}, u32[]{:S(2)}) collective-permute-start(bf16[2,2,256,256]{3,2,1,0:T(8,128)(2,1)S(1)} %get-tuple-element.99), channel_id=1, source_target_pairs={{0,48},{8,56},{16,0},{24,8},{32,16},{40,24},{48,32},{56,40},{64,11... | collective-permute-start | bytes 1572872 | tf_op jit(solution)/shard_map/ppermute | solution.py:213
  196.0 6.3 %collective-permute-start.45 = (bf16[80,256]{1,0:T(8,128)(2,1)S(1)}, bf16[80,256]{1,0:T(8,128)(2,1)S(1)}, u32[]{:S(2)}, u32[]{:S(2)}) collective-permute-start(bf16[80,256]{1,0:T(8,128)(2,1)S(1)} %add_convert_fusion.12), channel_id=1, source_target_pairs={{0,8},{8,0},{16,24},{24,16},{32,40},{40,32},{48,56},{56,48},{64,72... | collective-permute-start | bytes 122888 | tf_op jit(solution)/shard_map/ppermute | solution.py:200
  196.5 15.0 %collective-permute-start.39 = (bf16[2,256,256]{2,1,0:T(8,128)(2,1)S(1)}, bf16[2,256,256]{2,1,0:T(8,128)(2,1)S(1)}, u32[]{:S(2)}, u32[]{:S(2)}) collective-permute-start(bf16[2,256,256]{2,1,0:T(8,128)(2,1)S(1)} %get-tuple-element.101), channel_id=1, source_target_pairs={{0,16},{8,24},{16,32},{24,40},{32,48},{40,56},{48,0},{56,8},{64,80... | collective-permute-start | bytes 786440 | tf_op jit(solution)/shard_map/ppermute | solution.py:213
  198.3 14.7 %collective-permute-start.40 = (bf16[2,256,256]{2,1,0:T(8,128)(2,1)S(1)}, bf16[2,256,256]{2,1,0:T(8,128)(2,1)S(1)}, u32[]{:S(2)}, u32[]{:S(2)}) collective-permute-start(bf16[2,256,256]{2,1,0:T(8,128)(2,1)S(1)} %get-tuple-element.102), channel_id=1, source_target_pairs={{0,32},{8,40},{16,48},{24,56},{32,0},{40,8},{48,16},{56,24},{64,96... | collective-permute-start | bytes 786440 | tf_op jit(solution)/shard_map/ppermute | solution.py:213
  200.7 14.6 %collective-permute-start.41 = (bf16[2,256,256]{2,1,0:T(8,128)(2,1)S(1)}, bf16[2,256,256]{2,1,0:T(8,128)(2,1)S(1)}, u32[]{:S(2)}, u32[]{:S(2)}) collective-permute-start(bf16[2,256,256]{2,1,0:T(8,128)(2,1)S(1)} %get-tuple-element.103), channel_id=1, source_target_pairs={{0,48},{8,56},{16,0},{24,8},{32,16},{40,24},{48,32},{56,40},{64,11... | collective-permute-start | bytes 786440 | tf_op jit(solution)/shard_map/ppermute | solution.py:213
  202.3 5.4 %collective-permute-start.46 = (bf16[2,80,256]{2,1,0:T(8,128)(2,1)S(1)}, bf16[2,80,256]{2,1,0:T(8,128)(2,1)S(1)}, u32[]{:S(2)}, u32[]{:S(2)}) collective-permute-start(bf16[2,80,256]{2,1,0:T(8,128)(2,1)S(1)} %get-tuple-element.145), channel_id=1, source_target_pairs={{0,1},{1,0},{2,3},{3,2},{4,5},{5,4},{6,7},{7,6},{8,9},{9,8},{10,11... | collective-permute-start | bytes 245768 | tf_op jit(solution)/shard_map/ppermute | solution.py:205
  202.4 13.1 %collective-permute-start.43 = (bf16[2,256,256]{2,1,0:T(8,128)(2,1)S(1)}, bf16[2,256,256]{2,1,0:T(8,128)(2,1)S(1)}, u32[]{:S(2)}, u32[]{:S(2)}) collective-permute-start(bf16[2,256,256]{2,1,0:T(8,128)(2,1)S(1)} %get-tuple-element.105), channel_id=1, source_target_pairs={{0,64},{1,65},{2,66},{3,67},{4,68},{5,69},{6,70},{7,71},{8,72},{9,... | collective-permute-start | bytes 786440 | tf_op jit(solution)/shard_map/ppermute | solution.py:205
  207.8 9.2 %collective-permute-start.49 = (bf16[2,2,80,256]{3,2,1,0:T(8,128)(2,1)S(1)}, bf16[2,2,80,256]{3,2,1,0:T(8,128)(2,1)S(1)}, u32[]{:S(2)}, u32[]{:S(2)}) collective-permute-start(bf16[2,2,80,256]{3,2,1,0:T(8,128)(2,1)S(1)} %pad_maximum_fusion.12.own), channel_id=1, source_target_pairs={{0,6},{1,7},{2,0},{3,1},{4,2},{5,3},{6,4},{7,5},{8,14},{9,15},{10,... | collective-permute-start | bytes 491528 | tf_op jit(solution)/shard_map/ppermute | solution.py:213
  211.5 6.9 %collective-permute-start.48 = (bf16[2,2,80,256]{3,2,1,0:T(8,128)(2,1)S(1)}, bf16[2,2,80,256]{3,2,1,0:T(8,128)(2,1)S(1)}, u32[]{:S(2)}, u32[]{:S(2)}) collective-permute-start(bf16[2,2,80,256]{3,2,1,0:T(8,128)(2,1)S(1)} %pad_maximum_fusion.12.own), channel_id=1, source_target_pairs={{0,4},{1,5},{2,6},{3,7},{4,0},{5,1},{6,2},{7,3},{8,12},{9,13},{10,... | collective-permute-start | bytes 491528 | tf_op jit(solution)/shard_map/ppermute | solution.py:213
  213.0 8.9 %collective-permute-start.47 = (bf16[2,2,80,256]{3,2,1,0:T(8,128)(2,1)S(1)}, bf16[2,2,80,256]{3,2,1,0:T(8,128)(2,1)S(1)}, u32[]{:S(2)}, u32[]{:S(2)}) collective-permute-start(bf16[2,2,80,256]{3,2,1,0:T(8,128)(2,1)S(1)} %pad_maximum_fusion.12.own), channel_id=1, source_target_pairs={{0,2},{1,3},{2,4},{3,5},{4,6},{5,7},{6,0},{7,1},{8,10},{9,11},{10,... | collective-permute-start | bytes 491528 | tf_op jit(solution)/shard_map/ppermute | solution.py:213
  215.4 7.5 %collective-permute-start.42 = (bf16[256,256]{1,0:T(8,128)(2,1)S(1)}, bf16[256,256]{1,0:T(8,128)(2,1)S(1)}, u32[]{:S(2)}, u32[]{:S(2)}) collective-permute-start(bf16[256,256]{1,0:T(8,128)(2,1)S(1)} %get-tuple-element.133), channel_id=1, source_target_pairs={{0,8},{8,0},{16,24},{24,16},{32,40},{40,32},{48,56},{56,48},{64,72... | collective-permute-start | bytes 393224 | tf_op jit(solution)/shard_map/ppermute | solution.py:200
  215.6 7.3 %collective-permute-start.44 = (bf16[256,256]{1,0:T(8,128)(2,1)S(1)}, bf16[256,256]{1,0:T(8,128)(2,1)S(1)}, u32[]{:S(2)}, u32[]{:S(2)}) collective-permute-start(bf16[256,256]{1,0:T(8,128)(2,1)S(1)} %get-tuple-element.131), channel_id=1, source_target_pairs={{0,8},{8,0},{16,24},{24,16},{32,40},{40,32},{48,56},{56,48},{64,72... | collective-permute-start | bytes 393224 | tf_op jit(solution)/shard_map/ppermute | solution.py:200

commit v7 on v6

--- a/solution.py
+++ b/solution.py
@@ -158,8 +158,8 @@
         for y in range(2):
             for far in range(2):
                 at = share_rows(lax.rem(core + far, 2), lax.rem(col // 2 + 4 - d, 4), lax.rem(col + y, 2))
-                weight_grad[at, :HALF] = piece[y, far, :SHARE, :].astype(F32)
-                weight_grad[at, HALF:] = piece[y, far, SHARE : 2 * SHARE, :].astype(F32)
+                weight_grad[at, :HALF] = piece[far, y, :SHARE, :].astype(F32)
+                weight_grad[at, HALF:] = piece[far, y, SHARE : 2 * SHARE, :].astype(F32)
     bias_grad[:, :HALF] = own[0, 0, 2 * SHARE : 2 * SHARE + 1, :].astype(F32)
     bias_grad[:, HALF:] = own[0, 0, 2 * SHARE + 1 : 2 * SHARE + 2, :].astype(F32)
 
@@ -322,8 +322,8 @@
     parts = multiply(True, source)
     chunk, parts = lax.optimization_barrier((add(*ring(chunk, "row")), parts))
     first, rest, chunk = two_way_scatter(parts, "row", chunk)
-    chunks = jnp.stack([chunk, core_swap(chunk)])
-    chunks = jnp.stack([chunks, swap_y(chunks, 0, 1)])
+    chunks = jnp.stack([chunk, swap_y(chunk, 0, 1)])
+    chunks = jnp.stack([chunks, core_swap(chunks)])
     weight_grad, bias_grad = call(place_kernel, ring(chunks, "col"), [((512, 512), F32), ((1, 512), F32)])
     (feature_grad,) = call(final_kernel, (*first, *rest), [((512, 512), BF)])
     return (output, feature_grad, weight_grad, bias_grad.reshape(512))

time: 224 us -> 221 us (0.987)
  starting transfers between devices: 70.1 us -> 63.2 us
  Pallas kernels: 14.3 us -> 17.4 us
    ppermute x9, starting transfers between devices: 16.3 us -> 10.1 us  [swap_y(): return lax.ppermute(value, ('row', 'col'), to)]
    ppermute x30, waiting for transfers between devices: 123 us -> 126 us  [shift(): return lax.ppermute(value, axis, to)]
    pallas_call x8, Pallas kernels: 14.3 us -> 17.4 us  [call(): pl.pallas_call(kernel, grid_spec=pltpu.PrefetchScalarGridSpec(num_scalar_...]
  transfers between devices with their start and end apart: 50 -> 50, of which waited for: 27 -> 26; matrix products, arithmetic and copies ran while one was open for 2% -> 2% of each run, Pallas kernels for 3% -> 4%
where the time goes in v7:
time: 221 us; the launch traced here: 222 us
  waiting for transfers between devices  133 us (60%)
  starting transfers between devices  63.2 us (29%)
  Pallas kernels  17.4 us (8%)
  other arithmetic  4.01 us (2%)
  local copies, waits for them, and re-layouts  2.69 us (1%)
    ppermute x30, waiting for transfers between devices, shift(): return lax.ppermute(value, axis, to)  126 us
    ppermute x30, starting transfers between devices, shift(): return lax.ppermute(value, axis, to)  51.2 us
    pallas_call x8, Pallas kernels, call(): pl.pallas_call(kernel, grid_spec=pltpu.PrefetchScalarGridSpec(num_scalar_...  17.4 us
    ppermute x9, starting transfers between devices, swap_y(): return lax.ppermute(value, ('row', 'col'), to)  10.1 us
  transfers between devices with their start and end apart: 50, of which 26 were waited for; matrix products, arithmetic and copies ran while one was open for 2% of the time, Pallas kernels for 4%

profile of v7, /device:TPU:0, one launch (start us, length us, event | category | flops | bytes accessed | tf_op | source)
XLA Modules:
  0.0 221.6 jit_solution(270973239552493809)
XLA Ops:
  0.6 1.0 copy-done.3
  1.8 1.5 collective-permute-done.2
  3.4 3.4 %collective-permute-start.3 = (bf16[2,256,256]{2,1,0:T(8,128)(2,1)S(1)}, bf16[2,256,256]{2,1,0:T(8,128)(2,1)S(1)}, u32[]{:S(2)}, u32[]{:S(2)}) collective-permute-start(bf16[2,256,256]{2,1,0:T(8,128)(2,1)S(1)} %get-tuple-element.130), channel_id=1, source_target_pairs={{0,64},{1,65},{2,66},{3,67},{4,68},{5,69},{6,70},{7,71},{8,72},{9,... | collective-permute-start | bytes 786440 | tf_op jit(solution)/shard_map/ppermute | solution.py:205
  6.8 3.0 %collective-permute-start.5 = (bf16[2,256,256]{2,1,0:T(8,128)(2,1)S(1)}, bf16[2,256,256]{2,1,0:T(8,128)(2,1)S(1)}, u32[]{:S(2)}, u32[]{:S(2)}) collective-permute-start(bf16[2,256,256]{2,1,0:T(8,128)(2,1)S(1)} %get-tuple-element.129), channel_id=1, source_target_pairs={{0,32},{8,40},{16,48},{24,56},{32,0},{40,8},{48,16},{56,24},{64,96... | collective-permute-start | bytes 786440 | tf_op jit(solution)/shard_map/ppermute | solution.py:213
  9.8 0.6 collective-permute-start.4
  10.4 2.6 %collective-permute-start.6 = (bf16[2,256,256]{2,1,0:T(8,128)(2,1)S(1)}, bf16[2,256,256]{2,1,0:T(8,128)(2,1)S(1)}, u32[]{:S(2)}, u32[]{:S(2)}) collective-permute-start(bf16[2,256,256]{2,1,0:T(8,128)(2,1)S(1)} %get-tuple-element.129), channel_id=1, source_target_pairs={{0,48},{8,56},{16,0},{24,8},{32,16},{40,24},{48,32},{56,40},{64,11... | collective-permute-start | bytes 786440 | tf_op jit(solution)/shard_map/ppermute | solution.py:213
  13.4 4.0 %collective-permute-done.5 = bf16[2,256,256]{2,1,0:T(8,128)(2,1)S(1)} collective-permute-done((bf16[2,256,256]{2,1,0:T(8,128)(2,1)S(1)}, bf16[2,256,256]{2,1,0:T(8,128)(2,1)S(1)}, u32[]{:S(2)}, u32[]{:S(2)}) %collective-permute-start.5) | collective-permute-done | bytes 262176 | tf_op jit(solution)/shard_map/ppermute | solution.py:213
  17.4 5.2 %collective-permute-done.4 = bf16[2,256,256]{2,1,0:T(8,128)(2,1)S(1)} collective-permute-done((bf16[2,256,256]{2,1,0:T(8,128)(2,1)S(1)}, bf16[2,256,256]{2,1,0:T(8,128)(2,1)S(1)}, u32[]{:S(2)}, u32[]{:S(2)}) %collective-permute-start.4) | collective-permute-done | bytes 262176 | tf_op jit(solution)/shard_map/ppermute | solution.py:213
  23.3 2.6 %collective-permute-start.9 = (bf16[2,2,256,256]{3,2,1,0:T(8,128)(2,1)S(1)}, bf16[2,2,256,256]{3,2,1,0:T(8,128)(2,1)S(1)}, u32[]{:S(2)}, u32[]{:S(2)}) collective-permute-start(bf16[2,2,256,256]{3,2,1,0:T(8,128)(2,1)S(1)} %pad_maximum_fusion.6), channel_id=1, source_target_pairs={{0,48},{8,56},{16,0},{24,8},{32,16},{40,24},{48,32},{56,40},{64,11... | collective-permute-start | bytes 1572872 | tf_op jit(solution)/shard_map/ppermute | solution.py:213
  25.9 0.9 collective-permute-start.8
  27.5 20.7 %collective-permute-done.9 = bf16[2,2,256,256]{3,2,1,0:T(8,128)(2,1)S(1)} collective-permute-done((bf16[2,2,256,256]{3,2,1,0:T(8,128)(2,1)S(1)}, bf16[2,2,256,256]{3,2,1,0:T(8,128)(2,1)S(1)}, u32[]{:S(2)}, u32[]{:S(2)}) %collective-permute-start.9) | collective-permute-done | bytes 524320 | tf_op jit(solution)/shard_map/ppermute | solution.py:213
  48.3 3.7 %collective-permute-done.7 = bf16[2,2,256,256]{3,2,1,0:T(8,128)(2,1)S(1)} collective-permute-done((bf16[2,2,256,256]{3,2,1,0:T(8,128)(2,1)S(1)}, bf16[2,2,256,256]{3,2,1,0:T(8,128)(2,1)S(1)}, u32[]{:S(2)}, u32[]{:S(2)}) %collective-permute-start.7) | collective-permute-done | bytes 524320 | tf_op jit(solution)/shard_map/ppermute | solution.py:213
  52.3 1.3 copy-done
  53.6 6.8 %shard_map.112 = (bf16[4,2,256,256]{3,2,1,0:T(8,128)(2,1)S(1)}, bf16[4,2,256,256]{3,2,1,0:T(8,128)(2,1)S(1)}, bf16[2,2,256,256]{3,2,1,0:T(8,128)(2,1)S(1)}, bf16...) custom-call(s32[129]{0:T(256)S(1)} %pad_add_fusion.ids, ...), custom_call_target="tpu_custom_call" | custom-call | flops 1073741824 | bytes 16777216 | tf_op jit(solution)/shard_map/pallas_call | solution.py:185
  60.3 0.8 collective-permute-start.11
  61.2 1.1 collective-permute-start.12
  62.3 4.4 %collective-permute-start.13 = (bf16[2,2,256,256]{3,2,1,0:T(8,128)(2,1)S(1)}, bf16[2,2,256,256]{3,2,1,0:T(8,128)(2,1)S(1)}, u32[]{:S(2)}, u32[]{:S(2)}) collective-permute-start(bf16[2,2,256,256]{3,2,1,0:T(8,128)(2,1)S(1)} %get-tuple-element.64), channel_id=1, source_target_pairs={{0,4},{1,5},{2,6},{3,7},{4,0},{5,1},{6,2},{7,3},{8,12},{9,13},{10,... | collective-permute-start | bytes 1572872 | tf_op jit(solution)/shard_map/ppermute | solution.py:213
  66.9 10.2 %collective-permute-done.12 = bf16[2,2,256,256]{3,2,1,0:T(8,128)(2,1)S(1)} collective-permute-done((bf16[2,2,256,256]{3,2,1,0:T(8,128)(2,1)S(1)}, bf16[2,2,256,256]{3,2,1,0:T(8,128)(2,1)S(1)}, u32[]{:S(2)}, u32[]{:S(2)}) %collective-permute-start.12) | collective-permute-done | bytes 524320 | tf_op jit(solution)/shard_map/ppermute | solution.py:213
  77.1 12.3 %collective-permute-done.13 = bf16[2,2,256,256]{3,2,1,0:T(8,128)(2,1)S(1)} collective-permute-done((bf16[2,2,256,256]{3,2,1,0:T(8,128)(2,1)S(1)}, bf16[2,2,256,256]{3,2,1,0:T(8,128)(2,1)S(1)}, u32[]{:S(2)}, u32[]{:S(2)}) %collective-permute-start.13) | collective-permute-done | bytes 524320 | tf_op jit(solution)/shard_map/ppermute | solution.py:213
  90.1 0.4 collective-permute-start.19
  90.5 0.9 collective-permute-start.15
  91.4 2.7 %collective-permute-start.16 = (bf16[2,256,256]{2,1,0:T(8,128)(2,1)S(1)}, bf16[2,256,256]{2,1,0:T(8,128)(2,1)S(1)}, u32[]{:S(2)}, u32[]{:S(2)}) collective-permute-start(bf16[2,256,256]{2,1,0:T(8,128)(2,1)S(1)} %get-tuple-element.68), channel_id=1, source_target_pairs={{0,4},{1,5},{2,6},{3,7},{4,0},{5,1},{6,2},{7,3},{8,12},{9,13},{10,... | collective-permute-start | bytes 786440 | tf_op jit(solution)/shard_map/ppermute | solution.py:213
  94.1 0.5 collective-permute-start.17
  94.7 2.5 %collective-permute-done.19 = bf16[2,256,256]{2,1,0:T(8,128)(2,1)S(1)} collective-permute-done((bf16[2,256,256]{2,1,0:T(8,128)(2,1)S(1)}, bf16[2,256,256]{2,1,0:T(8,128)(2,1)S(1)}, u32[]{:S(2)}, u32[]{:S(2)}) %collective-permute-start.19) | collective-permute-done | bytes 262176 | tf_op jit(solution)/shard_map/ppermute | solution.py:205
  97.4 1.6 collective-permute-done.15
  98.9 6.7 %collective-permute-done.16 = bf16[2,256,256]{2,1,0:T(8,128)(2,1)S(1)} collective-permute-done((bf16[2,256,256]{2,1,0:T(8,128)(2,1)S(1)}, bf16[2,256,256]{2,1,0:T(8,128)(2,1)S(1)}, u32[]{:S(2)}, u32[]{:S(2)}) %collective-permute-start.16) | collective-permute-done | bytes 262176 | tf_op jit(solution)/shard_map/ppermute | solution.py:213
  106.0 0.8 shard_map.114
  106.8 0.5 collective-permute-done.18.other
  107.3 0.8 shard_map.113
  108.1 0.6 shard_map.115
  109.7 1.0 collective-permute-done.22
  111.0 1.7 collective-permute-start.23
  112.7 1.5 collective-permute-start.26
  114.2 1.5 collective-permute-start.25
  115.7 1.7 collective-permute-start.27
  117.5 6.1 %collective-permute-done.26 = bf16[2,256,256]{2,1,0:T(8,128)(2,1)S(1)} collective-permute-done((bf16[2,256,256]{2,1,0:T(8,128)(2,1)S(1)}, bf16[2,256,256]{2,1,0:T(8,128)(2,1)S(1)}, u32[]{:S(2)}, u32[]{:S(2)}) %collective-permute-start.26) | collective-permute-done | bytes 262176 | tf_op jit(solution)/shard_map/ppermute | solution.py:213
  123.6 4.5 %collective-permute-done.25 = bf16[2,256,256]{2,1,0:T(8,128)(2,1)S(1)} collective-permute-done((bf16[2,256,256]{2,1,0:T(8,128)(2,1)S(1)}, bf16[2,256,256]{2,1,0:T(8,128)(2,1)S(1)}, u32[]{:S(2)}, u32[]{:S(2)}) %collective-permute-start.25) | collective-permute-done | bytes 262176 | tf_op jit(solution)/shard_map/ppermute | solution.py:213
  128.4 0.5 collective-permute-start.31
  129.0 0.9 collective-permute-start.28
  129.9 2.7 %collective-permute-start.29 = (bf16[1104,256]{1,0:T(8,128)(2,1)S(1)}, bf16[1104,256]{1,0:T(8,128)(2,1)S(1)}, u32[]{:S(2)}, u32[]{:S(2)}) collective-permute-start(bf16[1104,256]{1,0:T(8,128)(2,1)S(1)} %get-tuple-element.127), channel_id=1, source_target_pairs={{0,4},{1,5},{2,6},{3,7},{4,0},{5,1},{6,2},{7,3},{8,12},{9,13},{10,... | collective-permute-start | bytes 1695752 | tf_op jit(solution)/shard_map/ppermute | solution.py:213
  132.6 0.6 collective-permute-start.30
  133.1 12.5 %collective-permute-done.28 = bf16[1104,256]{1,0:T(8,128)(2,1)S(1)} collective-permute-done((bf16[1104,256]{1,0:T(8,128)(2,1)S(1)}, bf16[1104,256]{1,0:T(8,128)(2,1)S(1)}, u32[]{:S(2)}, u32[]{:S(2)}) %collective-permute-start.28) | collective-permute-done | bytes 565280 | tf_op jit(solution)/shard_map/ppermute | solution.py:213
  145.7 11.4 %collective-permute-done.29 = bf16[1104,256]{1,0:T(8,128)(2,1)S(1)} collective-permute-done((bf16[1104,256]{1,0:T(8,128)(2,1)S(1)}, bf16[1104,256]{1,0:T(8,128)(2,1)S(1)}, u32[]{:S(2)}, u32[]{:S(2)}) %collective-permute-start.29) | collective-permute-done | bytes 565280 | tf_op jit(solution)/shard_map/ppermute | solution.py:213
  157.9 1.4 collective-permute-start.34
  159.7 1.3 collective-permute-start.32
  161.0 6.5 %shard_map.116 = (bf16[4,2,256,256]{3,2,1,0:T(8,128)(2,1)S(1)}, bf16[4,2,256,256]{3,2,1,0:T(8,128)(2,1)S(1)}, bf16[2,2,256,256]{3,2,1,0:T(8,128)(2,1)S(1)}, bf16...) custom-call(s32[129]{0:T(256)S(1)} %pad_add_fusion.ids, ...), custom_call_target="tpu_custom_call" | custom-call | flops 1073741824 | bytes 16777216 | tf_op jit(solution)/shard_map/pallas_call | solution.py:185
  167.7 1.7 collective-permute-start.35
  169.4 3.3 %collective-permute-start.36 = (bf16[2,2,256,256]{3,2,1,0:T(8,128)(2,1)S(1)}, bf16[2,2,256,256]{3,2,1,0:T(8,128)(2,1)S(1)}, u32[]{:S(2)}, u32[]{:S(2)}) collective-permute-start(bf16[2,2,256,256]{3,2,1,0:T(8,128)(2,1)S(1)} %get-tuple-element.97), channel_id=1, source_target_pairs={{0,16},{8,24},{16,32},{24,40},{32,48},{40,56},{48,0},{56,8},{64,80... | collective-permute-start | bytes 1572872 | tf_op jit(solution)/shard_map/ppermute | solution.py:213
  172.7 2.2 collective-permute-start.37
  174.9 2.6 %collective-permute-start.38 = (bf16[2,2,256,256]{3,2,1,0:T(8,128)(2,1)S(1)}, bf16[2,2,256,256]{3,2,1,0:T(8,128)(2,1)S(1)}, u32[]{:S(2)}, u32[]{:S(2)}) collective-permute-start(bf16[2,2,256,256]{3,2,1,0:T(8,128)(2,1)S(1)} %get-tuple-element.99), channel_id=1, source_target_pairs={{0,48},{8,56},{16,0},{24,8},{32,16},{40,24},{48,32},{56,40},{64,11... | collective-permute-start | bytes 1572872 | tf_op jit(solution)/shard_map/ppermute | solution.py:213
  177.5 7.6 %collective-permute-done.36 = bf16[2,2,256,256]{3,2,1,0:T(8,128)(2,1)S(1)} collective-permute-done((bf16[2,2,256,256]{3,2,1,0:T(8,128)(2,1)S(1)}, bf16[2,2,256,256]{3,2,1,0:T(8,128)(2,1)S(1)}, u32[]{:S(2)}, u32[]{:S(2)}) %collective-permute-start.36) | collective-permute-done | bytes 524320 | tf_op jit(solution)/shard_map/ppermute | solution.py:213
  185.0 11.0 %collective-permute-done.37 = bf16[2,2,256,256]{3,2,1,0:T(8,128)(2,1)S(1)} collective-permute-done((bf16[2,2,256,256]{3,2,1,0:T(8,128)(2,1)S(1)}, bf16[2,2,256,256]{3,2,1,0:T(8,128)(2,1)S(1)}, u32[]{:S(2)}, u32[]{:S(2)}) %collective-permute-start.37) | collective-permute-done | bytes 524320 | tf_op jit(solution)/shard_map/ppermute | solution.py:213
  196.8 1.5 collective-permute-start.39
  198.3 2.4 %collective-permute-start.40 = (bf16[2,256,256]{2,1,0:T(8,128)(2,1)S(1)}, bf16[2,256,256]{2,1,0:T(8,128)(2,1)S(1)}, u32[]{:S(2)}, u32[]{:S(2)}) collective-permute-start(bf16[2,256,256]{2,1,0:T(8,128)(2,1)S(1)} %get-tuple-element.102), channel_id=1, source_target_pairs={{0,32},{8,40},{16,48},{24,56},{32,0},{40,8},{48,16},{56,24},{64,96... | collective-permute-start | bytes 786440 | tf_op jit(solution)/shard_map/ppermute | solution.py:213
  200.7 2.4 %collective-permute-start.41 = (bf16[2,256,256]{2,1,0:T(8,128)(2,1)S(1)}, bf16[2,256,256]{2,1,0:T(8,128)(2,1)S(1)}, u32[]{:S(2)}, u32[]{:S(2)}) collective-permute-start(bf16[2,256,256]{2,1,0:T(8,128)(2,1)S(1)} %get-tuple-element.103), channel_id=1, source_target_pairs={{0,48},{8,56},{16,0},{24,8},{32,16},{40,24},{48,32},{56,40},{64,11... | collective-permute-start | bytes 786440 | tf_op jit(solution)/shard_map/ppermute | solution.py:213
  203.2 1.1 collective-permute-start.43
  204.5 3.8 %collective-permute-start.49 = (bf16[2,2,80,256]{3,2,1,0:T(8,128)(2,1)S(1)}, bf16[2,2,80,256]{3,2,1,0:T(8,128)(2,1)S(1)}, u32[]{:S(2)}, u32[]{:S(2)}) collective-permute-start(bf16[2,2,80,256]{3,2,1,0:T(8,128)(2,1)S(1)} %pad_maximum_fusion.12.own), channel_id=1, source_target_pairs={{0,6},{1,7},{2,0},{3,1},{4,2},{5,3},{6,4},{7,5},{8,14},{9,15},{10,... | collective-permute-start | bytes 491528 | tf_op jit(solution)/shard_map/ppermute | solution.py:213
  208.2 4.3 %collective-permute-done.40 = bf16[2,256,256]{2,1,0:T(8,128)(2,1)S(1)} collective-permute-done((bf16[2,256,256]{2,1,0:T(8,128)(2,1)S(1)}, bf16[2,256,256]{2,1,0:T(8,128)(2,1)S(1)}, u32[]{:S(2)}, u32[]{:S(2)}) %collective-permute-start.40) | collective-permute-done | bytes 262176 | tf_op jit(solution)/shard_map/ppermute | solution.py:213
  212.5 1.4 collective-permute-start.47
  214.2 0.6 collective-permute-start.44
  214.8 0.8 pad_maximum_fusion.7
  215.7 4.0 %collective-permute-done.47.moved_1 = bf16[2,2,80,256]{3,2,1,0:T(8,128)(2,1)S(1)} collective-permute-done((bf16[2,2,80,256]{3,2,1,0:T(8,128)(2,1)S(1)}, bf16[2,2,80,256]{3,2,1,0:T(8,128)(2,1)S(1)}, u32[]{:S(2)}, u32[]{:S(2)}) %collective-permute-start.47) | collective-permute-done | bytes 163872 | tf_op jit(solution)/shard_map/ppermute | solution.py:213
  219.7 1.0 shard_map.118
  220.8 0.8 shard_map.117
  (101 shorter events, 7.5 us)
Async XLA Ops:
  0.6 1.0 copy-start.3
  1.7 25.8 %copy-start.5 = (s32[1,1,64]{2,1,0:T(1,128)S(1)}, s32[1,1,64]{2,1,0:T(1,128)}, u32[]{:S(2)}) copy-start(s32[1,1,64]{2,1,0:T(1,128)} %param.13) | copy-start | bytes 772
  1.7 25.8 %copy-start.6 = (s32[1,1,64]{2,1,0:T(1,128)S(1)}, s32[1,1,64]{2,1,0:T(1,128)}, u32[]{:S(2)}) copy-start(s32[1,1,64]{2,1,0:T(1,128)} %param.14) | copy-start | bytes 772
  1.7 1.6 collective-permute-start.2
  3.4 10.0 %collective-permute-start.3 = (bf16[2,256,256]{2,1,0:T(8,128)(2,1)S(1)}, bf16[2,256,256]{2,1,0:T(8,128)(2,1)S(1)}, u32[]{:S(2)}, u32[]{:S(2)}) collective-permute-start(bf16[2,256,256]{2,1,0:T(8,128)(2,1)S(1)} %get-tuple-element.130), channel_id=1, source_target_pairs={{0,64},{1,65},{2,66},{3,67},{4,68},{5,69},{6,70},{7,71},{8,72},{9,... | collective-permute-start | bytes 786440 | tf_op jit(solution)/shard_map/ppermute | solution.py:205
  6.8 45.5 %collective-permute-start.1 = (bf16[64,128,128]{2,1,0:T(8,128)(2,1)}, bf16[64,128,128]{2,1,0:T(8,128)(2,1)S(1)}, u32[]{:S(2)}, u32[]{:S(2)}) collective-permute-start(bf16[64,128,128]{2,1,0:T(8,128)(2,1)} %bitcast.128), channel_id=1, source_target_pairs={{0,8},{8,0},{16,24},{24,16},{32,40},{40,32},{48,56},{56,48},{64,72... | collective-permute-start | bytes 6291464 | tf_op jit(solution)/shard_map/ppermute | solution.py:200
  6.8 10.7 %collective-permute-start.5 = (bf16[2,256,256]{2,1,0:T(8,128)(2,1)S(1)}, bf16[2,256,256]{2,1,0:T(8,128)(2,1)S(1)}, u32[]{:S(2)}, u32[]{:S(2)}) collective-permute-start(bf16[2,256,256]{2,1,0:T(8,128)(2,1)S(1)} %get-tuple-element.129), channel_id=1, source_target_pairs={{0,32},{8,40},{16,48},{24,56},{32,0},{40,8},{48,16},{56,24},{64,96... | collective-permute-start | bytes 786440 | tf_op jit(solution)/shard_map/ppermute | solution.py:213
  9.8 12.8 %collective-permute-start.4 = (bf16[2,256,256]{2,1,0:T(8,128)(2,1)S(1)}, bf16[2,256,256]{2,1,0:T(8,128)(2,1)S(1)}, u32[]{:S(2)}, u32[]{:S(2)}) collective-permute-start(bf16[2,256,256]{2,1,0:T(8,128)(2,1)S(1)} %get-tuple-element.129), channel_id=1, source_target_pairs={{0,16},{8,24},{16,32},{24,40},{32,48},{40,56},{48,0},{56,8},{64,80... | collective-permute-start | bytes 786440 | tf_op jit(solution)/shard_map/ppermute | solution.py:213
  10.4 12.4 %collective-permute-start.6 = (bf16[2,256,256]{2,1,0:T(8,128)(2,1)S(1)}, bf16[2,256,256]{2,1,0:T(8,128)(2,1)S(1)}, u32[]{:S(2)}, u32[]{:S(2)}) collective-permute-start(bf16[2,256,256]{2,1,0:T(8,128)(2,1)S(1)} %get-tuple-element.129), channel_id=1, source_target_pairs={{0,48},{8,56},{16,0},{24,8},{32,16},{40,24},{48,32},{56,40},{64,11... | collective-permute-start | bytes 786440 | tf_op jit(solution)/shard_map/ppermute | solution.py:213
  22.9 29.1 %collective-permute-start.10 = (bf16[4,2,256,256]{3,2,1,0:T(8,128)(2,1)S(1)}, bf16[4,2,256,256]{3,2,1,0:T(8,128)(2,1)S(1)}, u32[]{:S(2)}, u32[]{:S(2)}) collective-permute-start(bf16[4,2,256,256]{3,2,1,0:T(8,128)(2,1)S(1)} %pad_maximum_fusion.1), channel_id=1, source_target_pairs={{0,64},{1,65},{2,66},{3,67},{4,68},{5,69},{6,70},{7,71},{8,72},{9,... | collective-permute-start | bytes 3145736 | tf_op jit(solution)/shard_map/ppermute | solution.py:205
  23.3 25.0 %collective-permute-start.9 = (bf16[2,2,256,256]{3,2,1,0:T(8,128)(2,1)S(1)}, bf16[2,2,256,256]{3,2,1,0:T(8,128)(2,1)S(1)}, u32[]{:S(2)}, u32[]{:S(2)}) collective-permute-start(bf16[2,2,256,256]{3,2,1,0:T(8,128)(2,1)S(1)} %pad_maximum_fusion.6), channel_id=1, source_target_pairs={{0,48},{8,56},{16,0},{24,8},{32,16},{40,24},{48,32},{56,40},{64,11... | collective-permute-start | bytes 1572872 | tf_op jit(solution)/shard_map/ppermute | solution.py:213
  25.9 22.4 %collective-permute-start.8 = (bf16[2,2,256,256]{3,2,1,0:T(8,128)(2,1)S(1)}, bf16[2,2,256,256]{3,2,1,0:T(8,128)(2,1)S(1)}, u32[]{:S(2)}, u32[]{:S(2)}) collective-permute-start(bf16[2,2,256,256]{3,2,1,0:T(8,128)(2,1)S(1)} %pad_maximum_fusion.6), channel_id=1, source_target_pairs={{0,32},{8,40},{16,48},{24,56},{32,0},{40,8},{48,16},{56,24},{64,96... | collective-permute-start | bytes 1572872 | tf_op jit(solution)/shard_map/ppermute | solution.py:213
  26.8 25.2 %collective-permute-start.7 = (bf16[2,2,256,256]{3,2,1,0:T(8,128)(2,1)S(1)}, bf16[2,2,256,256]{3,2,1,0:T(8,128)(2,1)S(1)}, u32[]{:S(2)}, u32[]{:S(2)}) collective-permute-start(bf16[2,2,256,256]{3,2,1,0:T(8,128)(2,1)S(1)} %pad_maximum_fusion.6), channel_id=1, source_target_pairs={{0,16},{8,24},{16,32},{24,40},{32,48},{40,56},{48,0},{56,8},{64,80... | collective-permute-start | bytes 1572872 | tf_op jit(solution)/shard_map/ppermute | solution.py:213
  48.3 4.0 %collective-permute-start = (s32[129]{0:T(256)S(1)}, s32[129]{0:T(256)S(1)}, u32[]{:S(2)}, u32[]{:S(2)}) collective-permute-start(s32[129]{0:T(256)S(1)} %pad_add_fusion.ids), channel_id=1, source_target_pairs={{0,8},{8,0},{16,24},{24,16},{32,40},{40,32},{48,56},{56,48},{64,72... | collective-permute-start | bytes 1556 | tf_op jit(solution)/shard_map/ppermute | solution.py:200
  52.0 1.6 copy-start
  60.3 29.4 %collective-permute-start.11 = (bf16[4,2,256,256]{3,2,1,0:T(8,128)(2,1)S(1)}, bf16[4,2,256,256]{3,2,1,0:T(8,128)(2,1)S(1)}, u32[]{:S(2)}, u32[]{:S(2)}) collective-permute-start(bf16[4,2,256,256]{3,2,1,0:T(8,128)(2,1)S(1)} %get-tuple-element.61), channel_id=1, source_target_pairs={{0,1},{1,0},{2,3},{3,2},{4,5},{5,4},{6,7},{7,6},{8,9},{9,8},{10,11... | collective-permute-start | bytes 3145736 | tf_op jit(solution)/shard_map/ppermute | solution.py:205
  61.2 15.9 %collective-permute-start.12 = (bf16[2,2,256,256]{3,2,1,0:T(8,128)(2,1)S(1)}, bf16[2,2,256,256]{3,2,1,0:T(8,128)(2,1)S(1)}, u32[]{:S(2)}, u32[]{:S(2)}) collective-permute-start(bf16[2,2,256,256]{3,2,1,0:T(8,128)(2,1)S(1)} %get-tuple-element.63), channel_id=1, source_target_pairs={{0,2},{1,3},{2,4},{3,5},{4,6},{5,7},{6,0},{7,1},{8,10},{9,11},{10,... | collective-permute-start | bytes 1572872 | tf_op jit(solution)/shard_map/ppermute | solution.py:213
  62.3 27.2 %collective-permute-start.13 = (bf16[2,2,256,256]{3,2,1,0:T(8,128)(2,1)S(1)}, bf16[2,2,256,256]{3,2,1,0:T(8,128)(2,1)S(1)}, u32[]{:S(2)}, u32[]{:S(2)}) collective-permute-start(bf16[2,2,256,256]{3,2,1,0:T(8,128)(2,1)S(1)} %get-tuple-element.64), channel_id=1, source_target_pairs={{0,4},{1,5},{2,6},{3,7},{4,0},{5,1},{6,2},{7,3},{8,12},{9,13},{10,... | collective-permute-start | bytes 1572872 | tf_op jit(solution)/shard_map/ppermute | solution.py:213
  66.7 22.8 %collective-permute-start.14 = (bf16[2,2,256,256]{3,2,1,0:T(8,128)(2,1)S(1)}, bf16[2,2,256,256]{3,2,1,0:T(8,128)(2,1)S(1)}, u32[]{:S(2)}, u32[]{:S(2)}) collective-permute-start(bf16[2,2,256,256]{3,2,1,0:T(8,128)(2,1)S(1)} %get-tuple-element.65), channel_id=1, source_target_pairs={{0,6},{1,7},{2,0},{3,1},{4,2},{5,3},{6,4},{7,5},{8,14},{9,15},{10,... | collective-permute-start | bytes 1572872 | tf_op jit(solution)/shard_map/ppermute | solution.py:213
  89.4 16.5 %copy-start.1 = (bf16[512,512]{1,0:T(8,128)(2,1)S(1)}, bf16[512,512]{1,0:T(8,128)(2,1)}, u32[]{:S(2)}) copy-start(bf16[512,512]{1,0:T(8,128)(2,1)} %weight.3) | copy-start | bytes 1572868
  89.4 16.5 %copy-start.2 = (bf16[512,512]{1,0:T(8,128)(2,1)S(1)}, bf16[512,512]{1,0:T(8,128)(2,1)}, u32[]{:S(2)}) copy-start(bf16[512,512]{1,0:T(8,128)(2,1)} %cotangent.3) | copy-start | bytes 1572868
  89.4 16.5 %copy-start.4 = (f32[512]{0:T(512)S(1)}, f32[512]{0:T(512)}, u32[]{:S(2)}) copy-start(f32[512]{0:T(512)} %param.10) | copy-start | bytes 6148
  90.1 7.1 %collective-permute-start.19 = (bf16[2,256,256]{2,1,0:T(8,128)(2,1)S(1)}, bf16[2,256,256]{2,1,0:T(8,128)(2,1)S(1)}, u32[]{:S(2)}, u32[]{:S(2)}) collective-permute-start(bf16[2,256,256]{2,1,0:T(8,128)(2,1)S(1)} %get-tuple-element.72), channel_id=1, source_target_pairs={{0,1},{1,0},{2,3},{3,2},{4,5},{5,4},{6,7},{7,6},{8,9},{9,8},{10,11... | collective-permute-start | bytes 786440 | tf_op jit(solution)/shard_map/ppermute | solution.py:205
  90.5 8.4 %collective-permute-start.15 = (bf16[2,256,256]{2,1,0:T(8,128)(2,1)S(1)}, bf16[2,256,256]{2,1,0:T(8,128)(2,1)S(1)}, u32[]{:S(2)}, u32[]{:S(2)}) collective-permute-start(bf16[2,256,256]{2,1,0:T(8,128)(2,1)S(1)} %get-tuple-element.67), channel_id=1, source_target_pairs={{0,2},{1,3},{2,4},{3,5},{4,6},{5,7},{6,0},{7,1},{8,10},{9,11},{10,... | collective-permute-start | bytes 786440 | tf_op jit(solution)/shard_map/ppermute | solution.py:213
  91.4 14.3 %collective-permute-start.16 = (bf16[2,256,256]{2,1,0:T(8,128)(2,1)S(1)}, bf16[2,256,256]{2,1,0:T(8,128)(2,1)S(1)}, u32[]{:S(2)}, u32[]{:S(2)}) collective-permute-start(bf16[2,256,256]{2,1,0:T(8,128)(2,1)S(1)} %get-tuple-element.68), channel_id=1, source_target_pairs={{0,4},{1,5},{2,6},{3,7},{4,0},{5,1},{6,2},{7,3},{8,12},{9,13},{10,... | collective-permute-start | bytes 786440 | tf_op jit(solution)/shard_map/ppermute | solution.py:213
  94.1 11.5 %collective-permute-start.17 = (bf16[2,256,256]{2,1,0:T(8,128)(2,1)S(1)}, bf16[2,256,256]{2,1,0:T(8,128)(2,1)S(1)}, u32[]{:S(2)}, u32[]{:S(2)}) collective-permute-start(bf16[2,256,256]{2,1,0:T(8,128)(2,1)S(1)} %get-tuple-element.69), channel_id=1, source_target_pairs={{0,6},{1,7},{2,0},{3,1},{4,2},{5,3},{6,4},{7,5},{8,14},{9,15},{10,... | collective-permute-start | bytes 786440 | tf_op jit(solution)/shard_map/ppermute | solution.py:213
  97.3 8.6 %collective-permute-start.20 = (bf16[256,256]{1,0:T(8,128)(2,1)S(1)}, bf16[256,256]{1,0:T(8,128)(2,1)S(1)}, u32[]{:S(2)}, u32[]{:S(2)}) collective-permute-start(bf16[256,256]{1,0:T(8,128)(2,1)S(1)} %get-tuple-element.139), channel_id=1, source_target_pairs={{0,8},{8,0},{16,24},{24,16},{32,40},{40,32},{48,56},{56,48},{64,72... | collective-permute-start | bytes 393224 | tf_op jit(solution)/shard_map/ppermute | solution.py:200
  105.8 1.4 collective-permute-start.18
  108.7 1.9 collective-permute-start.22
  109.2 3.6 %collective-permute-start.24 = (bf16[256,256]{1,0:T(8,128)(2,1)S(1)}, bf16[256,256]{1,0:T(8,128)(2,1)S(1)}, u32[]{:S(2)}, u32[]{:S(2)}) collective-permute-start(bf16[256,256]{1,0:T(8,128)(2,1)S(1)} %get-tuple-element.81), channel_id=1, source_target_pairs={{0,8},{8,0},{16,24},{24,16},{32,40},{40,32},{48,56},{56,48},{64,72... | collective-permute-start | bytes 393224 | tf_op jit(solution)/shard_map/ppermute | solution.py:200
  109.5 1.5 collective-permute-start.21
  111.0 17.1 %collective-permute-start.23 = (bf16[2,416,256]{2,1,0:T(8,128)(2,1)S(1)}, bf16[2,416,256]{2,1,0:T(8,128)(2,1)S(1)}, u32[]{:S(2)}, u32[]{:S(2)}) collective-permute-start(bf16[2,416,256]{2,1,0:T(8,128)(2,1)S(1)} %pad_maximum_fusion.9), channel_id=1, source_target_pairs={{0,1},{1,0},{2,3},{3,2},{4,5},{5,4},{6,7},{7,6},{8,9},{9,8},{10,11... | collective-permute-start | bytes 1277960 | tf_op jit(solution)/shard_map/ppermute | solution.py:205
  112.7 10.8 %collective-permute-start.26 = (bf16[2,256,256]{2,1,0:T(8,128)(2,1)S(1)}, bf16[2,256,256]{2,1,0:T(8,128)(2,1)S(1)}, u32[]{:S(2)}, u32[]{:S(2)}) collective-permute-start(bf16[2,256,256]{2,1,0:T(8,128)(2,1)S(1)} %get-tuple-element.136), channel_id=1, source_target_pairs={{0,4},{1,5},{2,6},{3,7},{4,0},{5,1},{6,2},{7,3},{8,12},{9,13},{10,... | collective-permute-start | bytes 786440 | tf_op jit(solution)/shard_map/ppermute | solution.py:213
  114.2 13.8 %collective-permute-start.25 = (bf16[2,256,256]{2,1,0:T(8,128)(2,1)S(1)}, bf16[2,256,256]{2,1,0:T(8,128)(2,1)S(1)}, u32[]{:S(2)}, u32[]{:S(2)}) collective-permute-start(bf16[2,256,256]{2,1,0:T(8,128)(2,1)S(1)} %get-tuple-element.136), channel_id=1, source_target_pairs={{0,2},{1,3},{2,4},{3,5},{4,6},{5,7},{6,0},{7,1},{8,10},{9,11},{10,... | collective-permute-start | bytes 786440 | tf_op jit(solution)/shard_map/ppermute | solution.py:213
  115.7 12.3 %collective-permute-start.27 = (bf16[2,256,256]{2,1,0:T(8,128)(2,1)S(1)}, bf16[2,256,256]{2,1,0:T(8,128)(2,1)S(1)}, u32[]{:S(2)}, u32[]{:S(2)}) collective-permute-start(bf16[2,256,256]{2,1,0:T(8,128)(2,1)S(1)} %get-tuple-element.136), channel_id=1, source_target_pairs={{0,6},{1,7},{2,0},{3,1},{4,2},{5,3},{6,4},{7,5},{8,14},{9,15},{10,... | collective-permute-start | bytes 786440 | tf_op jit(solution)/shard_map/ppermute | solution.py:213
  128.4 29.2 %collective-permute-start.31 = (bf16[4,2,256,256]{3,2,1,0:T(8,128)(2,1)S(1)}, bf16[4,2,256,256]{3,2,1,0:T(8,128)(2,1)S(1)}, u32[]{:S(2)}, u32[]{:S(2)}) collective-permute-start(bf16[4,2,256,256]{3,2,1,0:T(8,128)(2,1)S(1)} %pad_maximum_fusion.2), channel_id=1, source_target_pairs={{0,1},{1,0},{2,3},{3,2},{4,5},{5,4},{6,7},{7,6},{8,9},{9,8},{10,11... | collective-permute-start | bytes 3145736 | tf_op jit(solution)/shard_map/ppermute | solution.py:205
  129.0 16.7 %collective-permute-start.28 = (bf16[1104,256]{1,0:T(8,128)(2,1)S(1)}, bf16[1104,256]{1,0:T(8,128)(2,1)S(1)}, u32[]{:S(2)}, u32[]{:S(2)}) collective-permute-start(bf16[1104,256]{1,0:T(8,128)(2,1)S(1)} %get-tuple-element.126), channel_id=1, source_target_pairs={{0,2},{1,3},{2,4},{3,5},{4,6},{5,7},{6,0},{7,1},{8,10},{9,11},{10,... | collective-permute-start | bytes 1695752 | tf_op jit(solution)/shard_map/ppermute | solution.py:213
  129.9 27.3 %collective-permute-start.29 = (bf16[1104,256]{1,0:T(8,128)(2,1)S(1)}, bf16[1104,256]{1,0:T(8,128)(2,1)S(1)}, u32[]{:S(2)}, u32[]{:S(2)}) collective-permute-start(bf16[1104,256]{1,0:T(8,128)(2,1)S(1)} %get-tuple-element.127), channel_id=1, source_target_pairs={{0,4},{1,5},{2,6},{3,7},{4,0},{5,1},{6,2},{7,3},{8,12},{9,13},{10,... | collective-permute-start | bytes 1695752 | tf_op jit(solution)/shard_map/ppermute | solution.py:213
  132.6 24.9 %collective-permute-start.30 = (bf16[1104,256]{1,0:T(8,128)(2,1)S(1)}, bf16[1104,256]{1,0:T(8,128)(2,1)S(1)}, u32[]{:S(2)}, u32[]{:S(2)}) collective-permute-start(bf16[1104,256]{1,0:T(8,128)(2,1)S(1)} %get-tuple-element.128), channel_id=1, source_target_pairs={{0,6},{1,7},{2,0},{3,1},{4,2},{5,3},{6,4},{7,5},{8,14},{9,15},{10,... | collective-permute-start | bytes 1695752 | tf_op jit(solution)/shard_map/ppermute | solution.py:213
  157.9 9.7 %collective-permute-start.34 = (bf16[80,256]{1,0:T(8,128)(2,1)S(1)}, bf16[80,256]{1,0:T(8,128)(2,1)S(1)}, u32[]{:S(2)}, u32[]{:S(2)}) collective-permute-start(bf16[80,256]{1,0:T(8,128)(2,1)S(1)} %fusion.17), channel_id=1, source_target_pairs={{0,48},{8,56},{16,0},{24,8},{32,16},{40,24},{48,32},{56,40},{64,11... | collective-permute-start | bytes 122888 | tf_op jit(solution)/shard_map/ppermute | solution.py:213
  159.3 8.3 %collective-permute-start.33 = (bf16[80,256]{1,0:T(8,128)(2,1)S(1)}, bf16[80,256]{1,0:T(8,128)(2,1)S(1)}, u32[]{:S(2)}, u32[]{:S(2)}) collective-permute-start(bf16[80,256]{1,0:T(8,128)(2,1)S(1)} %fusion.17), channel_id=1, source_target_pairs={{0,32},{8,40},{16,48},{24,56},{32,0},{40,8},{48,16},{56,24},{64,96... | collective-permute-start | bytes 122888 | tf_op jit(solution)/shard_map/ppermute | solution.py:213
  159.7 7.9 %collective-permute-start.32 = (bf16[80,256]{1,0:T(8,128)(2,1)S(1)}, bf16[80,256]{1,0:T(8,128)(2,1)S(1)}, u32[]{:S(2)}, u32[]{:S(2)}) collective-permute-start(bf16[80,256]{1,0:T(8,128)(2,1)S(1)} %fusion.17), channel_id=1, source_target_pairs={{0,16},{8,24},{16,32},{24,40},{32,48},{40,56},{48,0},{56,8},{64,80... | collective-permute-start | bytes 122888 | tf_op jit(solution)/shard_map/ppermute | solution.py:213
  167.7 28.6 %collective-permute-start.35 = (bf16[2128,256]{1,0:T(8,128)(2,1)S(1)}, bf16[2128,256]{1,0:T(8,128)(2,1)S(1)}, u32[]{:S(2)}, u32[]{:S(2)}) collective-permute-start(bf16[2128,256]{1,0:T(8,128)(2,1)S(1)} %pad_maximum_fusion), channel_id=1, source_target_pairs={{0,64},{1,65},{2,66},{3,67},{4,68},{5,69},{6,70},{7,71},{8,72},{9,... | collective-permute-start | bytes 3268616 | tf_op jit(solution)/shard_map/ppermute | solution.py:205
  169.4 15.6 %collective-permute-start.36 = (bf16[2,2,256,256]{3,2,1,0:T(8,128)(2,1)S(1)}, bf16[2,2,256,256]{3,2,1,0:T(8,128)(2,1)S(1)}, u32[]{:S(2)}, u32[]{:S(2)}) collective-permute-start(bf16[2,2,256,256]{3,2,1,0:T(8,128)(2,1)S(1)} %get-tuple-element.97), channel_id=1, source_target_pairs={{0,16},{8,24},{16,32},{24,40},{32,48},{40,56},{48,0},{56,8},{64,80... | collective-permute-start | bytes 1572872 | tf_op jit(solution)/shard_map/ppermute | solution.py:213
  172.7 23.3 %collective-permute-start.37 = (bf16[2,2,256,256]{3,2,1,0:T(8,128)(2,1)S(1)}, bf16[2,2,256,256]{3,2,1,0:T(8,128)(2,1)S(1)}, u32[]{:S(2)}, u32[]{:S(2)}) collective-permute-start(bf16[2,2,256,256]{3,2,1,0:T(8,128)(2,1)S(1)} %get-tuple-element.98), channel_id=1, source_target_pairs={{0,32},{8,40},{16,48},{24,56},{32,0},{40,8},{48,16},{56,24},{64,96... | collective-permute-start | bytes 1572872 | tf_op jit(solution)/shard_map/ppermute | solution.py:213
  174.9 21.2 %collective-permute-start.38 = (bf16[2,2,256,256]{3,2,1,0:T(8,128)(2,1)S(1)}, bf16[2,2,256,256]{3,2,1,0:T(8,128)(2,1)S(1)}, u32[]{:S(2)}, u32[]{:S(2)}) collective-permute-start(bf16[2,2,256,256]{3,2,1,0:T(8,128)(2,1)S(1)} %get-tuple-element.99), channel_id=1, source_target_pairs={{0,48},{8,56},{16,0},{24,8},{32,16},{40,24},{48,32},{56,40},{64,11... | collective-permute-start | bytes 1572872 | tf_op jit(solution)/shard_map/ppermute | solution.py:213
  196.3 6.8 %collective-permute-start.45 = (bf16[80,256]{1,0:T(8,128)(2,1)S(1)}, bf16[80,256]{1,0:T(8,128)(2,1)S(1)}, u32[]{:S(2)}, u32[]{:S(2)}) collective-permute-start(bf16[80,256]{1,0:T(8,128)(2,1)S(1)} %add_convert_fusion.12), channel_id=1, source_target_pairs={{0,1},{1,0},{2,3},{3,2},{4,5},{5,4},{6,7},{7,6},{8,9},{9,8},{10,11... | collective-permute-start | bytes 122888 | tf_op jit(solution)/shard_map/ppermute | solution.py:205
  196.8 11.4 %collective-permute-start.39 = (bf16[2,256,256]{2,1,0:T(8,128)(2,1)S(1)}, bf16[2,256,256]{2,1,0:T(8,128)(2,1)S(1)}, u32[]{:S(2)}, u32[]{:S(2)}) collective-permute-start(bf16[2,256,256]{2,1,0:T(8,128)(2,1)S(1)} %get-tuple-element.101), channel_id=1, source_target_pairs={{0,16},{8,24},{16,32},{24,40},{32,48},{40,56},{48,0},{56,8},{64,80... | collective-permute-start | bytes 786440 | tf_op jit(solution)/shard_map/ppermute | solution.py:213
  198.3 14.2 %collective-permute-start.40 = (bf16[2,256,256]{2,1,0:T(8,128)(2,1)S(1)}, bf16[2,256,256]{2,1,0:T(8,128)(2,1)S(1)}, u32[]{:S(2)}, u32[]{:S(2)}) collective-permute-start(bf16[2,256,256]{2,1,0:T(8,128)(2,1)S(1)} %get-tuple-element.102), channel_id=1, source_target_pairs={{0,32},{8,40},{16,48},{24,56},{32,0},{40,8},{48,16},{56,24},{64,96... | collective-permute-start | bytes 786440 | tf_op jit(solution)/shard_map/ppermute | solution.py:213
  200.7 13.2 %collective-permute-start.41 = (bf16[2,256,256]{2,1,0:T(8,128)(2,1)S(1)}, bf16[2,256,256]{2,1,0:T(8,128)(2,1)S(1)}, u32[]{:S(2)}, u32[]{:S(2)}) collective-permute-start(bf16[2,256,256]{2,1,0:T(8,128)(2,1)S(1)} %get-tuple-element.103), channel_id=1, source_target_pairs={{0,48},{8,56},{16,0},{24,8},{32,16},{40,24},{48,32},{56,40},{64,11... | collective-permute-start | bytes 786440 | tf_op jit(solution)/shard_map/ppermute | solution.py:213
  203.1 1.4 collective-permute-start.46
  203.2 11.0 %collective-permute-start.43 = (bf16[2,256,256]{2,1,0:T(8,128)(2,1)S(1)}, bf16[2,256,256]{2,1,0:T(8,128)(2,1)S(1)}, u32[]{:S(2)}, u32[]{:S(2)}) collective-permute-start(bf16[2,256,256]{2,1,0:T(8,128)(2,1)S(1)} %get-tuple-element.105), channel_id=1, source_target_pairs={{0,64},{1,65},{2,66},{3,67},{4,68},{5,69},{6,70},{7,71},{8,72},{9,... | collective-permute-start | bytes 786440 | tf_op jit(solution)/shard_map/ppermute | solution.py:205
  204.5 11.2 %collective-permute-start.49 = (bf16[2,2,80,256]{3,2,1,0:T(8,128)(2,1)S(1)}, bf16[2,2,80,256]{3,2,1,0:T(8,128)(2,1)S(1)}, u32[]{:S(2)}, u32[]{:S(2)}) collective-permute-start(bf16[2,2,80,256]{3,2,1,0:T(8,128)(2,1)S(1)} %pad_maximum_fusion.12.own), channel_id=1, source_target_pairs={{0,6},{1,7},{2,0},{3,1},{4,2},{5,3},{6,4},{7,5},{8,14},{9,15},{10,... | collective-permute-start | bytes 491528 | tf_op jit(solution)/shard_map/ppermute | solution.py:213
  208.2 7.5 %collective-permute-start.48 = (bf16[2,2,80,256]{3,2,1,0:T(8,128)(2,1)S(1)}, bf16[2,2,80,256]{3,2,1,0:T(8,128)(2,1)S(1)}, u32[]{:S(2)}, u32[]{:S(2)}) collective-permute-start(bf16[2,2,80,256]{3,2,1,0:T(8,128)(2,1)S(1)} %pad_maximum_fusion.12.own), channel_id=1, source_target_pairs={{0,4},{1,5},{2,6},{3,7},{4,0},{5,1},{6,2},{7,3},{8,12},{9,13},{10,... | collective-permute-start | bytes 491528 | tf_op jit(solution)/shard_map/ppermute | solution.py:213
  212.5 7.2 %collective-permute-start.47 = (bf16[2,2,80,256]{3,2,1,0:T(8,128)(2,1)S(1)}, bf16[2,2,80,256]{3,2,1,0:T(8,128)(2,1)S(1)}, u32[]{:S(2)}, u32[]{:S(2)}) collective-permute-start(bf16[2,2,80,256]{3,2,1,0:T(8,128)(2,1)S(1)} %pad_maximum_fusion.12.own), channel_id=1, source_target_pairs={{0,2},{1,3},{2,4},{3,5},{4,6},{5,7},{6,0},{7,1},{8,10},{9,11},{10,... | collective-permute-start | bytes 491528 | tf_op jit(solution)/shard_map/ppermute | solution.py:213
  214.0 6.7 %collective-permute-start.42 = (bf16[256,256]{1,0:T(8,128)(2,1)S(1)}, bf16[256,256]{1,0:T(8,128)(2,1)S(1)}, u32[]{:S(2)}, u32[]{:S(2)}) collective-permute-start(bf16[256,256]{1,0:T(8,128)(2,1)S(1)} %get-tuple-element.133), channel_id=1, source_target_pairs={{0,8},{8,0},{16,24},{24,16},{32,40},{40,32},{48,56},{56,48},{64,72... | collective-permute-start | bytes 393224 | tf_op jit(solution)/shard_map/ppermute | solution.py:200
  214.2 6.5 %collective-permute-start.44 = (bf16[256,256]{1,0:T(8,128)(2,1)S(1)}, bf16[256,256]{1,0:T(8,128)(2,1)S(1)}, u32[]{:S(2)}, u32[]{:S(2)}) collective-permute-start(bf16[256,256]{1,0:T(8,128)(2,1)S(1)} %get-tuple-element.131), channel_id=1, source_target_pairs={{0,8},{8,0},{16,24},{24,16},{32,40},{40,32},{48,56},{56,48},{64,72... | collective-permute-start | bytes 393224 | tf_op jit(solution)/shard_map/ppermute | solution.py:200
